TPU v7x, 32 devices: a whole 2x2x4 slice. The times are simulated.
32 devices in a mesh: fsdp: 8 (over z, y), ctx: 4 (over x, core).
Axes of the slice: x: 2, y: 2, z: 4, core: 2. Of those that a mesh axis runs over, the one named last changes fastest.
Arguments:
- hidden: bfloat16 [16, 1024, 896], P('fsdp', 'ctx'), may hold values from -6 to 6
- segments: int32 [16, 1024], P('fsdp'), may hold values from 0 to 2, as said below
- attn_gain: bfloat16 [896], P(('fsdp', 'ctx')), may hold values from 0.099609375 to 1.8984375
- qkv_weight: bfloat16 [896, 1152], P(('fsdp', 'ctx')), may hold values from -0.1875 to 0.1875
- qkv_bias: bfloat16 [1152], P(('fsdp', 'ctx')), may hold values from -0.29882812 to 0.29882812
- out_weight: bfloat16 [896, 896], P(None, ('fsdp', 'ctx')), may hold values from -0.75 to 0.75
- mlp_gain: bfloat16 [896], P(('fsdp', 'ctx')), may hold values from 0.099609375 to 1.8984375
- gate_weight: bfloat16 [896, 4864], P(('fsdp', 'ctx')), may hold values from -0.1875 to 0.1875
- up_weight: bfloat16 [896, 4864], P(('fsdp', 'ctx')), may hold values from -0.1875 to 0.1875
- down_weight: bfloat16 [4864, 896], P(None, ('fsdp', 'ctx')), may hold values from -0.078125 to 0.078125
- cotangent: bfloat16 [16, 1024, 896], P('fsdp', 'ctx'), may hold values from -6 to 6
Outputs:
- output: bfloat16 [16, 1024, 896], P('fsdp', 'ctx')
- input_grad: bfloat16 [16, 1024, 896], P('fsdp', 'ctx')
- attn_gain_grad: float32 [896], P(('fsdp', 'ctx'))
- qkv_weight_grad: float32 [896, 1152], P(('fsdp', 'ctx'))
- qkv_bias_grad: float32 [1024], P(('fsdp', 'ctx'))
- value_bias_grad: float32 [128], P(('fsdp', 'ctx'))
- out_weight_grad: float32 [896, 896], P(None, ('fsdp', 'ctx'))
- mlp_gain_grad: float32 [896], P(('fsdp', 'ctx'))
- gate_weight_grad: float32 [896, 4864], P(('fsdp', 'ctx'))
- up_weight_grad: float32 [896, 4864], P(('fsdp', 'ctx'))
- down_weight_grad: float32 [4864, 896], P(None, ('fsdp', 'ctx'))
Inputs may be any that keep to these rules, and one draw needn't show every extreme that they name: `segments`: along a sequence the numbers never fall; each of 0, 1 and 2 occurs, and document 1 holds positions 256 to 768.
All inputs are finite; a program needn't handle non-finite values.
Results may differ from a plain program's by a relative error of at most 0.029.
Values may be sent and summed in bfloat16 or wider, within the bound.
No kernel may reach another device: no remote copies, remote signals or barrier semaphores. Data moves between devices by JAX's collectives and lax.ppermute only.
A program may use at most 384 MiB of HBM per device.

v0:
```python
import functools

import jax
import jax.numpy as jnp
from jax import lax
from jax.experimental import pallas as pl
from jax.experimental.pallas import tpu as pltpu
from jax.sharding import Mesh
from jax.sharding import PartitionSpec as P

HD = 64
LANES = 128
EPSILON = 1e-06
ROPE_BASE = 1000000.0
MASKED = -1e30
SCALE = HD ** (-0.5)
TILE = 256
MIB = 1 << 20
VMEM_LIMIT = 60 * MIB
F32 = jnp.float32
BF16 = jnp.bfloat16
AXES = ("fz", "fy", "cx", "cc")
FSDP = ("fz", "fy")
CTX = ("cx", "cc")
TOKENS = ("fy", "cx")
WEIGHTS = ("fz", "cc")


def dot_nn(a, b):
    return lax.dot_general(a, b, (((1,), (0,)), ((), ())), preferred_element_type=F32)


def dot_nt(a, b):
    return lax.dot_general(a, b, (((1,), (1,)), ((), ())), preferred_element_type=F32)


def dot_tn(a, b):
    return lax.dot_general(a, b, (((0,), (0,)), ((), ())), preferred_element_type=F32)


def lane_of(shape):
    return lax.broadcasted_iota(jnp.int32, shape, len(shape) - 1)


def swap_halves(block):
    lead = lane_of(block.shape) % HD < HD // 2
    return jnp.where(
        lead, pltpu.roll(block, LANES - HD // 2, 1), pltpu.roll(block, HD // 2, 1)
    )


def other_head(block):
    return jnp.concatenate([block[:, HD:], block[:, :HD]], axis=1)


def read_out(extras, first, piece, total):
    owners, columns = extras.shape
    at = lax.broadcasted_iota(jnp.int32, (columns, total), 1) % piece + first
    chosen = (lax.broadcasted_iota(jnp.int32, (columns, total), 0) == at).astype(BF16)
    spread = dot_nn(extras, chosen)
    owner = lax.broadcasted_iota(jnp.int32, (owners, total), 1) // piece
    mine = owner == lax.broadcasted_iota(jnp.int32, (owners, total), 0)
    return jnp.sum(jnp.where(mine, spread, 0.0), axis=0, keepdims=True)


def prep_kernel(
    x_ref, order_ref, spread_ref, w_low_ref, w_high_ref, cos_ref, sin_ref,
    normed_low_ref, normed_high_ref, q_ref, kv_ref, gain_ref, gain_mlp_ref, bias_ref,
):
    x = x_ref[...].astype(F32)
    dim = x.shape[1]
    width = q_ref.shape[1]
    joint = w_low_ref.shape[1]
    middle = w_low_ref.shape[0]
    owners = spread_ref.shape[0]

    @pl.when(pl.program_id(0) == 0)
    def _():
        extras = dot_nn(spread_ref[:, :middle], w_low_ref[:, :LANES])
        extras = (extras + dot_nn(spread_ref[:, middle:], w_high_ref[:, :LANES])).astype(BF16)
        shard = dim // owners
        gain_ref[...] = read_out(extras, 0, shard, dim)
        gain_mlp_ref[...] = read_out(extras, shard, shard, dim)
        bias_ref[...] = read_out(extras, 2 * shard, joint // owners, joint)

    gain, bias = gain_ref[...], bias_ref[...]
    inverse = lax.rsqrt(jnp.mean(x * x, axis=-1, keepdims=True) + EPSILON)
    normed = (x * inverse * gain).astype(BF16)
    ordered = dot_nn(normed, order_ref[...]).astype(BF16)
    normed_low_ref[...] = ordered[:, :middle]
    normed_high_ref[...] = ordered[:, middle:]
    joined = dot_nn(ordered[:, :middle], w_low_ref[...])
    joined = joined + dot_nn(ordered[:, middle:], w_high_ref[...]) + bias
    cosine, sine = cos_ref[...], sin_ref[...]
    for begin in range(0, width + LANES, LANES):
        block = joined[:, begin : begin + LANES]
        turned = block * cosine + swap_halves(block) * sine
        if begin < width:
            q_ref[:, begin : begin + LANES] = (turned * SCALE).astype(BF16)
        else:
            kv_ref[:, :LANES] = turned.astype(BF16)
    kv_ref[:, LANES:] = joined[:, width + LANES :].astype(BF16)


def rows_of(rows, cols):
    return pl.BlockSpec((rows, cols), lambda i: (i, 0))


def whole(value):
    return pl.BlockSpec(value.shape, lambda i: (0,) * value.ndim)


def prep(x, order, spread, weights, cosine, sine, rows):
    count, dim = x.shape
    ordered = order.shape[1]
    joint = weights[0].shape[1]
    width = joint - 2 * LANES
    row = pl.BlockSpec((1, dim), lambda i: (0, 0))
    return pl.pallas_call(
        prep_kernel,
        grid=(count // rows,),
        in_specs=[
            rows_of(rows, dim),
            whole(order),
            whole(spread),
            whole(weights[0]),
            whole(weights[1]),
            rows_of(rows, LANES),
            rows_of(rows, LANES),
        ],
        out_specs=[
            rows_of(rows, ordered // 2),
            rows_of(rows, ordered // 2),
            rows_of(rows, width),
            rows_of(rows, 2 * LANES),
            row,
            row,
        ],
        out_shape=[
            jax.ShapeDtypeStruct((count, ordered // 2), BF16),
            jax.ShapeDtypeStruct((count, ordered // 2), BF16),
            jax.ShapeDtypeStruct((count, width), BF16),
            jax.ShapeDtypeStruct((count, 2 * LANES), BF16),
            jax.ShapeDtypeStruct((1, dim), F32),
            jax.ShapeDtypeStruct((1, dim), F32),
        ],
        scratch_shapes=[pltpu.VMEM((1, joint), F32)],
        compiler_params=pltpu.CompilerParams(vmem_limit_bytes=VMEM_LIMIT),
        cost_estimate=pl.CostEstimate(
            flops=2 * count * ordered * (joint + dim), bytes_accessed=12 * MIB, transcendentals=0
        ),
        name="norm_project_rotate",
    )(x, order, spread, weights[0], weights[1], cosine, sine)


def back_in_order(value, order):
    high = value.astype(BF16)
    low = (value - high.astype(F32)).astype(BF16)
    return dot_nt(high, order) + dot_nt(low, order)


def out_kernel(attended_ref, x_ref, w_low_ref, w_high_ref, order_ref, gain_ref, resid_ref, normed_ref):
    attended = attended_ref[...]
    branch = jnp.concatenate([dot_nt(attended, w_low_ref[...]), dot_nt(attended, w_high_ref[...])], axis=1)
    resid = x_ref[...].astype(F32) + back_in_order(branch, order_ref[...])
    inverse = lax.rsqrt(jnp.mean(resid * resid, axis=-1, keepdims=True) + EPSILON)
    resid_ref[...] = resid
    normed_ref[...] = (resid * inverse * gain_ref[...]).astype(BF16)


def project_out(attended, x, weights, order, gain, rows, seq):
    dim = x.shape[1]
    count = rows
    return pl.pallas_call(
        out_kernel,
        grid=(1,),
        in_specs=[
            rows_of(rows, attended.shape[1]),
            pl.BlockSpec((rows, dim), lambda i: (seq, 0)),
            whole(weights[0]),
            whole(weights[1]),
            whole(order),
            whole(gain),
        ],
        out_specs=[rows_of(rows, dim), rows_of(rows, dim)],
        out_shape=[jax.ShapeDtypeStruct((count, dim), F32), jax.ShapeDtypeStruct((count, dim), BF16)],
        compiler_params=pltpu.CompilerParams(vmem_limit_bytes=VMEM_LIMIT),
        cost_estimate=pl.CostEstimate(flops=6 * count * dim * dim, bytes_accessed=8 * MIB, transcendentals=0),
        name="project_out_norm",
    )(attended, x, weights[0], weights[1], order, gain)


def sum_rows(value):
    return jnp.sum(value, axis=0, keepdims=True)


def norm_back(values, inverse, gain, incoming):
    scaled = incoming * gain
    mean_term = jnp.mean(scaled * values, axis=-1, keepdims=True)
    return inverse * scaled - values * inverse**3 * mean_term


def total_of(own_ref, *away_refs):
    total = own_ref[...]
    for ref in away_refs:
        total = total + ref[...].astype(F32)
    return total


def out_back_kernel(
    own_ref, core_ref, x_ref, far_ref, resid_ref, cot_ref, w_low_ref, w_high_ref, order_ref, gain_ref,
    d_resid_ref, d_low_ref, d_high_ref, d_attended_ref, gain_grad_ref,
):
    middle = w_low_ref.shape[0]
    d_normed = total_of(own_ref, core_ref, x_ref, far_ref)
    resid = resid_ref[...]
    inverse = lax.rsqrt(jnp.mean(resid * resid, axis=-1, keepdims=True) + EPSILON)
    d_resid = cot_ref[...].astype(F32) + norm_back(resid, inverse, gain_ref[...], d_normed)
    d_resid_ref[...] = d_resid
    d_branch = dot_nn(d_resid.astype(BF16), order_ref[...]).astype(BF16)
    d_low_ref[...] = d_branch[:, :middle]
    d_high_ref[...] = d_branch[:, middle:]
    d_attended = dot_nn(d_branch[:, :middle], w_low_ref[...])
    d_attended = d_attended + dot_nn(d_branch[:, middle:], w_high_ref[...])
    d_attended_ref[...] = d_attended.astype(BF16)
    gain_grad_ref[...] = sum_rows(d_normed * resid * inverse)


def project_out_back(terms, resid, cot, weights, order, gain, rows, seq):
    count, dim = resid.shape
    ordered = order.shape[1]
    width = dim
    return pl.pallas_call(
        out_back_kernel,
        grid=(1,),
        in_specs=[
            rows_of(rows, dim),
            rows_of(rows, dim),
            rows_of(rows, dim),
            rows_of(rows, dim),
            rows_of(rows, dim),
            pl.BlockSpec((rows, dim), lambda i: (seq, 0)),
            whole(weights[0]),
            whole(weights[1]),
            whole(order),
            whole(gain),
        ],
        out_specs=[
            rows_of(rows, dim),
            rows_of(rows, ordered // 2),
            rows_of(rows, ordered // 2),
            rows_of(rows, width),
            pl.BlockSpec((1, dim), lambda i: (0, 0)),
        ],
        out_shape=[
            jax.ShapeDtypeStruct((count, dim), F32),
            jax.ShapeDtypeStruct((count, ordered // 2), BF16),
            jax.ShapeDtypeStruct((count, ordered // 2), BF16),
            jax.ShapeDtypeStruct((count, width), BF16),
            jax.ShapeDtypeStruct((1, dim), F32),
        ],
        compiler_params=pltpu.CompilerParams(vmem_limit_bytes=VMEM_LIMIT),
        cost_estimate=pl.CostEstimate(flops=4 * count * dim * dim, bytes_accessed=12 * MIB, transcendentals=0),
        name="norm_back_project",
    )(*terms, resid, cot, weights[0], weights[1], order, gain)


def call_whole(kernel, operands, out_shape, flops, name):
    return pl.pallas_call(
        kernel,
        in_specs=[pl.BlockSpec(memory_space=pltpu.VMEM)] * len(operands),
        out_specs=[pl.BlockSpec(memory_space=pltpu.VMEM)] * len(out_shape),
        out_shape=out_shape,
        compiler_params=pltpu.CompilerParams(vmem_limit_bytes=VMEM_LIMIT),
        cost_estimate=pl.CostEstimate(flops=flops, bytes_accessed=16 * MIB, transcendentals=0),
        name=name,
    )(*operands)


def input_back_kernel(*refs):
    dqs, terms = refs[:2], refs[2:10]
    x_ref, d_resid_ref, w_low_ref, w_high_ref, order_ref, gain_ref, cos_ref, sin_ref = refs[10:18]
    d_kv_ref, input_grad_ref, gain_grad_ref, bias_grad_ref = refs[18:]
    dkv = jnp.concatenate([total_of(*terms[:4]), total_of(*terms[4:])], axis=0)
    dk = dkv[:, :LANES]
    dk = dk * cos_ref[...] - swap_halves(dk) * sin_ref[...]
    d_kv = jnp.concatenate([dk.astype(BF16), dkv[:, LANES:].astype(BF16)], axis=1)
    d_kv_ref[...] = d_kv
    dq = jnp.concatenate([ref[...] for ref in dqs], axis=0)
    d_joined = jnp.concatenate([dq, d_kv], axis=1)
    d_normed = jnp.concatenate([dot_nt(d_joined, w_low_ref[...]), dot_nt(d_joined, w_high_ref[...])], axis=1)
    d_normed = back_in_order(d_normed, order_ref[...])
    x = x_ref[...].astype(F32)
    inverse = lax.rsqrt(jnp.mean(x * x, axis=-1, keepdims=True) + EPSILON)
    input_grad_ref[...] = (d_resid_ref[...] + norm_back(x, inverse, gain_ref[...], d_normed)).astype(BF16)
    gain_grad_ref[...] = sum_rows(d_normed * x * inverse)
    bias_grad_ref[...] = sum_rows(d_joined.astype(F32))


def input_back(dq, terms, x, d_resid, weights, order, gain, cosine, sine):
    count, dim = x.shape
    joint = dq[0].shape[1] + 2 * LANES
    return call_whole(
        input_back_kernel,
        (*dq, *terms[0], *terms[1], x, d_resid, *weights, order, gain, cosine, sine),
        [
            jax.ShapeDtypeStruct((count, 2 * LANES), BF16),
            jax.ShapeDtypeStruct((count, dim), BF16),
            jax.ShapeDtypeStruct((1, dim), F32),
            jax.ShapeDtypeStruct((1, joint), F32),
        ],
        6 * count * dim * joint,
        "input_gradient",
    )


def seq_rows(seq, rows, cols):
    return pl.BlockSpec((rows, cols), lambda i: (seq, 0))


def piece_of(seq, rows):
    return pl.BlockSpec((1, rows, 2 * LANES), lambda i: (seq, 0, 0))


def keys_and_values(piece_refs):
    joint = jnp.concatenate([ref[0] for ref in piece_refs], axis=0)
    key, value = joint[:, :LANES], joint[:, LANES:]
    return (key, other_head(key)), (value, other_head(value))


def attend_kernel(block_ref, q_ref, kv_0, kv_1, kv_2, kv_3, start_ref, out_ref, level_ref):
    rows, width = q_ref.shape
    length = 4 * rows
    heads = width // HD
    group = heads // 2
    keys, values = keys_and_values((kv_0, kv_1, kv_2, kv_3))
    upper_key = lane_of((length, LANES)) >= HD
    upper = lane_of((rows, LANES)) >= HD
    query_at = block_ref[0] * rows + lax.broadcasted_iota(jnp.int32, (rows, length), 0)
    key_at = jnp.concatenate(
        [
            (block_ref[0] ^ place) * rows + lax.broadcasted_iota(jnp.int32, (rows, rows), 1)
            for place in range(4)
        ],
        axis=1,
    )
    allowed = (key_at <= query_at) & (key_at >= start_ref[:, :1])
    bias = jnp.where(allowed, 0.0, MASKED)
    one = jnp.ones((), BF16)
    lane = lane_of((rows, LANES))
    levels = jnp.zeros((rows, LANES), F32)
    for pair in range(heads // 2):
        at = slice(pair * LANES, (pair + 1) * LANES)
        both = q_ref[:, at]
        parts = []
        for place in range(2):
            owner = (2 * pair + place) // group
            moved = int(owner != place)
            side = upper if place else ~upper
            side_key = upper_key if place else ~upper_key
            query = jnp.where(side, both, jnp.zeros_like(both))
            score = dot_nt(query, keys[moved]) + bias
            top = jnp.max(score, axis=1, keepdims=True)
            weight = jnp.exp(score - top).astype(BF16)
            mixed = dot_nn(weight, jnp.where(side_key, values[moved], one))
            total = pltpu.roll(mixed, HD, 1)
            parts.append(mixed / total)
            level = top + jnp.log(total[:, place * HD : place * HD + 1])
            levels = jnp.where(lane == 2 * pair + place, level, levels)
        out_ref[:, at] = jnp.where(upper, parts[1], parts[0]).astype(BF16)
    level_ref[...] = levels


def attend(block, q, kv_pieces, start, rows, seq):
    width = q.shape[1]
    heads = width // HD
    return pl.pallas_call(
        attend_kernel,
        grid=(1,),
        in_specs=[
            pl.BlockSpec(memory_space=pltpu.SMEM),
            seq_rows(seq, rows, width),
            *[piece_of(seq, rows)] * 4,
            seq_rows(seq, rows, LANES),
        ],
        out_specs=[seq_rows(0, rows, width), seq_rows(0, rows, LANES)],
        out_shape=[jax.ShapeDtypeStruct((rows, width), BF16), jax.ShapeDtypeStruct((rows, LANES), F32)],
        compiler_params=pltpu.CompilerParams(vmem_limit_bytes=VMEM_LIMIT),
        cost_estimate=pl.CostEstimate(
            flops=32 * rows * rows * LANES * heads,
            bytes_accessed=4 * rows * width,
            transcendentals=4 * rows * rows * heads,
        ),
        name="attention_forward",
    )(block, q, *kv_pieces, start)


def attend_back_kernel(
    block_ref, q_ref, kv_0, kv_1, kv_2, kv_3, back_ref, out_ref, level_ref, start_ref, cos_ref, sin_ref,
    dq_ref, own_ref, core_ref, x_ref, far_ref, dk_sum, dv_sum,
):
    rows, width = q_ref.shape
    heads = width // HD
    group = heads // 2
    keys, values = keys_and_values((kv_0, kv_1, kv_2, kv_3))
    key_t = keys[0].astype(F32).T.astype(BF16)
    keys_t = (key_t, jnp.concatenate([key_t[HD:], key_t[:HD]], axis=0))
    upper = lane_of((rows, LANES)) >= HD
    upper_t = lax.broadcasted_iota(jnp.int32, (LANES, rows), 0) >= HD
    query_at = block_ref[0] * rows + lax.broadcasted_iota(jnp.int32, (rows, rows), 1)
    key_at = lax.broadcasted_iota(jnp.int32, (rows, rows), 0)
    biases = []
    for place in range(4):
        at = (block_ref[0] ^ place) * rows + key_at
        biases.append(jnp.where((at <= query_at) & (at >= start_ref[0, :1, :]), 0.0, MASKED))
    head_of = lax.broadcasted_iota(jnp.int32, (width, LANES), 0) // HD
    by_head = (head_of == lane_of((width, LANES))).astype(BF16)
    product = back_ref[...].astype(F32) * out_ref[...].astype(F32)
    product_high = product.astype(BF16)
    product_low = (product - product_high.astype(F32)).astype(BF16)
    row_sums = (dot_nn(product_high, by_head) + dot_nn(product_low, by_head)).T
    levels = level_ref[...].T
    cosine, sine = cos_ref[...], sin_ref[...]
    dk_sum[...] = jnp.zeros_like(dk_sum)
    dv_sum[...] = jnp.zeros_like(dv_sum)
    for pair in range(heads // 2):
        at = slice(pair * LANES, (pair + 1) * LANES)
        both = q_ref[:, at]
        back_both = back_ref[:, at]
        zero = jnp.zeros_like(both)
        sides = (~upper, upper)
        queries = [jnp.where(side, both, zero) for side in sides]
        backs = [jnp.where(side, back_both, zero) for side in sides]
        owners = [(2 * pair + place) // group for place in range(2)]
        d_query_t = [jnp.zeros((LANES, rows), F32) for _ in range(2)]
        for piece in range(4):
            span = slice(piece * rows, (piece + 1) * rows)
            probs, d_scores = [], []
            for place in range(2):
                head = 2 * pair + place
                moved = int(owners[place] != place)
                score = dot_nt(keys[moved][span], queries[place]) + biases[piece]
                prob = jnp.exp(score - levels[head : head + 1])
                d_prob = dot_nt(values[moved][span], backs[place])
                d_score = (prob * (d_prob - row_sums[head : head + 1])).astype(BF16)
                d_query_t[place] = d_query_t[place] + dot_nn(keys_t[moved][:, span], d_score)
                probs.append(prob.astype(BF16))
                d_scores.append(d_score)
            if owners[0] == owners[1]:
                dv_sum[owners[0], span] += dot_nn(
                    jnp.concatenate(probs, axis=1), jnp.concatenate(backs, axis=0)
                )
                dk_sum[owners[0], span] += dot_nn(
                    jnp.concatenate(d_scores, axis=1), jnp.concatenate(queries, axis=0)
                )
            else:
                for place in range(2):
                    dv_sum[owners[place], span] += dot_nn(probs[place], backs[place])
                    dk_sum[owners[place], span] += dot_nn(d_scores[place], queries[place])
        d_query = jnp.where(upper_t, d_query_t[1], d_query_t[0]).T * SCALE
        dq_ref[:, at] = (d_query * cosine - swap_halves(d_query) * sine).astype(BF16)
    lower_key = lane_of((4 * rows, LANES)) < HD
    for total, begin in ((dk_sum, 0), (dv_sum, LANES)):
        first, second = total[0], total[1]
        first = first + pltpu.roll(first, HD, 1)
        second = second + pltpu.roll(second, HD, 1)
        both = jnp.where(lower_key, first, second)
        cols = slice(begin, begin + LANES)
        own_ref[:, cols] = both[:rows]
        for place, ref in enumerate((core_ref, x_ref, far_ref)):
            ref[:, cols] = both[(place + 1) * rows : (place + 2) * rows].astype(BF16)


def parts_of(rows, cols):
    shapes = [jax.ShapeDtypeStruct((rows, cols), F32)] + [jax.ShapeDtypeStruct((rows, cols), BF16)] * 3
    return [seq_rows(0, rows, cols)] * 4, shapes


def attend_back(block, q, kv_pieces, back, out, level, start, cosine, sine, rows, seq):
    width = q.shape[1]
    length = 4 * rows
    heads = width // HD
    specs, shapes = parts_of(rows, 2 * LANES)
    return pl.pallas_call(
        attend_back_kernel,
        grid=(1,),
        in_specs=[
            pl.BlockSpec(memory_space=pltpu.SMEM),
            seq_rows(seq, rows, width),
            *[piece_of(seq, rows)] * 4,
            seq_rows(0, rows, width),
            seq_rows(0, rows, width),
            seq_rows(0, rows, LANES),
            pl.BlockSpec((1, 8, rows), lambda i: (seq, 0, 0)),
            seq_rows(seq, rows, LANES),
            seq_rows(seq, rows, LANES),
        ],
        out_specs=[seq_rows(0, rows, width), *specs],
        out_shape=[jax.ShapeDtypeStruct((rows, width), BF16), *shapes],
        scratch_shapes=[
            pltpu.VMEM((2, length, LANES), F32),
            pltpu.VMEM((2, length, LANES), F32),
        ],
        compiler_params=pltpu.CompilerParams(vmem_limit_bytes=VMEM_LIMIT),
        cost_estimate=pl.CostEstimate(
            flops=80 * rows * rows * LANES * heads,
            bytes_accessed=8 * rows * width,
            transcendentals=4 * rows * rows * heads,
        ),
        name="attention_backward",
    )(block, q, *kv_pieces, back, out, level, start, cosine, sine)


def mlp_kernel(
    n_0, n_1, n_2, n_3, c_0, c_1, c_2, c_3, w_ref,
    own_ref, out_1, out_2, out_3, d_own_ref, d_1, d_2, d_3, kept_ref, turned_ref,
    normed_all, cot_all,
):
    step = pl.program_id(0)
    rows = own_ref.shape[0]
    columns = w_ref.shape[1] // 3

    @pl.when(step == 0)
    def _():
        for place, (n_ref, c_ref) in enumerate(zip((n_0, n_1, n_2, n_3), (c_0, c_1, c_2, c_3))):
            normed_all[place // 2, (place % 2) * rows : (place % 2 + 1) * rows] = n_ref[...]
            cot_all[place // 2, (place % 2) * rows : (place % 2 + 1) * rows] = c_ref[...]

    normed, cot = normed_all[step], cot_all[step]
    for begin in range(0, columns, TILE):
        at = slice(begin, begin + TILE)
        gate = dot_nn(normed, w_ref[:, begin : begin + TILE])
        up = dot_nn(normed, w_ref[:, columns + begin : columns + begin + TILE])
        d_act = dot_nn(cot, w_ref[:, 2 * columns + begin : 2 * columns + begin + TILE])
        sigmoid = 0.5 * jnp.tanh(0.5 * gate) + 0.5
        swish = gate * sigmoid
        kept_ref[0, :, at] = (d_act * up * (sigmoid + swish * (1.0 - sigmoid))).astype(BF16)
        kept_ref[1, :, at] = (d_act * swish).astype(BF16)
        kept_ref[2, :, at] = (swish * up).astype(BF16)
    turned_ref[0] = normed.T
    turned_ref[1] = cot.T
    out = dot_nt(kept_ref[2], w_ref[:, 2 * columns :])
    d_normed = dot_nt(kept_ref[0], w_ref[:, :columns]) + dot_nt(kept_ref[1], w_ref[:, columns : 2 * columns])

    @pl.when(step == 0)
    def _():
        own_ref[...] = out[:rows]
        out_1[...] = out[rows:].astype(BF16)
        d_own_ref[...] = d_normed[:rows]
        d_1[...] = d_normed[rows:].astype(BF16)

    @pl.when(step == 1)
    def _():
        out_2[...] = out[:rows].astype(BF16)
        out_3[...] = out[rows:].astype(BF16)
        d_2[...] = d_normed[:rows].astype(BF16)
        d_3[...] = d_normed[rows:].astype(BF16)


def mlp(normed, cot, weights, seq):
    rows, dim = normed[0].shape
    columns = weights.shape[1] // 3
    specs, shapes = parts_of(rows, dim)
    once = lambda at: pl.BlockSpec((rows, dim), lambda i: (at, 0), pipeline_mode=pl.Buffered(1))
    return pl.pallas_call(
        mlp_kernel,
        grid=(2,),
        in_specs=[
            *[once(0)] * 4,
            *[once(seq)] * 3,
            once(0),
            pl.BlockSpec(weights.shape, lambda i: (0, 0), pipeline_mode=pl.Buffered(1)),
        ],
        out_specs=[
            *specs,
            *specs,
            pl.BlockSpec((3, 2 * rows, columns), lambda i: (0, i, 0)),
            pl.BlockSpec((2, dim, 2 * rows), lambda i: (0, 0, i)),
        ],
        out_shape=[
            *shapes,
            *shapes,
            jax.ShapeDtypeStruct((3, 4 * rows, columns), BF16),
            jax.ShapeDtypeStruct((2, dim, 4 * rows), BF16),
        ],
        scratch_shapes=[
            pltpu.VMEM((2, 2 * rows, dim), BF16),
            pltpu.VMEM((2, 2 * rows, dim), BF16),
        ],
        compiler_params=pltpu.CompilerParams(vmem_limit_bytes=VMEM_LIMIT),
        cost_estimate=pl.CostEstimate(
            flops=48 * rows * dim * columns,
            bytes_accessed=6 * dim * columns + 24 * rows * columns,
            transcendentals=4 * rows * columns,
        ),
        name="feed_forward",
    )(*normed, *cot, weights)


def mlp_grad_kernel(turned_0, turned_1, kept_0, kept_1, grad_ref):
    grad_ref[...] = (dot_nn(turned_0[0], kept_0[0]) + dot_nn(turned_1[0], kept_1[0])).astype(BF16)


def mlp_grad(turned, kept):
    _, dim, count = turned[0].shape
    columns = kept[0].shape[2]
    turned_block = pl.BlockSpec((1, dim, count), lambda i: (i // 2, 0, 0))
    kept_block = pl.BlockSpec((1, count, columns), lambda i: (i, 0, 0))
    return pl.pallas_call(
        mlp_grad_kernel,
        grid=(3,),
        in_specs=[turned_block, turned_block, kept_block, kept_block],
        out_specs=pl.BlockSpec((dim, columns), lambda i: (0, i)),
        out_shape=jax.ShapeDtypeStruct((dim, 3 * columns), BF16),
        compiler_params=pltpu.CompilerParams(vmem_limit_bytes=VMEM_LIMIT),
        cost_estimate=pl.CostEstimate(
            flops=12 * count * dim * columns,
            bytes_accessed=6 * dim * columns + 12 * count * columns,
            transcendentals=0,
        ),
        name="feed_forward_gradients",
    )(*turned, *kept)


def pack_kernel(block_ref, gate_ref, up_ref, down_ref, *refs):
    out_refs, scratch = refs[:4], refs[4]
    shard, ff = gate_ref.shape
    quarter = scratch.shape[2] // 4
    for place, ref in enumerate((gate_ref, up_ref, down_ref)):
        scratch[place, :, :ff] = ref[...].astype(F32)
        scratch[place, :, ff:] = jnp.zeros((shard, 4 * quarter - ff), F32)
    for place, out_ref in enumerate(out_refs):
        begin = pl.multiple_of((block_ref[0] ^ place) * quarter, LANES)
        for part in range(3):
            out_ref[:, part * quarter : (part + 1) * quarter] = scratch[part, :, pl.ds(begin, quarter)].astype(BF16)


def pack(block, gate, up, down_t, quarter):
    shard = gate.shape[0]
    return pl.pallas_call(
        pack_kernel,
        in_specs=[pl.BlockSpec(memory_space=pltpu.SMEM)] + [pl.BlockSpec(memory_space=pltpu.VMEM)] * 3,
        out_specs=[pl.BlockSpec(memory_space=pltpu.VMEM)] * 4,
        out_shape=[jax.ShapeDtypeStruct((shard, 3 * quarter), BF16)] * 4,
        scratch_shapes=[pltpu.VMEM((3, shard, 4 * quarter), F32)],
        compiler_params=pltpu.CompilerParams(vmem_limit_bytes=VMEM_LIMIT),
        name="pack_columns",
    )(block, gate, up, down_t)


def pick(options, index):
    value = options[0]
    for place in range(1, len(options)):
        value = jnp.where(index == place, options[place], value)
    return value


def assemble_kernel(block_ref, *refs):
    pieces, out_ref, scratch = refs[:4], refs[4], refs[5]
    shard = pieces[0].shape[0]
    values = [ref[...].astype(F32) for ref in pieces]
    for owner in range(4):
        scratch[owner * shard : (owner + 1) * shard] = pick(values, block_ref[0] ^ owner)
    out_ref[...] = scratch[...].astype(BF16)


def assemble(block, pieces):
    shard, columns = pieces[0].shape
    return pl.pallas_call(
        assemble_kernel,
        in_specs=[pl.BlockSpec(memory_space=pltpu.SMEM)] + [pl.BlockSpec(memory_space=pltpu.VMEM)] * 4,
        out_specs=pl.BlockSpec(memory_space=pltpu.VMEM),
        out_shape=jax.ShapeDtypeStruct((4 * shard, columns), BF16),
        scratch_shapes=[pltpu.VMEM((4 * shard, columns), F32)],
        compiler_params=pltpu.CompilerParams(vmem_limit_bytes=VMEM_LIMIT),
        name="assemble_rows",
    )(block, *pieces)


def cut_kernel(block_ref, value_ref, *refs):
    out_refs, scratch = refs[:4], refs[4]
    shard = out_refs[0].shape[0]
    scratch[...] = value_ref[...].astype(F32)
    values = [scratch[owner * shard : (owner + 1) * shard] for owner in range(4)]
    for place, out_ref in enumerate(out_refs):
        out_ref[...] = pick(values, block_ref[0] ^ place).astype(BF16)


def cut(block, value):
    shard, columns = value.shape[0] // 4, value.shape[1]
    return pl.pallas_call(
        cut_kernel,
        in_specs=[pl.BlockSpec(memory_space=pltpu.SMEM), pl.BlockSpec(memory_space=pltpu.VMEM)],
        out_specs=[pl.BlockSpec(memory_space=pltpu.VMEM)] * 4,
        out_shape=[jax.ShapeDtypeStruct((shard, columns), BF16)] * 4,
        scratch_shapes=[pltpu.VMEM(value.shape, F32)],
        compiler_params=pltpu.CompilerParams(vmem_limit_bytes=VMEM_LIMIT),
        name="cut_rows",
    )(block, value)


def unpack_kernel(block_ref, *refs):
    pieces, out_refs, scratch = refs[:4], refs[4:7], refs[7]
    ff = out_refs[0].shape[1]
    quarter = scratch.shape[2] // 4
    for place, ref in enumerate(pieces):
        begin = pl.multiple_of((block_ref[0] ^ place) * quarter, LANES)
        for part in range(3):
            scratch[part, :, pl.ds(begin, quarter)] = ref[:, part * quarter : (part + 1) * quarter].astype(F32)
    for part, out_ref in enumerate(out_refs):
        out_ref[...] = scratch[part, :, :ff]


def unpack(block, pieces, ff):
    shard, columns = pieces[0].shape
    return pl.pallas_call(
        unpack_kernel,
        in_specs=[pl.BlockSpec(memory_space=pltpu.SMEM)] + [pl.BlockSpec(memory_space=pltpu.VMEM)] * 4,
        out_specs=[pl.BlockSpec(memory_space=pltpu.VMEM)] * 3,
        out_shape=[jax.ShapeDtypeStruct((shard, ff), F32)] * 3,
        scratch_shapes=[pltpu.VMEM((3, shard, columns // 3 * 4), F32)],
        compiler_params=pltpu.CompilerParams(vmem_limit_bytes=VMEM_LIMIT),
        name="unpack_columns",
    )(block, *pieces)


def bit_swap(value, axis, bit=0):
    size = lax.axis_size(axis)
    return lax.ppermute(value, axis, [(i, i ^ (1 << bit)) for i in range(size)])


def jump_swap(value, axes, jump):
    return lax.ppermute(value, axes, [(i, i ^ jump) for i in range(4)])


def to_plane(value, slot):
    high, low = slot >> 1, slot & 1
    pairs = [
        (4 * y + 2 * x + c, 4 * (c ^ low) + 2 * (x ^ high) + y) for y in range(2) for x in range(2) for c in range(2)
    ]
    return lax.ppermute(value, TOKENS + ("cc",), pairs)


def from_plane(value, slot):
    high, low = slot >> 1, slot & 1
    pairs = [
        (4 * y + 2 * x + c, 4 * c + 2 * (x ^ high) + (y ^ low)) for y in range(2) for x in range(2) for c in range(2)
    ]
    return lax.ppermute(value, TOKENS + ("cc",), pairs)


def after(first, *values):
    return lax.optimization_barrier((first, *values))


def gather_four(value, axes):
    from_first = bit_swap(value, axes[0])
    return [value, bit_swap(value, axes[1]), from_first, bit_swap(from_first, axes[1])]


def gather_direct(value, axes):
    return [value] + [jump_swap(value, axes, jump) for jump in range(1, 4)]


def sum_direct(axes, own, *away):
    return [own] + [jump_swap(value, axes, jump + 1) for jump, value in enumerate(away)]


def doubling_offsets(steps):
    weight = {"cc": 1, "cx": 2, "fy": 4, "fz": 8}
    offsets = [0]
    for axis, bit in steps:
        offsets += [offset ^ (weight[axis] << bit) for offset in offsets]
    return jnp.array(offsets, jnp.int32)


def double(value, axis, bit=0):
    return jnp.concatenate([value, bit_swap(value, axis, bit)], axis=0)


def plane_gather(value):
    return jnp.concatenate(gather_direct(value, TOKENS), axis=0)


def plane_sum(value):
    parts = jnp.split(value, 4, axis=0)
    terms = sum_direct(TOKENS, *parts)
    return sum(term.astype(F32) for term in terms).astype(BF16)


def core_sum(keep, send):
    return (keep.astype(F32) + bit_swap(send.astype(BF16), "cc").astype(F32)).astype(BF16)


def halve(value, axis, bit=0):
    middle = value.shape[0] // 2
    came = bit_swap(value[middle:], axis, bit)
    return (value[:middle].astype(F32) + came.astype(F32)).astype(BF16)


def on_device(
    hidden,
    segments,
    attn_gain,
    qkv_weight,
    qkv_bias,
    out_weight,
    mlp_gain,
    gate_weight,
    up_weight,
    down_weight,
    cotangent,
):
    seqs, rows, dim = hidden.shape
    count = seqs * rows
    shard = attn_gain.shape[0]
    world = dim // shard
    joint = qkv_weight.shape[1]
    width = joint - 2 * LANES
    ff = gate_weight.shape[1]
    block = lax.axis_index("cx") * lax.axis_size("cc") + lax.axis_index("cc")
    me = lax.axis_index(FSDP) * lax.axis_size(CTX) + block
    offset = block * rows
    block_arg = block.reshape(1).astype(jnp.int32)
    plane_arg = (lax.axis_index("cx") * 2 + lax.axis_index("fy")).reshape(1).astype(jnp.int32)
    x = hidden.reshape(count, dim)
    cot = cotangent.reshape(count, dim)

    cot_x = bit_swap(cot, "cx")

    far = [("fz", bit) for bit in reversed(range((lax.axis_size("fz")).bit_length() - 1))]
    padded = -(-(shard + 1) // 16) * 16
    small = jnp.concatenate([attn_gain, mlp_gain, qkv_bias])
    small_row = jnp.pad(small, (0, joint + width - small.shape[0]))[None]
    first = jnp.concatenate(
        [
            jnp.concatenate([qkv_weight, out_weight.T], axis=1),
            small_row,
            jnp.zeros((padded - shard - 1, joint + width), BF16),
        ],
        axis=0,
    )
    first = double(first, *far[0])

    quarter = -(-ff // (4 * TILE)) * TILE
    first, *pieces = after(first, *pack(block_arg, gate_weight, up_weight, down_weight.T, quarter))
    pieces = [to_plane(piece, slot) for slot, piece in enumerate(pieces)]
    for axis, bit in far[1:]:
        first = double(first, axis, bit)

    within = jnp.arange(padded, dtype=jnp.int32)
    owner = me ^ doubling_offsets(far + [("cx", 0), ("fy", 0), ("cc", 0)])
    target = jnp.where(within[None, :] < shard, owner[:, None] * shard + within[None, :], -1).reshape(1, -1)
    order = (jnp.arange(dim, dtype=jnp.int32)[:, None] == target).astype(BF16)
    place = jnp.where(within[None, :] == shard, owner[:, None], -1).reshape(1, -1)
    spread = (jnp.arange(world, dtype=jnp.int32)[:, None] == place).astype(BF16)

    at_row = lax.dynamic_slice_in_dim(segments, offset, rows, axis=1)
    zeros_before = jnp.sum((segments < 1).astype(jnp.int32), axis=1, keepdims=True)
    ones_before = jnp.sum((segments < 2).astype(jnp.int32), axis=1, keepdims=True)
    start = jnp.where(at_row == 0, 0, jnp.where(at_row == 1, zeros_before, ones_before))
    position = (offset + jnp.arange(rows, dtype=jnp.int32)[None, :] - start).reshape(count)
    lane = jnp.arange(LANES, dtype=jnp.int32)
    frequency = ROPE_BASE ** (-(lane % (HD // 2)).astype(F32) * 2.0 / HD)
    angle = position.astype(F32)[:, None] * frequency[None, :]
    cosine = jnp.cos(angle)
    sine = jnp.where(lane % HD < HD // 2, -1.0, 1.0)[None, :] * jnp.sin(angle)
    start_column = jnp.broadcast_to(start.reshape(count, 1), (count, LANES))
    start_row = jnp.broadcast_to(start[:, None, :], (seqs, 8, rows))

    first, cot_x, cot_late, order, spread, cosine, sine, start_column, *pieces = after(
        first, cot_x, cot, order, spread, cosine, sine, start_column, *pieces
    )
    w_joint = plane_gather(first[:, :joint])
    mlp_shard = assemble(plane_arg, pieces)
    mlp_weights = lax.all_gather(mlp_shard, WEIGHTS, axis=0, tiled=True)
    w_joint, cot_late = after(w_joint, cot_late)
    w_joint = (w_joint, bit_swap(w_joint, "cc"))
    cot_y = bit_swap(cot_late, "fy")

    normed_low, normed_high, q, kv, gain_attn, gain_mlp = prep(x, order, spread, w_joint, cosine, sine, rows)
    kv_all = gather_four(kv.reshape(seqs, rows, 2 * LANES), CTX)
    kv_all[3], out_rows, cot_y = after(kv_all[3], first[:, joint:], cot_y)
    w_out = plane_gather(out_rows)
    attended, levels, resid, normed_all = [], [], [], []
    for seq in range(seqs):
        turn = block_arg if seq == 0 else after(resid[0], block_arg)[1]
        attended_one, level_one = attend(turn, q, kv_all, start_column, rows, seq)
        if seq == 0:
            attended_one, w_out, far_0, far_1 = after(attended_one, w_out, cot_x[:rows], cot_y[rows:])
            cot_far = [bit_swap(far_0, "fy"), bit_swap(far_1, "cx")]
            w_out = (w_out, bit_swap(w_out, "cc"))
        else:
            attended_one, *cot_far = after(attended_one, *cot_far)
        attended.append(attended_one)
        levels.append(level_one)
        resid_one, normed_one = project_out(attended[seq], x, w_out, order, gain_mlp, rows, seq)
        resid.append(resid_one)
        normed_all.append(gather_direct(normed_one, TOKENS))

    out_parts, d_terms, kept, turned = [], [], [], []
    for seq in range(seqs):
        if seq == 1:
            out_parts[0], normed_all[1] = lax.optimization_barrier((out_parts[0], normed_all[1]))
        result = mlp(normed_all[seq], [cot, cot_x, cot_y, cot_far[seq]], mlp_weights, seq)
        out_parts.append(result[:4])
        d_terms.append(sum_direct(TOKENS, *result[4:8]))
        kept.append(result[8])
        turned.append(result[9])
    d_resid, d_low, d_high, d_attended, mlp_gain_grad, dq, dkv_terms, out_terms = [], [], [], [], [], [], [], []
    for seq in range(seqs):
        if seq == 0:
            _, *d_terms[0] = after(kept[1], *d_terms[0])
        else:
            dq[0], d_terms[1][0], *out_terms[0] = after(dq[0], d_terms[1][0], *out_terms[0])
        result = project_out_back(d_terms[seq], resid[seq], cot, w_out, order, gain_mlp, rows, seq)
        for place, value in zip((d_resid, d_low, d_high, d_attended, mlp_gain_grad), result):
            place.append(value)
        out_terms.append(sum_direct(TOKENS, *after(d_terms[seq][1], *out_parts[seq])[1:]))
        if seq == 0:
            _, turned[1] = after(d_resid[0], turned[1])
            grads = mlp_grad(turned, kept)
            grads, d_attended[0], *d_terms[1] = after(grads, d_attended[0], *d_terms[1])
            grads = lax.psum_scatter(
                grads.reshape(world // 4, 4 * shard, 3 * quarter), WEIGHTS, scatter_dimension=0, tiled=False
            )
        else:
            both = jnp.concatenate(attended, axis=0)
            out_grad = core_sum(
                dot_tn(jnp.concatenate(d_low, axis=0), both).astype(BF16), dot_tn(jnp.concatenate(d_high, axis=0), both)
            )
            d_attended[1], *dkv_terms[0] = after(d_attended[1], *dkv_terms[0])
        result = attend_back(
            block_arg, q, kv_all, d_attended[seq], attended[seq], levels[seq], start_row, cosine, sine, rows, seq
        )
        dq.append(result[0])
        dkv_terms.append(sum_direct(CTX, *result[1:]))
    dq[1], out_grad, *out_terms[1] = after(dq[1], out_grad, *out_terms[1])
    dq_both = jnp.concatenate(dq, axis=0)
    q_grad = core_sum(dot_tn(normed_low, dq_both).astype(BF16), dot_tn(normed_high, dq_both))
    q_grad, *dkv_terms[1] = after(q_grad, *dkv_terms[1])
    q_grad = plane_sum(q_grad)
    d_resid = jnp.concatenate(d_resid, axis=0)
    d_kv, input_grad, attn_gain_grad, bias_grad = input_back(
        dq, dkv_terms, x, d_resid, w_joint, order, gain_attn, cosine, sine
    )
    d_kv, q_grad, attn_gain_grad, bias_grad = after(d_kv, q_grad, attn_gain_grad, bias_grad)

    output = []
    for seq in range(seqs):
        own, *away = out_terms[seq]
        output.append((resid[seq] + own + sum(term.astype(F32) for term in away)).astype(BF16))

    split_at = width + LANES
    bias_grad = bias_grad[0]
    small_grads = jnp.concatenate(
        [
            attn_gain_grad.reshape(world, -1),
            sum(mlp_gain_grad).reshape(world, -1),
            bias_grad[:split_at].reshape(world, -1),
            bias_grad[split_at:].reshape(world, -1),
        ],
        axis=1,
    ).astype(BF16)
    small_count = small_grads.shape[1]
    small_grads = jnp.pad(small_grads, ((0, 0), (0, 2 * LANES - small_count)))
    middle = spread.shape[1] // 2
    kv_grad = core_sum(
        (dot_tn(normed_low, d_kv) + dot_tn(spread[:, :middle], small_grads)).astype(BF16),
        dot_tn(normed_high, d_kv) + dot_tn(spread[:, middle:], small_grads),
    )
    pieces = cut(plane_arg, lax.optimization_barrier(grads))
    kv_grad, *pieces = after(kv_grad, *pieces)
    pieces = [from_plane(piece, slot) for slot, piece in enumerate(pieces)]
    kv_grad, out_grad = plane_sum(kv_grad), plane_sum(out_grad)
    first_sum = jnp.concatenate([q_grad, kv_grad, out_grad], axis=1)
    for axis, bit in reversed(far):
        first_sum = halve(first_sum, axis, bit)
    gate_grad, up_grad, down_grad_t = unpack(block_arg, pieces, ff)
    first_sum = first_sum.astype(F32)
    qkv_sum, out_sum = first_sum[:, :joint], first_sum[:, joint:]
    small_sum = qkv_sum[shard, width : width + small_count]
    at = (shard, 2 * shard, 2 * shard + split_at // world)

    return (
        jnp.stack(output),
        input_grad.reshape(hidden.shape),
        small_sum[: at[0]],
        qkv_sum[:shard],
        small_sum[at[1] : at[2]],
        small_sum[at[2] :],
        out_sum[:shard].T,
        small_sum[at[0] : at[1]],
        gate_grad,
        up_grad,
        down_grad_t.T,
    )


def solution(mesh):
    fsdp, ctx = mesh.shape["fsdp"], mesh.shape["ctx"]
    inner = Mesh(mesh.devices.reshape(fsdp // 2, 2, 2, ctx // 2), AXES)
    tokens = P(FSDP, CTX, None)
    vector = P(AXES)
    by_row = P(AXES, None)
    by_column = P(None, AXES)
    return jax.shard_map(
        on_device,
        mesh=inner,
        in_specs=(
            tokens,
            P(FSDP, None),
            vector,
            by_row,
            vector,
            by_column,
            vector,
            by_row,
            by_row,
            by_column,
            tokens,
        ),
        out_specs=(
            tokens,
            tokens,
            vector,
            by_row,
            vector,
            vector,
            by_column,
            vector,
            by_row,
            by_row,
            by_column,
        ),
        check_vma=False,
    )
```

profile of v0, /device:TPU:0, one launch (start us, length us, event | category | flops | bytes accessed | tf_op | source)
XLA Modules:
  0.0 362.6 jit_solution(9260295157277473659)
XLA Ops:
  9.0 4.1 %collective-permute-start = (bf16[32,2048]{1,0:T(8,128)(2,1)S(1)}, bf16[32,2048]{1,0:T(8,128)(2,1)S(1)}, u32[]{:S(2)}, u32[]{:S(2)}) collective-permute-start(bf16[32,2048]{1,0:T(8,128)(2,1)S(1)} %pad_maximum_fusion.7), channel_id=1, source_target_pairs={{0,16},{8,24},{16,0},{24,8},{1,17},{9,25},{17,1},{25,9},{2,18},{10... | collective-permute-start | bytes 393224 | tf_op jit(solution)/shard_map/ppermute | solution.py:729
  13.1 1.5 collective-permute-start.2
  17.1 1.8 fusion.14
  18.9 2.2 pack_columns.1
  21.9 1.6 collective-permute-start.1
  23.6 2.0 fusion.order_ref.refs_14_
  26.2 2.8 collective-permute-start.4
  29.6 2.2 collective-permute-start.6
  31.8 4.9 %collective-permute-done.4.refs_1_ = bf16[28,3840]{1,0:T(8,128)(2,1)S(1)} collective-permute-done((bf16[28,3840]{1,0:T(8,128)(2,1)S(1)}, bf16[28,3840]{1,0:T(8,128)(2,1)S(1)}, u32[]{:S(2)}, u32[]{:S(2)}) %collective-permute-start.4) | collective-permute-done | bytes 215072 | tf_op jit(solution)/shard_map/ppermute | solution.py:741
  36.7 5.1 %collective-permute-done.5.refs_2_ = bf16[28,3840]{1,0:T(8,128)(2,1)S(1)} collective-permute-done((bf16[28,3840]{1,0:T(8,128)(2,1)S(1)}, bf16[28,3840]{1,0:T(8,128)(2,1)S(1)}, u32[]{:S(2)}, u32[]{:S(2)}) %collective-permute-start.5) | collective-permute-done | bytes 215072 | tf_op jit(solution)/shard_map/ppermute | solution.py:741
  41.9 2.8 collective-permute-done.6.refs_3_
  45.7 2.9 assemble_rows.1
  49.8 2.9 collective-permute-start.8
  52.7 5.9 %collective-permute-done.7 = bf16[128,1152]{1,0:T(8,128)(2,1)S(1)} collective-permute-done((bf16[128,1152]{1,0:T(8,128)(2,1)S(1)}, bf16[128,1152]{1,0:T(8,128)(2,1)S(1)}, u32[]{:S(2)}, u32[]{:S(2)}) %collective-permute-start.7) | collective-permute-done | bytes 294944 | tf_op jit(solution)/shard_map/ppermute | solution.py:733
  58.6 6.7 %collective-permute-done.8 = bf16[128,1152]{1,0:T(8,128)(2,1)S(1)} collective-permute-done((bf16[128,1152]{1,0:T(8,128)(2,1)S(1)}, bf16[128,1152]{1,0:T(8,128)(2,1)S(1)}, u32[]{:S(2)}, u32[]{:S(2)}) %collective-permute-start.8) | collective-permute-done | bytes 294944 | tf_op jit(solution)/shard_map/ppermute | solution.py:733
  66.2 1.8 collective-permute-start.14
  70.1 8.0 %norm_project_rotate.1 = (bf16[512,512]{1,0:T(8,128)(2,1)}, bf16[512,512]{1,0:T(8,128)(2,1)}, bf16[512,896]{1,0:T(8,128)(2,1)}, bf16[512,256]{1,0:T(8,128)(2,1)}, f32[1,896]{1,0:T(1,128)}, /*index=5*/f32[1,896]{1,0:T(1,128)}) custom-call(bf16[512,896]{1,0:T(8,128)(2,1)} %bitcast.47, bf16[896,1024]{1,0:T(8,128)(2,1)} %fusion.order_ref.refs_14_, ...), custom_call_target="tpu_custom_call" | custom-call | flops 2147483648 | bytes 12582912 | tf_op jit(solution)/shard_map/norm_project_rotate/pallas_call | solution.py:119
  78.1 1.5 collective-permute-start.12
  79.6 7.1 %collective-permute-done.12.kv_2 = bf16[2,256,256]{2,1,0:T(8,128)(2,1)S(1)} collective-permute-done((bf16[2,256,256]{2,1,0:T(8,128)(2,1)}, bf16[2,256,256]{2,1,0:T(8,128)(2,1)S(1)}, u32[]{:S(2)}, u32[]{:S(2)}) %collective-permute-start.12) | collective-permute-done | bytes 262176 | tf_op jit(solution)/shard_map/ppermute | solution.py:729
  87.3 1.7 collective-permute-done.14.c_2
  89.1 1.5 collective-permute-start.15
  91.4 1.2 collective-permute-start.17
  93.7 9.4 %attention_forward.2 = (bf16[256,896]{1,0:T(8,128)(2,1)}, f32[256,128]{1,0:T(8,128)}) custom-call(s32[1]{0:T(128)} %bitcast.block_ref, bf16[512,896]{1,0:T(8,128)(2,1)} %get-tuple-element.184.q_ref, bf16[2,256,256]{2,1,0:T(8,128)(2,1)} %bitcast.61, bf16[2,256,256]{2,1,0:T(8,128)(2,1)} %collective-permute-done.11.kv_1, bf16[2,256,256]{2,1,0:T(8,128)(2,1)} %copy-done.61, ...), custom_call_target="tpu_custom_call" | custom-call | flops 3758096384 | bytes 917504 | tf_op jit(solution)/shard_map/attention_forward/pallas_call | solution.py:377
  103.3 1.8 collective-permute-start.22
  106.7 5.3 %project_out_norm.2 = (f32[256,896]{1,0:T(8,128)}, bf16[256,896]{1,0:T(8,128)(2,1)}) custom-call(bf16[256,896]{1,0:T(8,128)(2,1)} %get-tuple-element.193.attended_ref.out_ref, bf16[512,896]{1,0:T(8,128)(2,1)} %bitcast.48, bf16[512,896]{1,0:T(8,128)(2,1)} %copy-done, bf16[512,896]{1,0:T(8,128)(2,1)} %copy-done.1, bf16[896,1024]{1,0:T(8,128)(2,1)} %fusion.order_ref.refs_14_, ...), custom_call_target="tpu_custom_call" | custom-call | flops 1233125376 | bytes 8388608 | tf_op jit(solution)/shard_map/project_out_norm/pallas_call | solution.py:174
  112.0 1.5 collective-permute-start.19
  115.5 9.8 %attention_forward.3 = (bf16[256,896]{1,0:T(8,128)(2,1)}, f32[256,128]{1,0:T(8,128)}) custom-call(s32[1]{0:T(128)} %bitcast.block_ref, bf16[512,896]{1,0:T(8,128)(2,1)} %get-tuple-element.184.q_ref, bf16[2,256,256]{2,1,0:T(8,128)(2,1)} %bitcast.62, bf16[2,256,256]{2,1,0:T(8,128)(2,1)} %collective-permute-done.11.kv_1, bf16[2,256,256]{2,1,0:T(8,128)(2,1)} %copy-done.61, ...), custom_call_target="tpu_custom_call" | custom-call | flops 3758096384 | bytes 917504 | tf_op jit(solution)/shard_map/attention_forward/pallas_call | solution.py:377
  125.3 5.6 %project_out_norm.3 = (f32[256,896]{1,0:T(8,128)}, bf16[256,896]{1,0:T(8,128)(2,1)}) custom-call(bf16[256,896]{1,0:T(8,128)(2,1)} %get-tuple-element.212.attended_ref.out_ref, bf16[512,896]{1,0:T(8,128)(2,1)} %bitcast.49, bf16[512,896]{1,0:T(8,128)(2,1)} %copy-done, bf16[512,896]{1,0:T(8,128)(2,1)} %copy-done.1, bf16[896,1024]{1,0:T(8,128)(2,1)} %fusion.order_ref.refs_14_, ...), custom_call_target="tpu_custom_call" | custom-call | flops 1233125376 | bytes 8388608 | tf_op jit(solution)/shard_map/project_out_norm/pallas_call | solution.py:174
  130.9 1.5 collective-permute-start.24
  134.4 3.5 collective-permute-done.21.n_3
  138.0 25.5 %feed_forward.2 = (f32[256,896]{1,0:T(8,128)}, bf16[256,896]{1,0:T(8,128)(2,1)}, bf16[256,896]{1,0:T(8,128)(2,1)}, bf16[256,896]{1,0:T(8,128)(2,1)}, f32[256,896...) custom-call(bf16[256,896]{1,0:T(8,128)(2,1)} %get-tuple-element.197., ...), custom_call_target="tpu_custom_call" | custom-call | flops 14092861440 | bytes 14745600 | tf_op jit(solution)/shard_map/feed_forward/pallas_call | solution.py:565
  163.5 1.5 collective-permute-start.27
  167.1 25.8 %feed_forward.3 = (f32[256,896]{1,0:T(8,128)}, bf16[256,896]{1,0:T(8,128)(2,1)}, bf16[256,896]{1,0:T(8,128)(2,1)}, bf16[256,896]{1,0:T(8,128)(2,1)}, f32[256,896...) custom-call(bf16[256,896]{1,0:T(8,128)(2,1)} %get-tuple-element.214., ...), custom_call_target="tpu_custom_call" | custom-call | flops 14092861440 | bytes 14745600 | tf_op jit(solution)/shard_map/feed_forward/pallas_call | solution.py:565
  192.9 1.5 collective-permute-start.30
  195.2 1.2 collective-permute-start.32
  197.4 5.8 %norm_back_project.2 = (f32[256,896]{1,0:T(8,128)}, bf16[256,512]{1,0:T(8,128)(2,1)}, bf16[256,512]{1,0:T(8,128)(2,1)}, bf16[256,896]{1,0:T(8,128)(2,1)}, f32[1,896]{1,0:T(1,128)}) custom-call(f32[256,896]{1,0:T(8,128)} %get-tuple-element.224.own_ref, bf16[256,896]{1,0:T(8,128)(2,1)} %copy-done.31, bf16[256,896]{1,0:T(8,128)(2,1)} %copy-done.32, ...), custom_call_target="tpu_custom_call" | custom-call | flops 822083584 | bytes 12582912 | tf_op jit(solution)/shard_map/norm_back_project/pallas_call | solution.py:233
  203.2 20.1 %feed_forward_gradients.1 = bf16[896,3840]{1,0:T(8,128)(2,1)} custom-call(bf16[2,896,1024]{2,1,0:T(8,128)(2,1)} %get-tuple-element.207.turned_0, bf16[2,896,1024]{2,1,0:T(8,128)(2,1)} %get-tuple-element.230.turned_1, bf16[3,1024,1280]{2,1,0:T(8,128)(2,1)} %get-tuple-element.231.kept_0, bf16[3,1024,1280]{2,1,0:T(8,128)(2,1)} %get-tuple-element.219.kept_1), custom_call_target="tpu_custom_call" | custom-call | flops 14092861440 | bytes 22609920 | tf_op jit(solution)/shard_map/feed_forward_gradients/pallas_call | solution.py:609
  225.0 1.5 collective-permute-start.33
  228.6 1.4 collective-permute-start.40
  231.4 18.4 %attention_backward.2 = (bf16[256,896]{1,0:T(8,128)(2,1)}, f32[256,256]{1,0:T(8,128)}, bf16[256,256]{1,0:T(8,128)(2,1)}, bf16[256,256]{1,0:T(8,128)(2,1)}, bf16[256,256]{1,0:T(8,128)(2,1)}) custom-call(s32[1]{0:T(128)} %bitcast.block_ref, bf16[512,896]{1,0:T(8,128)(2,1)} %get-tuple-element.184.q_ref, bf16[2,256,256]{2,1,0:T(8,128)(2,1)} %bitcast.63, ...), custom_call_target="tpu_custom_call" | custom-call | flops 9395240960 | bytes 1835008 | tf_op jit(solution)/shard_map/attention_backward/pallas_call | solution.py:484
  250.0 1.5 collective-permute-start.37
  251.8 5.9 %norm_back_project.3 = (f32[256,896]{1,0:T(8,128)}, bf16[256,512]{1,0:T(8,128)(2,1)}, bf16[256,512]{1,0:T(8,128)(2,1)}, bf16[256,896]{1,0:T(8,128)(2,1)}, f32[1,896]{1,0:T(1,128)}) custom-call(f32[256,896]{1,0:T(8,128)} %get-tuple-element.254.own_ref, bf16[256,896]{1,0:T(8,128)(2,1)} %copy-done.28, bf16[256,896]{1,0:T(8,128)(2,1)} %copy-done.29, ...), custom_call_target="tpu_custom_call" | custom-call | flops 822083584 | bytes 12582912 | tf_op jit(solution)/shard_map/norm_back_project/pallas_call | solution.py:233
  257.8 2.6 convolution_convert_fusion.2
  262.3 18.2 %attention_backward.3 = (bf16[256,896]{1,0:T(8,128)(2,1)}, f32[256,256]{1,0:T(8,128)}, bf16[256,256]{1,0:T(8,128)(2,1)}, bf16[256,256]{1,0:T(8,128)(2,1)}, bf16[256,256]{1,0:T(8,128)(2,1)}) custom-call(s32[1]{0:T(128)} %bitcast.block_ref, bf16[512,896]{1,0:T(8,128)(2,1)} %get-tuple-element.184.q_ref, bf16[2,256,256]{2,1,0:T(8,128)(2,1)} %bitcast.64, ...), custom_call_target="tpu_custom_call" | custom-call | flops 9395240960 | bytes 1835008 | tf_op jit(solution)/shard_map/attention_backward/pallas_call | solution.py:484
  280.7 2.0 add_convert_fusion.1
  282.9 1.7 convolution_convert_fusion
  286.7 1.4 pad_maximum_fusion.refs_11_
  291.3 1.4 add_convert_fusion
  293.7 1.7 collective-permute-start.47
  297.2 9.1 %input_gradient.1 = (bf16[512,256]{1,0:T(8,128)(2,1)}, bf16[512,896]{1,0:T(8,128)(2,1)}, f32[1,896]{1,0:T(1,128)}, f32[1,1152]{1,0:T(1,128)}) custom-call(bf16[256,896]{1,0:T(8,128)(2,1)} %get-tuple-element.282.refs_0_, bf16[256,896]{1,0:T(8,128)(2,1)} %get-tuple-element.283.refs_1_, f32[256,256]{1,0:T(8,128)} %get-tuple-element.284.refs_2_, ...), custom_call_target="tpu_custom_call" | custom-call | flops 3170893824 | bytes 16777216 | tf_op jit(solution)/shard_map/input_gradient/pallas_call | solution.py:269
  306.9 1.7 collective-permute-done.49
  308.6 1.3 add_convert_fusion.6
  314.0 1.6 collective-permute-start.55
  317.4 3.0 cut_rows.1
  321.2 1.6 collective-permute-start.52
  324.0 2.9 collective-permute-done.55
  327.1 1.3 add_convert_fusion.5
  328.4 1.2 collective-permute-done.52
  329.8 1.5 collective-permute-start.57
  331.4 1.3 fusion.13
  333.4 2.7 collective-permute-start.60
  339.6 5.6 %collective-permute-done.60.refs_1_ = bf16[28,3840]{1,0:T(8,128)(2,1)S(1)} collective-permute-done((bf16[28,3840]{1,0:T(8,128)(2,1)S(1)}, bf16[28,3840]{1,0:T(8,128)(2,1)S(1)}, u32[]{:S(2)}, u32[]{:S(2)}) %collective-permute-start.60) | collective-permute-done | bytes 215072 | tf_op jit(solution)/shard_map/ppermute | solution.py:749
  345.2 3.9 %collective-permute-done.62.refs_3_ = bf16[28,3840]{1,0:T(8,128)(2,1)S(1)} collective-permute-done((bf16[28,3840]{1,0:T(8,128)(2,1)S(1)}, bf16[28,3840]{1,0:T(8,128)(2,1)S(1)}, u32[]{:S(2)}, u32[]{:S(2)}) %collective-permute-start.62) | collective-permute-done | bytes 215072 | tf_op jit(solution)/shard_map/ppermute | solution.py:749
  349.8 2.7 unpack_columns.1
  (318 shorter events, 55.9 us)
Async XLA Ops:
  7.2 130.8 %all-gather.2.cloned.1.call-start = ((), (), s32[]{:S(2)}) async-start(), calls=%async_computation.1 | async-start | bytes 7741440 | tf_op jit(solution)/shard_map/all_gather | solution.py:876
  9.0 12.9 %collective-permute-start = (bf16[32,2048]{1,0:T(8,128)(2,1)S(1)}, bf16[32,2048]{1,0:T(8,128)(2,1)S(1)}, u32[]{:S(2)}, u32[]{:S(2)}) collective-permute-start(bf16[32,2048]{1,0:T(8,128)(2,1)S(1)} %pad_maximum_fusion.7), channel_id=1, source_target_pairs={{0,16},{8,24},{16,0},{24,8},{1,17},{9,25},{17,1},{25,9},{2,18},{10... | collective-permute-start | bytes 393224 | tf_op jit(solution)/shard_map/ppermute | solution.py:729
  13.1 31.6 %collective-permute-start.2 = (bf16[512,896]{1,0:T(8,128)(2,1)}, bf16[512,896]{1,0:T(8,128)(2,1)S(1)}, u32[]{:S(2)}, u32[]{:S(2)}) collective-permute-start(bf16[512,896]{1,0:T(8,128)(2,1)} %bitcast.41), channel_id=1, source_target_pairs={{0,2},{2,0},{1,3},{3,1},{4,6},{6,4},{5,7},{7,5},{8,10},{10,8},{9,1... | collective-permute-start | bytes 2752520 | tf_op jit(solution)/shard_map/ppermute | solution.py:729
  21.9 7.6 %collective-permute-start.1 = (bf16[64,2048]{1,0:T(8,128)(2,1)S(1)}, bf16[64,2048]{1,0:T(8,128)(2,1)S(1)}, u32[]{:S(2)}, u32[]{:S(2)}) collective-permute-start(bf16[64,2048]{1,0:T(8,128)(2,1)S(1)} %pad_maximum_fusion.6), channel_id=1, source_target_pairs={{0,8},{8,0},{16,24},{24,16},{1,9},{9,1},{17,25},{25,17},{2,10},{10... | collective-permute-start | bytes 786440 | tf_op jit(solution)/shard_map/ppermute | solution.py:729
  25.6 6.2 %collective-permute-start.3 = (bf16[28,3840]{1,0:T(8,128)(2,1)S(1)}, bf16[28,3840]{1,0:T(8,128)(2,1)S(1)}, u32[]{:S(2)}, u32[]{:S(2)}) collective-permute-start(bf16[28,3840]{1,0:T(8,128)(2,1)S(1)} %copy-done.73), channel_id=1, source_target_pairs={{0,0},{1,4},{2,2},{3,6},{4,1},{5,5},{6,3},{7,7},{8,8},{9,12},{10,1... | collective-permute-start | bytes 645128 | tf_op jit(solution)/shard_map/ppermute | solution.py:741
  26.2 10.5 %collective-permute-start.4 = (bf16[28,3840]{1,0:T(8,128)(2,1)S(1)}, bf16[28,3840]{1,0:T(8,128)(2,1)S(1)}, u32[]{:S(2)}, u32[]{:S(2)}) collective-permute-start(bf16[28,3840]{1,0:T(8,128)(2,1)S(1)} %copy-done.72), channel_id=1, source_target_pairs={{0,4},{1,0},{2,6},{3,2},{4,5},{5,1},{6,7},{7,3},{8,12},{9,8},{10,1... | collective-permute-start | bytes 645128 | tf_op jit(solution)/shard_map/ppermute | solution.py:741
  29.0 12.8 %collective-permute-start.5 = (bf16[28,3840]{1,0:T(8,128)(2,1)S(1)}, bf16[28,3840]{1,0:T(8,128)(2,1)S(1)}, u32[]{:S(2)}, u32[]{:S(2)}) collective-permute-start(bf16[28,3840]{1,0:T(8,128)(2,1)S(1)} %copy-done.71), channel_id=1, source_target_pairs={{0,2},{1,6},{2,0},{3,4},{4,3},{5,7},{6,1},{7,5},{8,10},{9,14},{10,... | collective-permute-start | bytes 645128 | tf_op jit(solution)/shard_map/ppermute | solution.py:741
  29.6 15.1 %collective-permute-start.6 = (bf16[28,3840]{1,0:T(8,128)(2,1)S(1)}, bf16[28,3840]{1,0:T(8,128)(2,1)S(1)}, u32[]{:S(2)}, u32[]{:S(2)}) collective-permute-start(bf16[28,3840]{1,0:T(8,128)(2,1)S(1)} %copy-done.70), channel_id=1, source_target_pairs={{0,6},{1,2},{2,4},{3,0},{4,7},{5,3},{6,5},{7,1},{8,14},{9,10},{10,... | collective-permute-start | bytes 645128 | tf_op jit(solution)/shard_map/ppermute | solution.py:741
  48.6 268.8 %reduce-scatter.2.cloned.1.call-start = ((), (), s32[]{:S(2)}) async-start(), calls=%async_computation.2 | async-start | bytes 7741440 | tf_op jit(solution)/shard_map/reduce_scatter | solution.py:924
  48.7 9.9 %collective-permute-start.7 = (bf16[128,1152]{1,0:T(8,128)(2,1)S(1)}, bf16[128,1152]{1,0:T(8,128)(2,1)S(1)}, u32[]{:S(2)}, u32[]{:S(2)}) collective-permute-start(bf16[128,1152]{1,0:T(8,128)(2,1)S(1)} %slice.80), channel_id=1, source_target_pairs={{0,2},{2,0},{4,6},{6,4},{1,3},{3,1},{5,7},{7,5},{8,10},{10,8},{12,... | collective-permute-start | bytes 884744 | tf_op jit(solution)/shard_map/ppermute | solution.py:733
  49.8 15.5 %collective-permute-start.8 = (bf16[128,1152]{1,0:T(8,128)(2,1)S(1)}, bf16[128,1152]{1,0:T(8,128)(2,1)S(1)}, u32[]{:S(2)}, u32[]{:S(2)}) collective-permute-start(bf16[128,1152]{1,0:T(8,128)(2,1)S(1)} %slice.80), channel_id=1, source_target_pairs={{0,4},{2,6},{4,0},{6,2},{1,5},{3,7},{5,1},{7,3},{8,12},{10,14},{12... | collective-permute-start | bytes 884744 | tf_op jit(solution)/shard_map/ppermute | solution.py:733
  52.7 13.3 %collective-permute-start.9 = (bf16[128,1152]{1,0:T(8,128)(2,1)S(1)}, bf16[128,1152]{1,0:T(8,128)(2,1)S(1)}, u32[]{:S(2)}, u32[]{:S(2)}) collective-permute-start(bf16[128,1152]{1,0:T(8,128)(2,1)S(1)} %slice.80), channel_id=1, source_target_pairs={{0,6},{2,4},{4,2},{6,0},{1,7},{3,5},{5,3},{7,1},{8,14},{10,12},{12... | collective-permute-start | bytes 884744 | tf_op jit(solution)/shard_map/ppermute | solution.py:733
  66.1 2.9 collective-permute-start.10
  66.2 22.9 %collective-permute-start.14 = (bf16[512,896]{1,0:T(8,128)(2,1)S(1)}, bf16[512,896]{1,0:T(8,128)(2,1)}, u32[]{:S(2)}, u32[]{:S(2)}) collective-permute-start(bf16[512,896]{1,0:T(8,128)(2,1)S(1)} %bitcast.46), channel_id=1, source_target_pairs={{0,4},{4,0},{1,5},{5,1},{2,6},{6,2},{3,7},{7,3},{8,12},{12,8},{9,1... | collective-permute-start | bytes 2752520 | tf_op jit(solution)/shard_map/ppermute | solution.py:729
  78.1 8.6 %collective-permute-start.12 = (bf16[2,256,256]{2,1,0:T(8,128)(2,1)}, bf16[2,256,256]{2,1,0:T(8,128)(2,1)S(1)}, u32[]{:S(2)}, u32[]{:S(2)}) collective-permute-start(bf16[2,256,256]{2,1,0:T(8,128)(2,1)} %bitcast.59), channel_id=1, source_target_pairs={{0,2},{2,0},{1,3},{3,1},{4,6},{6,4},{5,7},{7,5},{8,10},{10,8},{9,1... | collective-permute-start | bytes 786440 | tf_op jit(solution)/shard_map/ppermute | solution.py:729
  86.7 6.9 %collective-permute-start.11 = (bf16[2,256,256]{2,1,0:T(8,128)(2,1)}, bf16[2,256,256]{2,1,0:T(8,128)(2,1)}, u32[]{:S(2)}, u32[]{:S(2)}) collective-permute-start(bf16[2,256,256]{2,1,0:T(8,128)(2,1)} %bitcast.60), channel_id=1, source_target_pairs={{0,1},{1,0},{2,3},{3,2},{4,5},{5,4},{6,7},{7,6},{8,9},{9,8},{10,11... | collective-permute-start | bytes 786440 | tf_op jit(solution)/shard_map/ppermute | solution.py:729
  89.1 14.0 %collective-permute-start.15 = (bf16[128,896]{1,0:T(8,128)(2,1)S(1)}, bf16[128,896]{1,0:T(8,128)(2,1)S(1)}, u32[]{:S(2)}, u32[]{:S(2)}) collective-permute-start(bf16[128,896]{1,0:T(8,128)(2,1)S(1)} %slice.81), channel_id=1, source_target_pairs={{0,2},{2,0},{4,6},{6,4},{1,3},{3,1},{5,7},{7,5},{8,10},{10,8},{12,... | collective-permute-start | bytes 688136 | tf_op jit(solution)/shard_map/ppermute | solution.py:733
  90.5 12.6 %collective-permute-start.16 = (bf16[128,896]{1,0:T(8,128)(2,1)S(1)}, bf16[128,896]{1,0:T(8,128)(2,1)S(1)}, u32[]{:S(2)}, u32[]{:S(2)}) collective-permute-start(bf16[128,896]{1,0:T(8,128)(2,1)S(1)} %slice.81), channel_id=1, source_target_pairs={{0,4},{2,6},{4,0},{6,2},{1,5},{3,7},{5,1},{7,3},{8,12},{10,14},{12... | collective-permute-start | bytes 688136 | tf_op jit(solution)/shard_map/ppermute | solution.py:733
  91.4 11.7 %collective-permute-start.17 = (bf16[128,896]{1,0:T(8,128)(2,1)S(1)}, bf16[128,896]{1,0:T(8,128)(2,1)S(1)}, u32[]{:S(2)}, u32[]{:S(2)}) collective-permute-start(bf16[128,896]{1,0:T(8,128)(2,1)S(1)} %slice.81), channel_id=1, source_target_pairs={{0,6},{2,4},{4,2},{6,0},{1,7},{3,5},{5,3},{7,1},{8,14},{10,12},{12... | collective-permute-start | bytes 688136 | tf_op jit(solution)/shard_map/ppermute | solution.py:733
  103.2 2.5 collective-permute-start.18
  103.3 22.0 %collective-permute-start.22 = (bf16[256,896]{1,0:T(8,128)(2,1)S(1)}, bf16[256,896]{1,0:T(8,128)(2,1)S(1)}, u32[]{:S(2)}, u32[]{:S(2)}) collective-permute-start(bf16[256,896]{1,0:T(8,128)(2,1)S(1)} %slice.82), channel_id=1, source_target_pairs={{0,4},{4,0},{1,5},{5,1},{2,6},{6,2},{3,7},{7,3},{8,12},{12,8},{9,1... | collective-permute-start | bytes 1376264 | tf_op jit(solution)/shard_map/ppermute | solution.py:729
  105.1 20.2 %collective-permute-start.23 = (bf16[256,896]{1,0:T(8,128)(2,1)S(1)}, bf16[256,896]{1,0:T(8,128)(2,1)S(1)}, u32[]{:S(2)}, u32[]{:S(2)}) collective-permute-start(bf16[256,896]{1,0:T(8,128)(2,1)S(1)} %slice.83), channel_id=1, source_target_pairs={{0,2},{2,0},{1,3},{3,1},{4,6},{6,4},{5,7},{7,5},{8,10},{10,8},{9,1... | collective-permute-start | bytes 1376264 | tf_op jit(solution)/shard_map/ppermute | solution.py:729
  112.0 21.6 %collective-permute-start.19 = (bf16[256,896]{1,0:T(8,128)(2,1)}, bf16[256,896]{1,0:T(8,128)(2,1)S(1)}, u32[]{:S(2)}, u32[]{:S(2)}) collective-permute-start(bf16[256,896]{1,0:T(8,128)(2,1)} %get-tuple-element.197.n_0), channel_id=1, source_target_pairs={{0,2},{2,0},{4,6},{6,4},{1,3},{3,1},{5,7},{7,5},{8,10},{10,8},{12,... | collective-permute-start | bytes 1376264 | tf_op jit(solution)/shard_map/ppermute | solution.py:733
  113.4 21.0 %collective-permute-start.20 = (bf16[256,896]{1,0:T(8,128)(2,1)}, bf16[256,896]{1,0:T(8,128)(2,1)}, u32[]{:S(2)}, u32[]{:S(2)}) collective-permute-start(bf16[256,896]{1,0:T(8,128)(2,1)} %get-tuple-element.197.n_0), channel_id=1, source_target_pairs={{0,4},{2,6},{4,0},{6,2},{1,5},{3,7},{5,1},{7,3},{8,12},{10,14},{12... | collective-permute-start | bytes 1376264 | tf_op jit(solution)/shard_map/ppermute | solution.py:733
  114.6 23.4 %collective-permute-start.21 = (bf16[256,896]{1,0:T(8,128)(2,1)}, bf16[256,896]{1,0:T(8,128)(2,1)}, u32[]{:S(2)}, u32[]{:S(2)}) collective-permute-start(bf16[256,896]{1,0:T(8,128)(2,1)} %get-tuple-element.197.n_0), channel_id=1, source_target_pairs={{0,6},{2,4},{4,2},{6,0},{1,7},{3,5},{5,3},{7,1},{8,14},{10,12},{12... | collective-permute-start | bytes 1376264 | tf_op jit(solution)/shard_map/ppermute | solution.py:733
  130.9 32.6 %collective-permute-start.24 = (bf16[256,896]{1,0:T(8,128)(2,1)}, bf16[256,896]{1,0:T(8,128)(2,1)S(1)}, u32[]{:S(2)}, u32[]{:S(2)}) collective-permute-start(bf16[256,896]{1,0:T(8,128)(2,1)} %get-tuple-element.214.n_0), channel_id=1, source_target_pairs={{0,2},{2,0},{4,6},{6,4},{1,3},{3,1},{5,7},{7,5},{8,10},{10,8},{12,... | collective-permute-start | bytes 1376264 | tf_op jit(solution)/shard_map/ppermute | solution.py:733
  132.4 31.1 %collective-permute-start.25 = (bf16[256,896]{1,0:T(8,128)(2,1)}, bf16[256,896]{1,0:T(8,128)(2,1)S(1)}, u32[]{:S(2)}, u32[]{:S(2)}) collective-permute-start(bf16[256,896]{1,0:T(8,128)(2,1)} %get-tuple-element.214.n_0), channel_id=1, source_target_pairs={{0,4},{2,6},{4,0},{6,2},{1,5},{3,7},{5,1},{7,3},{8,12},{10,14},{12... | collective-permute-start | bytes 1376264 | tf_op jit(solution)/shard_map/ppermute | solution.py:733
  133.6 29.9 %collective-permute-start.26 = (bf16[256,896]{1,0:T(8,128)(2,1)}, bf16[256,896]{1,0:T(8,128)(2,1)S(1)}, u32[]{:S(2)}, u32[]{:S(2)}) collective-permute-start(bf16[256,896]{1,0:T(8,128)(2,1)} %get-tuple-element.214.n_0), channel_id=1, source_target_pairs={{0,6},{2,4},{4,2},{6,0},{1,7},{3,5},{5,3},{7,1},{8,14},{10,12},{12... | collective-permute-start | bytes 1376264 | tf_op jit(solution)/shard_map/ppermute | solution.py:733
  163.5 31.7 %collective-permute-start.27 = (bf16[256,896]{1,0:T(8,128)(2,1)}, bf16[256,896]{1,0:T(8,128)(2,1)S(1)}, u32[]{:S(2)}, u32[]{:S(2)}) collective-permute-start(bf16[256,896]{1,0:T(8,128)(2,1)} %get-tuple-element.221), channel_id=1, source_target_pairs={{0,2},{2,0},{4,6},{6,4},{1,3},{3,1},{5,7},{7,5},{8,10},{10,8},{12,... | collective-permute-start | bytes 1376264 | tf_op jit(solution)/shard_map/ppermute | solution.py:733
  165.0 31.3 %collective-permute-start.28 = (bf16[256,896]{1,0:T(8,128)(2,1)}, bf16[256,896]{1,0:T(8,128)(2,1)S(1)}, u32[]{:S(2)}, u32[]{:S(2)}) collective-permute-start(bf16[256,896]{1,0:T(8,128)(2,1)} %get-tuple-element.222), channel_id=1, source_target_pairs={{0,4},{2,6},{4,0},{6,2},{1,5},{3,7},{5,1},{7,3},{8,12},{10,14},{12... | collective-permute-start | bytes 1376264 | tf_op jit(solution)/shard_map/ppermute | solution.py:733
  165.9 30.5 %collective-permute-start.29 = (bf16[256,896]{1,0:T(8,128)(2,1)}, bf16[256,896]{1,0:T(8,128)(2,1)S(1)}, u32[]{:S(2)}, u32[]{:S(2)}) collective-permute-start(bf16[256,896]{1,0:T(8,128)(2,1)} %get-tuple-element.223), channel_id=1, source_target_pairs={{0,6},{2,4},{4,2},{6,0},{1,7},{3,5},{5,3},{7,1},{8,14},{10,12},{12... | collective-permute-start | bytes 1376264 | tf_op jit(solution)/shard_map/ppermute | solution.py:733
  192.9 30.4 %collective-permute-start.30 = (bf16[256,896]{1,0:T(8,128)(2,1)}, bf16[256,896]{1,0:T(8,128)(2,1)S(1)}, u32[]{:S(2)}, u32[]{:S(2)}) collective-permute-start(bf16[256,896]{1,0:T(8,128)(2,1)} %get-tuple-element.234), channel_id=1, source_target_pairs={{0,2},{2,0},{4,6},{6,4},{1,3},{3,1},{5,7},{7,5},{8,10},{10,8},{12,... | collective-permute-start | bytes 1376264 | tf_op jit(solution)/shard_map/ppermute | solution.py:733
  194.3 28.9 %collective-permute-start.31 = (bf16[256,896]{1,0:T(8,128)(2,1)}, bf16[256,896]{1,0:T(8,128)(2,1)S(1)}, u32[]{:S(2)}, u32[]{:S(2)}) collective-permute-start(bf16[256,896]{1,0:T(8,128)(2,1)} %get-tuple-element.235), channel_id=1, source_target_pairs={{0,4},{2,6},{4,0},{6,2},{1,5},{3,7},{5,1},{7,3},{8,12},{10,14},{12... | collective-permute-start | bytes 1376264 | tf_op jit(solution)/shard_map/ppermute | solution.py:733
  195.2 28.1 %collective-permute-start.32 = (bf16[256,896]{1,0:T(8,128)(2,1)}, bf16[256,896]{1,0:T(8,128)(2,1)S(1)}, u32[]{:S(2)}, u32[]{:S(2)}) collective-permute-start(bf16[256,896]{1,0:T(8,128)(2,1)} %get-tuple-element.236), channel_id=1, source_target_pairs={{0,6},{2,4},{4,2},{6,0},{1,7},{3,5},{5,3},{7,1},{8,14},{10,12},{12... | collective-permute-start | bytes 1376264 | tf_op jit(solution)/shard_map/ppermute | solution.py:733
  225.0 24.9 %collective-permute-start.33 = (bf16[256,896]{1,0:T(8,128)(2,1)}, bf16[256,896]{1,0:T(8,128)(2,1)S(1)}, u32[]{:S(2)}, u32[]{:S(2)}) collective-permute-start(bf16[256,896]{1,0:T(8,128)(2,1)} %get-tuple-element.246), channel_id=1, source_target_pairs={{0,2},{2,0},{4,6},{6,4},{1,3},{3,1},{5,7},{7,5},{8,10},{10,8},{12,... | collective-permute-start | bytes 1376264 | tf_op jit(solution)/shard_map/ppermute | solution.py:733
  226.5 23.5 %collective-permute-start.34 = (bf16[256,896]{1,0:T(8,128)(2,1)}, bf16[256,896]{1,0:T(8,128)(2,1)S(1)}, u32[]{:S(2)}, u32[]{:S(2)}) collective-permute-start(bf16[256,896]{1,0:T(8,128)(2,1)} %get-tuple-element.247), channel_id=1, source_target_pairs={{0,4},{2,6},{4,0},{6,2},{1,5},{3,7},{5,1},{7,3},{8,12},{10,14},{12... | collective-permute-start | bytes 1376264 | tf_op jit(solution)/shard_map/ppermute | solution.py:733
  227.4 24.2 %collective-permute-start.35 = (bf16[256,896]{1,0:T(8,128)(2,1)}, bf16[256,896]{1,0:T(8,128)(2,1)S(1)}, u32[]{:S(2)}, u32[]{:S(2)}) collective-permute-start(bf16[256,896]{1,0:T(8,128)(2,1)} %get-tuple-element.248), channel_id=1, source_target_pairs={{0,6},{2,4},{4,2},{6,0},{1,7},{3,5},{5,3},{7,1},{8,14},{10,12},{12... | collective-permute-start | bytes 1376264 | tf_op jit(solution)/shard_map/ppermute | solution.py:733
  228.6 54.2 %collective-permute-start.40 = (bf16[256,896]{1,0:T(8,128)(2,1)}, bf16[256,896]{1,0:T(8,128)(2,1)S(1)}, u32[]{:S(2)}, u32[]{:S(2)}) collective-permute-start(bf16[256,896]{1,0:T(8,128)(2,1)} %get-tuple-element.275), channel_id=1, source_target_pairs={{0,2},{2,0},{4,6},{6,4},{1,3},{3,1},{5,7},{7,5},{8,10},{10,8},{12,... | collective-permute-start | bytes 1376264 | tf_op jit(solution)/shard_map/ppermute | solution.py:733
  230.0 52.7 %collective-permute-start.41 = (bf16[256,896]{1,0:T(8,128)(2,1)}, bf16[256,896]{1,0:T(8,128)(2,1)S(1)}, u32[]{:S(2)}, u32[]{:S(2)}) collective-permute-start(bf16[256,896]{1,0:T(8,128)(2,1)} %get-tuple-element.276), channel_id=1, source_target_pairs={{0,4},{2,6},{4,0},{6,2},{1,5},{3,7},{5,1},{7,3},{8,12},{10,14},{12... | collective-permute-start | bytes 1376264 | tf_op jit(solution)/shard_map/ppermute | solution.py:733
  249.9 10.6 %collective-permute-start.36 = (bf16[256,256]{1,0:T(8,128)(2,1)}, bf16[256,256]{1,0:T(8,128)(2,1)S(1)}, u32[]{:S(2)}, u32[]{:S(2)}) collective-permute-start(bf16[256,256]{1,0:T(8,128)(2,1)} %get-tuple-element.260), channel_id=1, source_target_pairs={{0,1},{1,0},{2,3},{3,2},{4,5},{5,4},{6,7},{7,6},{8,9},{9,8},{10,11... | collective-permute-start | bytes 393224 | tf_op jit(solution)/shard_map/ppermute | solution.py:733
  250.0 11.6 %collective-permute-start.37 = (bf16[256,256]{1,0:T(8,128)(2,1)}, bf16[256,256]{1,0:T(8,128)(2,1)S(1)}, u32[]{:S(2)}, u32[]{:S(2)}) collective-permute-start(bf16[256,256]{1,0:T(8,128)(2,1)} %get-tuple-element.261), channel_id=1, source_target_pairs={{0,2},{1,3},{2,0},{3,1},{4,6},{5,7},{6,4},{7,5},{8,10},{9,11},{10,... | collective-permute-start | bytes 393224 | tf_op jit(solution)/shard_map/ppermute | solution.py:733
  251.5 10.7 %collective-permute-start.38 = (bf16[256,256]{1,0:T(8,128)(2,1)}, bf16[256,256]{1,0:T(8,128)(2,1)S(1)}, u32[]{:S(2)}, u32[]{:S(2)}) collective-permute-start(bf16[256,256]{1,0:T(8,128)(2,1)} %get-tuple-element.262), channel_id=1, source_target_pairs={{0,3},{1,2},{2,1},{3,0},{4,7},{5,6},{6,5},{7,4},{8,11},{9,10},{10,... | collective-permute-start | bytes 393224 | tf_op jit(solution)/shard_map/ppermute | solution.py:733
  260.4 22.3 %collective-permute-start.42 = (bf16[256,896]{1,0:T(8,128)(2,1)}, bf16[256,896]{1,0:T(8,128)(2,1)}, u32[]{:S(2)}, u32[]{:S(2)}) collective-permute-start(bf16[256,896]{1,0:T(8,128)(2,1)} %get-tuple-element.277), channel_id=1, source_target_pairs={{0,6},{2,4},{4,2},{6,0},{1,7},{3,5},{5,3},{7,1},{8,14},{10,12},{12... | collective-permute-start | bytes 1376264 | tf_op jit(solution)/shard_map/ppermute | solution.py:733
  261.6 19.0 %collective-permute-start.39 = (bf16[512,896]{1,0:T(8,128)(2,1)}, bf16[512,896]{1,0:T(8,128)(2,1)}, u32[]{:S(2)}, u32[]{:S(2)}) collective-permute-start(bf16[512,896]{1,0:T(8,128)(2,1)} %convolution_convert_fusion.2), channel_id=1, source_target_pairs={{0,1},{1,0},{2,3},{3,2},{4,5},{5,4},{6,7},{7,6},{8,9},{9,8},{10,11... | collective-permute-start | bytes 2752520 | tf_op jit(solution)/shard_map/ppermute | solution.py:729
  284.5 6.8 %collective-permute-start.43 = (bf16[512,896]{1,0:T(8,128)(2,1)}, bf16[512,896]{1,0:T(8,128)(2,1)}, u32[]{:S(2)}, u32[]{:S(2)}) collective-permute-start(bf16[512,896]{1,0:T(8,128)(2,1)} %convolution_convert_fusion), channel_id=1, source_target_pairs={{0,1},{1,0},{2,3},{3,2},{4,5},{5,4},{6,7},{7,6},{8,9},{9,8},{10,11... | collective-permute-start | bytes 2752520 | tf_op jit(solution)/shard_map/ppermute | solution.py:729
  284.7 8.0 %collective-permute-start.44 = (bf16[256,256]{1,0:T(8,128)(2,1)}, bf16[256,256]{1,0:T(8,128)(2,1)S(1)}, u32[]{:S(2)}, u32[]{:S(2)}) collective-permute-start(bf16[256,256]{1,0:T(8,128)(2,1)} %get-tuple-element.291), channel_id=1, source_target_pairs={{0,1},{1,0},{2,3},{3,2},{4,5},{5,4},{6,7},{7,6},{8,9},{9,8},{10,11... | collective-permute-start | bytes 393224 | tf_op jit(solution)/shard_map/ppermute | solution.py:733
  285.2 7.5 %collective-permute-start.45 = (bf16[256,256]{1,0:T(8,128)(2,1)}, bf16[256,256]{1,0:T(8,128)(2,1)S(1)}, u32[]{:S(2)}, u32[]{:S(2)}) collective-permute-start(bf16[256,256]{1,0:T(8,128)(2,1)} %get-tuple-element.292), channel_id=1, source_target_pairs={{0,2},{1,3},{2,0},{3,1},{4,6},{5,7},{6,4},{7,5},{8,10},{9,11},{10,... | collective-permute-start | bytes 393224 | tf_op jit(solution)/shard_map/ppermute | solution.py:733
  286.2 6.7 %collective-permute-start.46 = (bf16[256,256]{1,0:T(8,128)(2,1)S(1)}, bf16[256,256]{1,0:T(8,128)(2,1)S(1)}, u32[]{:S(2)}, u32[]{:S(2)}) collective-permute-start(bf16[256,256]{1,0:T(8,128)(2,1)S(1)} %copy-done.77), channel_id=1, source_target_pairs={{0,3},{1,2},{2,1},{3,0},{4,7},{5,6},{6,5},{7,4},{8,11},{9,10},{10,... | collective-permute-start | bytes 393224 | tf_op jit(solution)/shard_map/ppermute | solution.py:733
  293.7 12.6 %collective-permute-start.47 = (bf16[128,896]{1,0:T(8,128)(2,1)}, bf16[128,896]{1,0:T(8,128)(2,1)}, u32[]{:S(2)}, u32[]{:S(2)}) collective-permute-start(bf16[128,896]{1,0:T(8,128)(2,1)} %get-tuple-element.329), channel_id=1, source_target_pairs={{0,2},{2,0},{4,6},{6,4},{1,3},{3,1},{5,7},{7,5},{8,10},{10,8},{12,... | collective-permute-start | bytes 688136 | tf_op jit(solution)/shard_map/ppermute | solution.py:733
  295.4 11.5 %collective-permute-start.48 = (bf16[128,896]{1,0:T(8,128)(2,1)}, bf16[128,896]{1,0:T(8,128)(2,1)}, u32[]{:S(2)}, u32[]{:S(2)}) collective-permute-start(bf16[128,896]{1,0:T(8,128)(2,1)} %get-tuple-element.331), channel_id=1, source_target_pairs={{0,4},{2,6},{4,0},{6,2},{1,5},{3,7},{5,1},{7,3},{8,12},{10,14},{12... | collective-permute-start | bytes 688136 | tf_op jit(solution)/shard_map/ppermute | solution.py:733
  296.2 12.4 %collective-permute-start.49 = (bf16[128,896]{1,0:T(8,128)(2,1)S(1)}, bf16[128,896]{1,0:T(8,128)(2,1)}, u32[]{:S(2)}, u32[]{:S(2)}) collective-permute-start(bf16[128,896]{1,0:T(8,128)(2,1)S(1)} %get-tuple-element.330), channel_id=1, source_target_pairs={{0,6},{2,4},{4,2},{6,0},{1,7},{3,5},{5,3},{7,1},{8,14},{10,12},{12... | collective-permute-start | bytes 688136 | tf_op jit(solution)/shard_map/ppermute | solution.py:733
  312.3 4.7 %collective-permute-start.50 = (bf16[512,256]{1,0:T(8,128)(2,1)S(1)}, bf16[512,256]{1,0:T(8,128)(2,1)S(1)}, u32[]{:S(2)}, u32[]{:S(2)}) collective-permute-start(bf16[512,256]{1,0:T(8,128)(2,1)S(1)} %fusion.5), channel_id=1, source_target_pairs={{0,1},{1,0},{2,3},{3,2},{4,5},{5,4},{6,7},{7,6},{8,9},{9,8},{10,11... | collective-permute-start | bytes 786440 | tf_op jit(solution)/shard_map/ppermute | solution.py:729
  313.3 9.6 %collective-permute-start.54 = (bf16[128,896]{1,0:T(8,128)(2,1)}, bf16[128,896]{1,0:T(8,128)(2,1)}, u32[]{:S(2)}, u32[]{:S(2)}) collective-permute-start(bf16[128,896]{1,0:T(8,128)(2,1)} %get-tuple-element.332), channel_id=1, source_target_pairs={{0,2},{2,0},{4,6},{6,4},{1,3},{3,1},{5,7},{7,5},{8,10},{10,8},{12,... | collective-permute-start | bytes 688136 | tf_op jit(solution)/shard_map/ppermute | solution.py:733
  314.0 12.9 %collective-permute-start.55 = (bf16[128,896]{1,0:T(8,128)(2,1)}, bf16[128,896]{1,0:T(8,128)(2,1)}, u32[]{:S(2)}, u32[]{:S(2)}) collective-permute-start(bf16[128,896]{1,0:T(8,128)(2,1)} %get-tuple-element.334), channel_id=1, source_target_pairs={{0,4},{2,6},{4,0},{6,2},{1,5},{3,7},{5,1},{7,3},{8,12},{10,14},{12... | collective-permute-start | bytes 688136 | tf_op jit(solution)/shard_map/ppermute | solution.py:733
  315.6 11.5 %collective-permute-start.56 = (bf16[128,896]{1,0:T(8,128)(2,1)}, bf16[128,896]{1,0:T(8,128)(2,1)}, u32[]{:S(2)}, u32[]{:S(2)}) collective-permute-start(bf16[128,896]{1,0:T(8,128)(2,1)} %get-tuple-element.333), channel_id=1, source_target_pairs={{0,6},{2,4},{4,2},{6,0},{1,7},{3,5},{5,3},{7,1},{8,14},{10,12},{12... | collective-permute-start | bytes 688136 | tf_op jit(solution)/shard_map/ppermute | solution.py:733
  320.4 8.0 %collective-permute-start.51 = (bf16[128,256]{1,0:T(8,128)(2,1)S(1)}, bf16[128,256]{1,0:T(8,128)(2,1)S(1)}, u32[]{:S(2)}, u32[]{:S(2)}) collective-permute-start(bf16[128,256]{1,0:T(8,128)(2,1)S(1)} %get-tuple-element.337), channel_id=1, source_target_pairs={{0,2},{2,0},{4,6},{6,4},{1,3},{3,1},{5,7},{7,5},{8,10},{10,8},{12,... | collective-permute-start | bytes 196616 | tf_op jit(solution)/shard_map/ppermute | solution.py:733
  321.2 8.4 %collective-permute-start.52 = (bf16[128,256]{1,0:T(8,128)(2,1)S(1)}, bf16[128,256]{1,0:T(8,128)(2,1)S(1)}, u32[]{:S(2)}, u32[]{:S(2)}) collective-permute-start(bf16[128,256]{1,0:T(8,128)(2,1)S(1)} %get-tuple-element.339), channel_id=1, source_target_pairs={{0,4},{2,6},{4,0},{6,2},{1,5},{3,7},{5,1},{7,3},{8,12},{10,14},{12... | collective-permute-start | bytes 196616 | tf_op jit(solution)/shard_map/ppermute | solution.py:733
  322.8 6.8 %collective-permute-start.53 = (bf16[128,256]{1,0:T(8,128)(2,1)S(1)}, bf16[128,256]{1,0:T(8,128)(2,1)S(1)}, u32[]{:S(2)}, u32[]{:S(2)}) collective-permute-start(bf16[128,256]{1,0:T(8,128)(2,1)S(1)} %get-tuple-element.338), channel_id=1, source_target_pairs={{0,6},{2,4},{4,2},{6,0},{1,7},{3,5},{5,3},{7,1},{8,14},{10,12},{12... | collective-permute-start | bytes 196616 | tf_op jit(solution)/shard_map/ppermute | solution.py:733
  329.8 8.3 %collective-permute-start.57 = (bf16[64,2048]{1,0:T(8,128)(2,1)S(1)}, bf16[64,2048]{1,0:T(8,128)(2,1)S(1)}, u32[]{:S(2)}, u32[]{:S(2)}) collective-permute-start(bf16[64,2048]{1,0:T(8,128)(2,1)S(1)} %slice.105), channel_id=1, source_target_pairs={{0,8},{8,0},{16,24},{24,16},{1,9},{9,1},{17,25},{25,17},{2,10},{10... | collective-permute-start | bytes 786440 | tf_op jit(solution)/shard_map/ppermute | solution.py:729
  332.7 6.9 %collective-permute-start.59 = (bf16[28,3840]{1,0:T(8,128)(2,1)S(1)}, bf16[28,3840]{1,0:T(8,128)(2,1)S(1)}, u32[]{:S(2)}, u32[]{:S(2)}) collective-permute-start(bf16[28,3840]{1,0:T(8,128)(2,1)S(1)} %copy-done.69), channel_id=1, source_target_pairs={{0,0},{1,4},{2,2},{3,6},{4,1},{5,5},{6,3},{7,7},{8,8},{9,12},{10,1... | collective-permute-start | bytes 645128 | tf_op jit(solution)/shard_map/ppermute | solution.py:749
  333.4 11.8 %collective-permute-start.60 = (bf16[28,3840]{1,0:T(8,128)(2,1)S(1)}, bf16[28,3840]{1,0:T(8,128)(2,1)S(1)}, u32[]{:S(2)}, u32[]{:S(2)}) collective-permute-start(bf16[28,3840]{1,0:T(8,128)(2,1)S(1)} %copy-done.68), channel_id=1, source_target_pairs={{0,1},{1,5},{2,3},{3,7},{4,0},{5,4},{6,2},{7,6},{8,9},{9,13},{10,1... | collective-permute-start | bytes 645128 | tf_op jit(solution)/shard_map/ppermute | solution.py:749
  336.1 9.1 %collective-permute-start.61 = (bf16[28,3840]{1,0:T(8,128)(2,1)S(1)}, bf16[28,3840]{1,0:T(8,128)(2,1)S(1)}, u32[]{:S(2)}, u32[]{:S(2)}) collective-permute-start(bf16[28,3840]{1,0:T(8,128)(2,1)S(1)} %copy-done.67), channel_id=1, source_target_pairs={{0,2},{1,6},{2,0},{3,4},{4,3},{5,7},{6,1},{7,5},{8,10},{9,14},{10,... | collective-permute-start | bytes 645128 | tf_op jit(solution)/shard_map/ppermute | solution.py:749
  337.0 12.0 %collective-permute-start.62 = (bf16[28,3840]{1,0:T(8,128)(2,1)S(1)}, bf16[28,3840]{1,0:T(8,128)(2,1)S(1)}, u32[]{:S(2)}, u32[]{:S(2)}) collective-permute-start(bf16[28,3840]{1,0:T(8,128)(2,1)S(1)} %copy-done.66), channel_id=1, source_target_pairs={{0,3},{1,7},{2,1},{3,5},{4,2},{5,6},{6,0},{7,4},{8,11},{9,15},{10,... | collective-permute-start | bytes 645128 | tf_op jit(solution)/shard_map/ppermute | solution.py:749
  338.2 14.3 %collective-permute-start.58 = (bf16[32,2048]{1,0:T(8,128)(2,1)S(1)}, bf16[32,2048]{1,0:T(8,128)(2,1)S(1)}, u32[]{:S(2)}, u32[]{:S(2)}) collective-permute-start(bf16[32,2048]{1,0:T(8,128)(2,1)S(1)} %slice.107), channel_id=1, source_target_pairs={{0,16},{8,24},{16,0},{24,8},{1,17},{9,25},{17,1},{25,9},{2,18},{10... | collective-permute-start | bytes 393224 | tf_op jit(solution)/shard_map/ppermute | solution.py:729
  (82 other events, 505.5 us)
Sparse Core Ops, SparseCore 0:
  48.7 69.7 all-gather.1
  223.5 73.9 reduce-scatter.1
where the time goes:
time: 368 us; the launch traced here: 363 us
  Pallas kernels  178 us (48%)
  starting transfers between devices  70 us (19%)
  waiting for transfers between devices  57 us (15%)
  other arithmetic  18.3 us (5%)
  local copies, waits for them, and re-layouts  16 us (4%)
  between operations  15.4 us (4%)
  matrix products  8.2 us (2%)
    pallas_call x2, Pallas kernels, mlp(): pl.pallas_call(mlp_kernel, grid=(2,), in_specs=[*[once(0)] * 4, *[once(se...  51.3 us
    ppermute x39, starting transfers between devices, jump_swap(): return lax.ppermute(value, axes, [(i, i ^ jump) for i in range(4)])  43 us
    pallas_call x2, Pallas kernels, attend_back(): pl.pallas_call(attend_back_kernel, grid=(1,), in_specs=[pl.BlockSpec(memo...  36.6 us
    ppermute x39, waiting for transfers between devices, jump_swap(): return lax.ppermute(value, axes, [(i, i ^ jump) for i in range(4)])  23.7 us
    pallas_call x1, Pallas kernels, mlp_grad(): pl.pallas_call(mlp_grad_kernel, grid=(3,), in_specs=[turned_block, turned...  20.1 us
    pallas_call x2, Pallas kernels, attend(): pl.pallas_call(attend_kernel, grid=(1,), in_specs=[pl.BlockSpec(memory_sp...  19.3 us
    ppermute x16, starting transfers between devices, bit_swap(): return lax.ppermute(value, axis, [(i, i ^ 1 << bit) for i in range(size)])  16.2 us
    ppermute x4, waiting for transfers between devices, to_plane(): return lax.ppermute(value, TOKENS + ('cc',), pairs)  12.8 us
  transfers between devices with their start and end apart: 65, of which 21 were waited for; matrix products, arithmetic and copies ran while one was open for 8% of the time, Pallas kernels for 48%

commit v1 on v0

--- a/solution.py
+++ b/solution.py
@@ -527,16 +527,14 @@
             cot_all[place // 2, (place % 2) * rows : (place % 2 + 1) * rows] = c_ref[...]
 
     normed, cot = normed_all[step], cot_all[step]
-    for begin in range(0, columns, TILE):
-        at = slice(begin, begin + TILE)
-        gate = dot_nn(normed, w_ref[:, begin : begin + TILE])
-        up = dot_nn(normed, w_ref[:, columns + begin : columns + begin + TILE])
-        d_act = dot_nn(cot, w_ref[:, 2 * columns + begin : 2 * columns + begin + TILE])
-        sigmoid = 0.5 * jnp.tanh(0.5 * gate) + 0.5
-        swish = gate * sigmoid
-        kept_ref[0, :, at] = (d_act * up * (sigmoid + swish * (1.0 - sigmoid))).astype(BF16)
-        kept_ref[1, :, at] = (d_act * swish).astype(BF16)
-        kept_ref[2, :, at] = (swish * up).astype(BF16)
+    gate = dot_nn(normed, w_ref[:, :columns])
+    up = dot_nn(normed, w_ref[:, columns : 2 * columns])
+    d_act = dot_nn(cot, w_ref[:, 2 * columns :])
+    sigmoid = 0.5 * jnp.tanh(0.5 * gate) + 0.5
+    swish = gate * sigmoid
+    kept_ref[0] = (d_act * up * (sigmoid + swish * (1.0 - sigmoid))).astype(BF16)
+    kept_ref[1] = (d_act * swish).astype(BF16)
+    kept_ref[2] = (swish * up).astype(BF16)
     turned_ref[0] = normed.T
     turned_ref[1] = cot.T
     out = dot_nt(kept_ref[2], w_ref[:, 2 * columns :])
@@ -946,11 +944,6 @@
     )
     d_kv, q_grad, attn_gain_grad, bias_grad = after(d_kv, q_grad, attn_gain_grad, bias_grad)
 
-    output = []
-    for seq in range(seqs):
-        own, *away = out_terms[seq]
-        output.append((resid[seq] + own + sum(term.astype(F32) for term in away)).astype(BF16))
-
     split_at = width + LANES
     bias_grad = bias_grad[0]
     small_grads = jnp.concatenate(
@@ -974,8 +967,14 @@
     pieces = [from_plane(piece, slot) for slot, piece in enumerate(pieces)]
     kv_grad, out_grad = plane_sum(kv_grad), plane_sum(out_grad)
     first_sum = jnp.concatenate([q_grad, kv_grad, out_grad], axis=1)
+    first_sum, out_terms = lax.optimization_barrier((first_sum, out_terms))
     for axis, bit in reversed(far):
         first_sum = halve(first_sum, axis, bit)
+    output = []
+    for seq in range(seqs):
+        own, *away = out_terms[seq]
+        output.append((resid[seq] + own + sum(term.astype(F32) for term in away)).astype(BF16))
+
     gate_grad, up_grad, down_grad_t = unpack(block_arg, pieces, ff)
     first_sum = first_sum.astype(F32)
     qkv_sum, out_sum = first_sum[:, :joint], first_sum[:, joint:]

time: 368 us -> 366 us (level)
    ppermute x4, waiting for transfers between devices: 9.45 us -> 1.83 us  [from_plane(): return lax.ppermute(value, TOKENS + ('cc',), pairs)]
    ppermute x16, waiting for transfers between devices: 10.9 us -> 16.7 us  [bit_swap(): return lax.ppermute(value, axis, [(i, i ^ 1 << bit) for i in range(size)])]
    unnamed x166 -> x152, local copies, waits for them, and re-layouts: 7.66 us -> 6 us
  transfers between devices with their start and end apart: 65 -> 65, of which waited for: 21 -> 21; matrix products, arithmetic and copies ran while one was open for 8% -> 8% of each run, Pallas kernels for 48% -> 49%
where the time goes in v1:
time: 366 us; the launch traced here: 360 us
  Pallas kernels  179 us (49%)
  starting transfers between devices  70.6 us (19%)
  waiting for transfers between devices  55.8 us (15%)
  other arithmetic  18 us (5%)
  between operations  15.3 us (4%)
  local copies, waits for them, and re-layouts  14.3 us (4%)
  matrix products  7.24 us (2%)
    pallas_call x2, Pallas kernels, mlp(): pl.pallas_call(mlp_kernel, grid=(2,), in_specs=[*[once(0)] * 4, *[once(se...  52.3 us
    ppermute x39, starting transfers between devices, jump_swap(): return lax.ppermute(value, axes, [(i, i ^ jump) for i in range(4)])  43 us
    pallas_call x2, Pallas kernels, attend_back(): pl.pallas_call(attend_back_kernel, grid=(1,), in_specs=[pl.BlockSpec(memo...  36.6 us
    ppermute x39, waiting for transfers between devices, jump_swap(): return lax.ppermute(value, axes, [(i, i ^ jump) for i in range(4)])  24.3 us
    pallas_call x1, Pallas kernels, mlp_grad(): pl.pallas_call(mlp_grad_kernel, grid=(3,), in_specs=[turned_block, turned...  20.1 us
    pallas_call x2, Pallas kernels, attend(): pl.pallas_call(attend_kernel, grid=(1,), in_specs=[pl.BlockSpec(memory_sp...  19.3 us
    ppermute x16, waiting for transfers between devices, bit_swap(): return lax.ppermute(value, axis, [(i, i ^ 1 << bit) for i in range(size)])  16.7 us
    ppermute x16, starting transfers between devices, bit_swap(): return lax.ppermute(value, axis, [(i, i ^ 1 << bit) for i in range(size)])  16.5 us
  transfers between devices with their start and end apart: 65, of which 21 were waited for; matrix products, arithmetic and copies ran while one was open for 8% of the time, Pallas kernels for 49%

profile of v1, /device:TPU:0, one launch (start us, length us, event | category | flops | bytes accessed | tf_op | source)
XLA Modules:
  0.0 360.2 jit_solution(2468632846512545233)
XLA Ops:
  9.0 4.1 %collective-permute-start = (bf16[32,2048]{1,0:T(8,128)(2,1)S(1)}, bf16[32,2048]{1,0:T(8,128)(2,1)S(1)}, u32[]{:S(2)}, u32[]{:S(2)}) collective-permute-start(bf16[32,2048]{1,0:T(8,128)(2,1)S(1)} %pad_maximum_fusion.7), channel_id=1, source_target_pairs={{0,16},{8,24},{16,0},{24,8},{1,17},{9,25},{17,1},{25,9},{2,18},{10... | collective-permute-start | bytes 393224 | tf_op jit(solution)/shard_map/ppermute | solution.py:727
  13.1 1.5 collective-permute-start.2
  17.1 1.8 fusion.14
  18.9 2.2 pack_columns.1
  21.9 1.6 collective-permute-start.1
  23.6 2.0 fusion.order_ref.refs_14_
  26.2 2.8 collective-permute-start.4
  29.5 2.2 collective-permute-start.6
  31.8 4.9 %collective-permute-done.4.refs_1_ = bf16[28,3840]{1,0:T(8,128)(2,1)S(1)} collective-permute-done((bf16[28,3840]{1,0:T(8,128)(2,1)S(1)}, bf16[28,3840]{1,0:T(8,128)(2,1)S(1)}, u32[]{:S(2)}, u32[]{:S(2)}) %collective-permute-start.4) | collective-permute-done | bytes 215072 | tf_op jit(solution)/shard_map/ppermute | solution.py:739
  36.7 5.2 %collective-permute-done.5.refs_2_ = bf16[28,3840]{1,0:T(8,128)(2,1)S(1)} collective-permute-done((bf16[28,3840]{1,0:T(8,128)(2,1)S(1)}, bf16[28,3840]{1,0:T(8,128)(2,1)S(1)}, u32[]{:S(2)}, u32[]{:S(2)}) %collective-permute-start.5) | collective-permute-done | bytes 215072 | tf_op jit(solution)/shard_map/ppermute | solution.py:739
  41.9 2.8 collective-permute-done.6.refs_3_
  45.7 2.9 assemble_rows.1
  49.8 2.9 collective-permute-start.8
  52.7 5.9 %collective-permute-done.7 = bf16[128,1152]{1,0:T(8,128)(2,1)S(1)} collective-permute-done((bf16[128,1152]{1,0:T(8,128)(2,1)S(1)}, bf16[128,1152]{1,0:T(8,128)(2,1)S(1)}, u32[]{:S(2)}, u32[]{:S(2)}) %collective-permute-start.7) | collective-permute-done | bytes 294944 | tf_op jit(solution)/shard_map/ppermute | solution.py:731
  58.6 6.7 %collective-permute-done.8 = bf16[128,1152]{1,0:T(8,128)(2,1)S(1)} collective-permute-done((bf16[128,1152]{1,0:T(8,128)(2,1)S(1)}, bf16[128,1152]{1,0:T(8,128)(2,1)S(1)}, u32[]{:S(2)}, u32[]{:S(2)}) %collective-permute-start.8) | collective-permute-done | bytes 294944 | tf_op jit(solution)/shard_map/ppermute | solution.py:731
  66.2 1.8 collective-permute-start.14
  70.0 8.0 %norm_project_rotate.1 = (bf16[512,512]{1,0:T(8,128)(2,1)}, bf16[512,512]{1,0:T(8,128)(2,1)}, bf16[512,896]{1,0:T(8,128)(2,1)}, bf16[512,256]{1,0:T(8,128)(2,1)}, f32[1,896]{1,0:T(1,128)}, /*index=5*/f32[1,896]{1,0:T(1,128)}) custom-call(bf16[512,896]{1,0:T(8,128)(2,1)} %bitcast.47, bf16[896,1024]{1,0:T(8,128)(2,1)} %fusion.order_ref.refs_14_, ...), custom_call_target="tpu_custom_call" | custom-call | flops 2147483648 | bytes 12582912 | tf_op jit(solution)/shard_map/norm_project_rotate/pallas_call | solution.py:119
  78.1 1.5 collective-permute-start.12
  79.6 7.1 %collective-permute-done.12.kv_2 = bf16[2,256,256]{2,1,0:T(8,128)(2,1)S(1)} collective-permute-done((bf16[2,256,256]{2,1,0:T(8,128)(2,1)}, bf16[2,256,256]{2,1,0:T(8,128)(2,1)S(1)}, u32[]{:S(2)}, u32[]{:S(2)}) %collective-permute-start.12) | collective-permute-done | bytes 262176 | tf_op jit(solution)/shard_map/ppermute | solution.py:727
  87.3 1.8 collective-permute-done.14.c_2
  89.1 1.5 collective-permute-start.15
  93.7 9.4 %attention_forward.2 = (bf16[256,896]{1,0:T(8,128)(2,1)}, f32[256,128]{1,0:T(8,128)}) custom-call(s32[1]{0:T(128)} %bitcast.block_ref, bf16[512,896]{1,0:T(8,128)(2,1)} %get-tuple-element.193.q_ref, bf16[2,256,256]{2,1,0:T(8,128)(2,1)} %bitcast.61, bf16[2,256,256]{2,1,0:T(8,128)(2,1)} %collective-permute-done.11.kv_1, bf16[2,256,256]{2,1,0:T(8,128)(2,1)} %copy-done.61, ...), custom_call_target="tpu_custom_call" | custom-call | flops 3758096384 | bytes 917504 | tf_op jit(solution)/shard_map/attention_forward/pallas_call | solution.py:377
  103.3 1.8 collective-permute-start.22
  106.7 5.3 %project_out_norm.2 = (f32[256,896]{1,0:T(8,128)}, bf16[256,896]{1,0:T(8,128)(2,1)}) custom-call(bf16[256,896]{1,0:T(8,128)(2,1)} %get-tuple-element.202.attended_ref.out_ref, bf16[512,896]{1,0:T(8,128)(2,1)} %bitcast.48, bf16[512,896]{1,0:T(8,128)(2,1)} %copy-done, bf16[512,896]{1,0:T(8,128)(2,1)} %copy-done.1, bf16[896,1024]{1,0:T(8,128)(2,1)} %fusion.order_ref.refs_14_, ...), custom_call_target="tpu_custom_call" | custom-call | flops 1233125376 | bytes 8388608 | tf_op jit(solution)/shard_map/project_out_norm/pallas_call | solution.py:174
  111.9 1.5 collective-permute-start.19
  115.4 9.8 %attention_forward.3 = (bf16[256,896]{1,0:T(8,128)(2,1)}, f32[256,128]{1,0:T(8,128)}) custom-call(s32[1]{0:T(128)} %bitcast.block_ref, bf16[512,896]{1,0:T(8,128)(2,1)} %get-tuple-element.193.q_ref, bf16[2,256,256]{2,1,0:T(8,128)(2,1)} %bitcast.62, bf16[2,256,256]{2,1,0:T(8,128)(2,1)} %collective-permute-done.11.kv_1, bf16[2,256,256]{2,1,0:T(8,128)(2,1)} %copy-done.61, ...), custom_call_target="tpu_custom_call" | custom-call | flops 3758096384 | bytes 917504 | tf_op jit(solution)/shard_map/attention_forward/pallas_call | solution.py:377
  125.3 5.6 %project_out_norm.3 = (f32[256,896]{1,0:T(8,128)}, bf16[256,896]{1,0:T(8,128)(2,1)}) custom-call(bf16[256,896]{1,0:T(8,128)(2,1)} %get-tuple-element.221.attended_ref.out_ref, bf16[512,896]{1,0:T(8,128)(2,1)} %bitcast.49, bf16[512,896]{1,0:T(8,128)(2,1)} %copy-done, bf16[512,896]{1,0:T(8,128)(2,1)} %copy-done.1, bf16[896,1024]{1,0:T(8,128)(2,1)} %fusion.order_ref.refs_14_, ...), custom_call_target="tpu_custom_call" | custom-call | flops 1233125376 | bytes 8388608 | tf_op jit(solution)/shard_map/project_out_norm/pallas_call | solution.py:174
  130.9 1.5 collective-permute-start.24
  134.4 3.5 collective-permute-done.21.n_3
  138.0 26.0 %feed_forward.2 = (f32[256,896]{1,0:T(8,128)}, bf16[256,896]{1,0:T(8,128)(2,1)}, bf16[256,896]{1,0:T(8,128)(2,1)}, bf16[256,896]{1,0:T(8,128)(2,1)}, f32[256,896...) custom-call(bf16[256,896]{1,0:T(8,128)(2,1)} %get-tuple-element.206., ...), custom_call_target="tpu_custom_call" | custom-call | flops 14092861440 | bytes 14745600 | tf_op jit(solution)/shard_map/feed_forward/pallas_call | solution.py:563
  164.1 1.5 collective-permute-start.27
  167.6 26.3 %feed_forward.3 = (f32[256,896]{1,0:T(8,128)}, bf16[256,896]{1,0:T(8,128)(2,1)}, bf16[256,896]{1,0:T(8,128)(2,1)}, bf16[256,896]{1,0:T(8,128)(2,1)}, f32[256,896...) custom-call(bf16[256,896]{1,0:T(8,128)(2,1)} %get-tuple-element.223., ...), custom_call_target="tpu_custom_call" | custom-call | flops 14092861440 | bytes 14745600 | tf_op jit(solution)/shard_map/feed_forward/pallas_call | solution.py:563
  193.9 1.5 collective-permute-start.30
  198.4 5.8 %norm_back_project.2 = (f32[256,896]{1,0:T(8,128)}, bf16[256,512]{1,0:T(8,128)(2,1)}, bf16[256,512]{1,0:T(8,128)(2,1)}, bf16[256,896]{1,0:T(8,128)(2,1)}, f32[1,896]{1,0:T(1,128)}) custom-call(f32[256,896]{1,0:T(8,128)} %get-tuple-element.233.own_ref, bf16[256,896]{1,0:T(8,128)(2,1)} %copy-done.31, bf16[256,896]{1,0:T(8,128)(2,1)} %copy-done.32, ...), custom_call_target="tpu_custom_call" | custom-call | flops 822083584 | bytes 12582912 | tf_op jit(solution)/shard_map/norm_back_project/pallas_call | solution.py:233
  204.2 20.1 %feed_forward_gradients.1 = bf16[896,3840]{1,0:T(8,128)(2,1)} custom-call(bf16[2,896,1024]{2,1,0:T(8,128)(2,1)} %get-tuple-element.216.turned_0, bf16[2,896,1024]{2,1,0:T(8,128)(2,1)} %get-tuple-element.239.turned_1, bf16[3,1024,1280]{2,1,0:T(8,128)(2,1)} %get-tuple-element.240.kept_0, bf16[3,1024,1280]{2,1,0:T(8,128)(2,1)} %get-tuple-element.228.kept_1), custom_call_target="tpu_custom_call" | custom-call | flops 14092861440 | bytes 22609920 | tf_op jit(solution)/shard_map/feed_forward_gradients/pallas_call | solution.py:607
  226.0 1.5 collective-permute-start.33
  229.6 1.5 collective-permute-start.40
  232.5 18.4 %attention_backward.2 = (bf16[256,896]{1,0:T(8,128)(2,1)}, f32[256,256]{1,0:T(8,128)}, bf16[256,256]{1,0:T(8,128)(2,1)}, bf16[256,256]{1,0:T(8,128)(2,1)}, bf16[256,256]{1,0:T(8,128)(2,1)}) custom-call(s32[1]{0:T(128)} %bitcast.block_ref, bf16[512,896]{1,0:T(8,128)(2,1)} %get-tuple-element.193.q_ref, bf16[2,256,256]{2,1,0:T(8,128)(2,1)} %bitcast.63, ...), custom_call_target="tpu_custom_call" | custom-call | flops 9395240960 | bytes 1835008 | tf_op jit(solution)/shard_map/attention_backward/pallas_call | solution.py:484
  251.0 1.5 collective-permute-start.37
  252.8 5.9 %norm_back_project.3 = (f32[256,896]{1,0:T(8,128)}, bf16[256,512]{1,0:T(8,128)(2,1)}, bf16[256,512]{1,0:T(8,128)(2,1)}, bf16[256,896]{1,0:T(8,128)(2,1)}, f32[1,896]{1,0:T(1,128)}) custom-call(f32[256,896]{1,0:T(8,128)} %get-tuple-element.259.own_ref, bf16[256,896]{1,0:T(8,128)(2,1)} %copy-done.28, bf16[256,896]{1,0:T(8,128)(2,1)} %copy-done.29, ...), custom_call_target="tpu_custom_call" | custom-call | flops 822083584 | bytes 12582912 | tf_op jit(solution)/shard_map/norm_back_project/pallas_call | solution.py:233
  258.8 1.7 convolution_convert_fusion.2
  260.5 1.2 collective-permute-start.42
  262.4 18.2 %attention_backward.3 = (bf16[256,896]{1,0:T(8,128)(2,1)}, f32[256,256]{1,0:T(8,128)}, bf16[256,256]{1,0:T(8,128)(2,1)}, bf16[256,256]{1,0:T(8,128)(2,1)}, bf16[256,256]{1,0:T(8,128)(2,1)}) custom-call(s32[1]{0:T(128)} %bitcast.block_ref, bf16[512,896]{1,0:T(8,128)(2,1)} %get-tuple-element.193.q_ref, bf16[2,256,256]{2,1,0:T(8,128)(2,1)} %bitcast.64, ...), custom_call_target="tpu_custom_call" | custom-call | flops 9395240960 | bytes 1835008 | tf_op jit(solution)/shard_map/attention_backward/pallas_call | solution.py:484
  280.7 2.0 add_convert_fusion.1
  282.9 1.7 convolution_convert_fusion
  286.7 1.4 pad_maximum_fusion.refs_11_
  289.5 1.4 add_convert_fusion
  293.7 1.7 collective-permute-start.47
  297.2 9.2 %input_gradient.1 = (bf16[512,256]{1,0:T(8,128)(2,1)}, bf16[512,896]{1,0:T(8,128)(2,1)}, f32[1,896]{1,0:T(1,128)}, f32[1,1152]{1,0:T(1,128)}) custom-call(bf16[256,896]{1,0:T(8,128)(2,1)} %get-tuple-element.258.refs_0_, bf16[256,896]{1,0:T(8,128)(2,1)} %get-tuple-element.284.refs_1_, f32[256,256]{1,0:T(8,128)} %get-tuple-element.285.refs_2_, ...), custom_call_target="tpu_custom_call" | custom-call | flops 3170893824 | bytes 16777216 | tf_op jit(solution)/shard_map/input_gradient/pallas_call | solution.py:269
  307.0 1.6 collective-permute-done.49
  313.7 1.5 collective-permute-start.55
  315.2 1.3 collective-permute-start.56
  317.1 3.0 cut_rows.1
  320.9 1.5 collective-permute-start.52
  322.4 1.3 collective-permute-start.53
  323.7 2.7 collective-permute-done.55
  328.1 1.6 collective-permute-start.59
  329.7 2.0 collective-permute-start.60
  333.0 1.8 collective-permute-start.57
  335.1 1.3 fusion.13
  336.4 5.0 %collective-permute-done.57 = bf16[64,2048]{1,0:T(8,128)(2,1)S(1)} collective-permute-done((bf16[64,2048]{1,0:T(8,128)(2,1)S(1)}, bf16[64,2048]{1,0:T(8,128)(2,1)S(1)}, u32[]{:S(2)}, u32[]{:S(2)}) %collective-permute-start.57) | collective-permute-done | bytes 262176 | tf_op jit(solution)/shard_map/ppermute | solution.py:727
  343.0 1.8 collective-permute-done.62.refs_3_
  345.6 2.7 unpack_columns.1
  348.3 1.7 collective-permute-done.58
  (304 shorter events, 55.9 us)
Async XLA Ops:
  7.2 130.8 %all-gather.2.cloned.1.call-start = ((), (), s32[]{:S(2)}) async-start(), calls=%async_computation.1 | async-start | bytes 7741440 | tf_op jit(solution)/shard_map/all_gather | solution.py:874
  9.0 12.8 %collective-permute-start = (bf16[32,2048]{1,0:T(8,128)(2,1)S(1)}, bf16[32,2048]{1,0:T(8,128)(2,1)S(1)}, u32[]{:S(2)}, u32[]{:S(2)}) collective-permute-start(bf16[32,2048]{1,0:T(8,128)(2,1)S(1)} %pad_maximum_fusion.7), channel_id=1, source_target_pairs={{0,16},{8,24},{16,0},{24,8},{1,17},{9,25},{17,1},{25,9},{2,18},{10... | collective-permute-start | bytes 393224 | tf_op jit(solution)/shard_map/ppermute | solution.py:727
  13.1 31.6 %collective-permute-start.2 = (bf16[512,896]{1,0:T(8,128)(2,1)}, bf16[512,896]{1,0:T(8,128)(2,1)S(1)}, u32[]{:S(2)}, u32[]{:S(2)}) collective-permute-start(bf16[512,896]{1,0:T(8,128)(2,1)} %bitcast.41), channel_id=1, source_target_pairs={{0,2},{2,0},{1,3},{3,1},{4,6},{6,4},{5,7},{7,5},{8,10},{10,8},{9,1... | collective-permute-start | bytes 2752520 | tf_op jit(solution)/shard_map/ppermute | solution.py:727
  21.9 7.6 %collective-permute-start.1 = (bf16[64,2048]{1,0:T(8,128)(2,1)S(1)}, bf16[64,2048]{1,0:T(8,128)(2,1)S(1)}, u32[]{:S(2)}, u32[]{:S(2)}) collective-permute-start(bf16[64,2048]{1,0:T(8,128)(2,1)S(1)} %pad_maximum_fusion.6), channel_id=1, source_target_pairs={{0,8},{8,0},{16,24},{24,16},{1,9},{9,1},{17,25},{25,17},{2,10},{10... | collective-permute-start | bytes 786440 | tf_op jit(solution)/shard_map/ppermute | solution.py:727
  25.5 6.2 %collective-permute-start.3 = (bf16[28,3840]{1,0:T(8,128)(2,1)S(1)}, bf16[28,3840]{1,0:T(8,128)(2,1)S(1)}, u32[]{:S(2)}, u32[]{:S(2)}) collective-permute-start(bf16[28,3840]{1,0:T(8,128)(2,1)S(1)} %copy-done.69), channel_id=1, source_target_pairs={{0,0},{1,4},{2,2},{3,6},{4,1},{5,5},{6,3},{7,7},{8,8},{9,12},{10,1... | collective-permute-start | bytes 645128 | tf_op jit(solution)/shard_map/ppermute | solution.py:739
  26.2 10.4 %collective-permute-start.4 = (bf16[28,3840]{1,0:T(8,128)(2,1)S(1)}, bf16[28,3840]{1,0:T(8,128)(2,1)S(1)}, u32[]{:S(2)}, u32[]{:S(2)}) collective-permute-start(bf16[28,3840]{1,0:T(8,128)(2,1)S(1)} %copy-done.68), channel_id=1, source_target_pairs={{0,4},{1,0},{2,6},{3,2},{4,5},{5,1},{6,7},{7,3},{8,12},{9,8},{10,1... | collective-permute-start | bytes 645128 | tf_op jit(solution)/shard_map/ppermute | solution.py:739
  29.0 12.8 %collective-permute-start.5 = (bf16[28,3840]{1,0:T(8,128)(2,1)S(1)}, bf16[28,3840]{1,0:T(8,128)(2,1)S(1)}, u32[]{:S(2)}, u32[]{:S(2)}) collective-permute-start(bf16[28,3840]{1,0:T(8,128)(2,1)S(1)} %copy-done.67), channel_id=1, source_target_pairs={{0,2},{1,6},{2,0},{3,4},{4,3},{5,7},{6,1},{7,5},{8,10},{9,14},{10,... | collective-permute-start | bytes 645128 | tf_op jit(solution)/shard_map/ppermute | solution.py:739
  29.5 15.1 %collective-permute-start.6 = (bf16[28,3840]{1,0:T(8,128)(2,1)S(1)}, bf16[28,3840]{1,0:T(8,128)(2,1)S(1)}, u32[]{:S(2)}, u32[]{:S(2)}) collective-permute-start(bf16[28,3840]{1,0:T(8,128)(2,1)S(1)} %copy-done.66), channel_id=1, source_target_pairs={{0,6},{1,2},{2,4},{3,0},{4,7},{5,3},{6,5},{7,1},{8,14},{9,10},{10,... | collective-permute-start | bytes 645128 | tf_op jit(solution)/shard_map/ppermute | solution.py:739
  48.6 268.5 %reduce-scatter.2.cloned.1.call-start = ((), (), s32[]{:S(2)}) async-start(), calls=%async_computation.2 | async-start | bytes 7741440 | tf_op jit(solution)/shard_map/reduce_scatter | solution.py:922
  48.7 9.9 %collective-permute-start.7 = (bf16[128,1152]{1,0:T(8,128)(2,1)S(1)}, bf16[128,1152]{1,0:T(8,128)(2,1)S(1)}, u32[]{:S(2)}, u32[]{:S(2)}) collective-permute-start(bf16[128,1152]{1,0:T(8,128)(2,1)S(1)} %slice.80), channel_id=1, source_target_pairs={{0,2},{2,0},{4,6},{6,4},{1,3},{3,1},{5,7},{7,5},{8,10},{10,8},{12,... | collective-permute-start | bytes 884744 | tf_op jit(solution)/shard_map/ppermute | solution.py:731
  49.8 15.5 %collective-permute-start.8 = (bf16[128,1152]{1,0:T(8,128)(2,1)S(1)}, bf16[128,1152]{1,0:T(8,128)(2,1)S(1)}, u32[]{:S(2)}, u32[]{:S(2)}) collective-permute-start(bf16[128,1152]{1,0:T(8,128)(2,1)S(1)} %slice.80), channel_id=1, source_target_pairs={{0,4},{2,6},{4,0},{6,2},{1,5},{3,7},{5,1},{7,3},{8,12},{10,14},{12... | collective-permute-start | bytes 884744 | tf_op jit(solution)/shard_map/ppermute | solution.py:731
  52.7 13.3 %collective-permute-start.9 = (bf16[128,1152]{1,0:T(8,128)(2,1)S(1)}, bf16[128,1152]{1,0:T(8,128)(2,1)S(1)}, u32[]{:S(2)}, u32[]{:S(2)}) collective-permute-start(bf16[128,1152]{1,0:T(8,128)(2,1)S(1)} %slice.80), channel_id=1, source_target_pairs={{0,6},{2,4},{4,2},{6,0},{1,7},{3,5},{5,3},{7,1},{8,14},{10,12},{12... | collective-permute-start | bytes 884744 | tf_op jit(solution)/shard_map/ppermute | solution.py:731
  66.1 2.9 collective-permute-start.10
  66.2 22.9 %collective-permute-start.14 = (bf16[512,896]{1,0:T(8,128)(2,1)S(1)}, bf16[512,896]{1,0:T(8,128)(2,1)}, u32[]{:S(2)}, u32[]{:S(2)}) collective-permute-start(bf16[512,896]{1,0:T(8,128)(2,1)S(1)} %bitcast.46), channel_id=1, source_target_pairs={{0,4},{4,0},{1,5},{5,1},{2,6},{6,2},{3,7},{7,3},{8,12},{12,8},{9,1... | collective-permute-start | bytes 2752520 | tf_op jit(solution)/shard_map/ppermute | solution.py:727
  78.1 8.6 %collective-permute-start.12 = (bf16[2,256,256]{2,1,0:T(8,128)(2,1)}, bf16[2,256,256]{2,1,0:T(8,128)(2,1)S(1)}, u32[]{:S(2)}, u32[]{:S(2)}) collective-permute-start(bf16[2,256,256]{2,1,0:T(8,128)(2,1)} %bitcast.59), channel_id=1, source_target_pairs={{0,2},{2,0},{1,3},{3,1},{4,6},{6,4},{5,7},{7,5},{8,10},{10,8},{9,1... | collective-permute-start | bytes 786440 | tf_op jit(solution)/shard_map/ppermute | solution.py:727
  86.7 6.9 %collective-permute-start.11 = (bf16[2,256,256]{2,1,0:T(8,128)(2,1)}, bf16[2,256,256]{2,1,0:T(8,128)(2,1)}, u32[]{:S(2)}, u32[]{:S(2)}) collective-permute-start(bf16[2,256,256]{2,1,0:T(8,128)(2,1)} %bitcast.60), channel_id=1, source_target_pairs={{0,1},{1,0},{2,3},{3,2},{4,5},{5,4},{6,7},{7,6},{8,9},{9,8},{10,11... | collective-permute-start | bytes 786440 | tf_op jit(solution)/shard_map/ppermute | solution.py:727
  89.1 14.0 %collective-permute-start.15 = (bf16[128,896]{1,0:T(8,128)(2,1)S(1)}, bf16[128,896]{1,0:T(8,128)(2,1)S(1)}, u32[]{:S(2)}, u32[]{:S(2)}) collective-permute-start(bf16[128,896]{1,0:T(8,128)(2,1)S(1)} %slice.81), channel_id=1, source_target_pairs={{0,2},{2,0},{4,6},{6,4},{1,3},{3,1},{5,7},{7,5},{8,10},{10,8},{12,... | collective-permute-start | bytes 688136 | tf_op jit(solution)/shard_map/ppermute | solution.py:731
  90.5 12.6 %collective-permute-start.16 = (bf16[128,896]{1,0:T(8,128)(2,1)S(1)}, bf16[128,896]{1,0:T(8,128)(2,1)S(1)}, u32[]{:S(2)}, u32[]{:S(2)}) collective-permute-start(bf16[128,896]{1,0:T(8,128)(2,1)S(1)} %slice.81), channel_id=1, source_target_pairs={{0,4},{2,6},{4,0},{6,2},{1,5},{3,7},{5,1},{7,3},{8,12},{10,14},{12... | collective-permute-start | bytes 688136 | tf_op jit(solution)/shard_map/ppermute | solution.py:731
  91.4 11.7 %collective-permute-start.17 = (bf16[128,896]{1,0:T(8,128)(2,1)S(1)}, bf16[128,896]{1,0:T(8,128)(2,1)S(1)}, u32[]{:S(2)}, u32[]{:S(2)}) collective-permute-start(bf16[128,896]{1,0:T(8,128)(2,1)S(1)} %slice.81), channel_id=1, source_target_pairs={{0,6},{2,4},{4,2},{6,0},{1,7},{3,5},{5,3},{7,1},{8,14},{10,12},{12... | collective-permute-start | bytes 688136 | tf_op jit(solution)/shard_map/ppermute | solution.py:731
  103.2 2.5 collective-permute-start.18
  103.3 22.0 %collective-permute-start.22 = (bf16[256,896]{1,0:T(8,128)(2,1)S(1)}, bf16[256,896]{1,0:T(8,128)(2,1)S(1)}, u32[]{:S(2)}, u32[]{:S(2)}) collective-permute-start(bf16[256,896]{1,0:T(8,128)(2,1)S(1)} %slice.82), channel_id=1, source_target_pairs={{0,4},{4,0},{1,5},{5,1},{2,6},{6,2},{3,7},{7,3},{8,12},{12,8},{9,1... | collective-permute-start | bytes 1376264 | tf_op jit(solution)/shard_map/ppermute | solution.py:727
  105.1 20.2 %collective-permute-start.23 = (bf16[256,896]{1,0:T(8,128)(2,1)S(1)}, bf16[256,896]{1,0:T(8,128)(2,1)S(1)}, u32[]{:S(2)}, u32[]{:S(2)}) collective-permute-start(bf16[256,896]{1,0:T(8,128)(2,1)S(1)} %slice.83), channel_id=1, source_target_pairs={{0,2},{2,0},{1,3},{3,1},{4,6},{6,4},{5,7},{7,5},{8,10},{10,8},{9,1... | collective-permute-start | bytes 1376264 | tf_op jit(solution)/shard_map/ppermute | solution.py:727
  111.9 21.6 %collective-permute-start.19 = (bf16[256,896]{1,0:T(8,128)(2,1)}, bf16[256,896]{1,0:T(8,128)(2,1)S(1)}, u32[]{:S(2)}, u32[]{:S(2)}) collective-permute-start(bf16[256,896]{1,0:T(8,128)(2,1)} %get-tuple-element.206.n_0), channel_id=1, source_target_pairs={{0,2},{2,0},{4,6},{6,4},{1,3},{3,1},{5,7},{7,5},{8,10},{10,8},{12,... | collective-permute-start | bytes 1376264 | tf_op jit(solution)/shard_map/ppermute | solution.py:731
  113.4 21.0 %collective-permute-start.20 = (bf16[256,896]{1,0:T(8,128)(2,1)}, bf16[256,896]{1,0:T(8,128)(2,1)}, u32[]{:S(2)}, u32[]{:S(2)}) collective-permute-start(bf16[256,896]{1,0:T(8,128)(2,1)} %get-tuple-element.206.n_0), channel_id=1, source_target_pairs={{0,4},{2,6},{4,0},{6,2},{1,5},{3,7},{5,1},{7,3},{8,12},{10,14},{12... | collective-permute-start | bytes 1376264 | tf_op jit(solution)/shard_map/ppermute | solution.py:731
  114.5 23.5 %collective-permute-start.21 = (bf16[256,896]{1,0:T(8,128)(2,1)}, bf16[256,896]{1,0:T(8,128)(2,1)}, u32[]{:S(2)}, u32[]{:S(2)}) collective-permute-start(bf16[256,896]{1,0:T(8,128)(2,1)} %get-tuple-element.206.n_0), channel_id=1, source_target_pairs={{0,6},{2,4},{4,2},{6,0},{1,7},{3,5},{5,3},{7,1},{8,14},{10,12},{12... | collective-permute-start | bytes 1376264 | tf_op jit(solution)/shard_map/ppermute | solution.py:731
  130.9 33.1 %collective-permute-start.24 = (bf16[256,896]{1,0:T(8,128)(2,1)}, bf16[256,896]{1,0:T(8,128)(2,1)S(1)}, u32[]{:S(2)}, u32[]{:S(2)}) collective-permute-start(bf16[256,896]{1,0:T(8,128)(2,1)} %get-tuple-element.223.n_0), channel_id=1, source_target_pairs={{0,2},{2,0},{4,6},{6,4},{1,3},{3,1},{5,7},{7,5},{8,10},{10,8},{12,... | collective-permute-start | bytes 1376264 | tf_op jit(solution)/shard_map/ppermute | solution.py:731
  132.4 31.6 %collective-permute-start.25 = (bf16[256,896]{1,0:T(8,128)(2,1)}, bf16[256,896]{1,0:T(8,128)(2,1)S(1)}, u32[]{:S(2)}, u32[]{:S(2)}) collective-permute-start(bf16[256,896]{1,0:T(8,128)(2,1)} %get-tuple-element.223.n_0), channel_id=1, source_target_pairs={{0,4},{2,6},{4,0},{6,2},{1,5},{3,7},{5,1},{7,3},{8,12},{10,14},{12... | collective-permute-start | bytes 1376264 | tf_op jit(solution)/shard_map/ppermute | solution.py:731
  133.5 30.5 %collective-permute-start.26 = (bf16[256,896]{1,0:T(8,128)(2,1)}, bf16[256,896]{1,0:T(8,128)(2,1)S(1)}, u32[]{:S(2)}, u32[]{:S(2)}) collective-permute-start(bf16[256,896]{1,0:T(8,128)(2,1)} %get-tuple-element.223.n_0), channel_id=1, source_target_pairs={{0,6},{2,4},{4,2},{6,0},{1,7},{3,5},{5,3},{7,1},{8,14},{10,12},{12... | collective-permute-start | bytes 1376264 | tf_op jit(solution)/shard_map/ppermute | solution.py:731
  164.1 32.1 %collective-permute-start.27 = (bf16[256,896]{1,0:T(8,128)(2,1)}, bf16[256,896]{1,0:T(8,128)(2,1)S(1)}, u32[]{:S(2)}, u32[]{:S(2)}) collective-permute-start(bf16[256,896]{1,0:T(8,128)(2,1)} %get-tuple-element.230), channel_id=1, source_target_pairs={{0,2},{2,0},{4,6},{6,4},{1,3},{3,1},{5,7},{7,5},{8,10},{10,8},{12,... | collective-permute-start | bytes 1376264 | tf_op jit(solution)/shard_map/ppermute | solution.py:731
  165.6 31.8 %collective-permute-start.28 = (bf16[256,896]{1,0:T(8,128)(2,1)}, bf16[256,896]{1,0:T(8,128)(2,1)S(1)}, u32[]{:S(2)}, u32[]{:S(2)}) collective-permute-start(bf16[256,896]{1,0:T(8,128)(2,1)} %get-tuple-element.231), channel_id=1, source_target_pairs={{0,4},{2,6},{4,0},{6,2},{1,5},{3,7},{5,1},{7,3},{8,12},{10,14},{12... | collective-permute-start | bytes 1376264 | tf_op jit(solution)/shard_map/ppermute | solution.py:731
  166.4 31.0 %collective-permute-start.29 = (bf16[256,896]{1,0:T(8,128)(2,1)}, bf16[256,896]{1,0:T(8,128)(2,1)S(1)}, u32[]{:S(2)}, u32[]{:S(2)}) collective-permute-start(bf16[256,896]{1,0:T(8,128)(2,1)} %get-tuple-element.232), channel_id=1, source_target_pairs={{0,6},{2,4},{4,2},{6,0},{1,7},{3,5},{5,3},{7,1},{8,14},{10,12},{12... | collective-permute-start | bytes 1376264 | tf_op jit(solution)/shard_map/ppermute | solution.py:731
  193.9 30.4 %collective-permute-start.30 = (bf16[256,896]{1,0:T(8,128)(2,1)}, bf16[256,896]{1,0:T(8,128)(2,1)S(1)}, u32[]{:S(2)}, u32[]{:S(2)}) collective-permute-start(bf16[256,896]{1,0:T(8,128)(2,1)} %get-tuple-element.243), channel_id=1, source_target_pairs={{0,2},{2,0},{4,6},{6,4},{1,3},{3,1},{5,7},{7,5},{8,10},{10,8},{12,... | collective-permute-start | bytes 1376264 | tf_op jit(solution)/shard_map/ppermute | solution.py:731
  195.4 28.9 %collective-permute-start.31 = (bf16[256,896]{1,0:T(8,128)(2,1)}, bf16[256,896]{1,0:T(8,128)(2,1)S(1)}, u32[]{:S(2)}, u32[]{:S(2)}) collective-permute-start(bf16[256,896]{1,0:T(8,128)(2,1)} %get-tuple-element.244), channel_id=1, source_target_pairs={{0,4},{2,6},{4,0},{6,2},{1,5},{3,7},{5,1},{7,3},{8,12},{10,14},{12... | collective-permute-start | bytes 1376264 | tf_op jit(solution)/shard_map/ppermute | solution.py:731
  196.2 28.1 %collective-permute-start.32 = (bf16[256,896]{1,0:T(8,128)(2,1)}, bf16[256,896]{1,0:T(8,128)(2,1)S(1)}, u32[]{:S(2)}, u32[]{:S(2)}) collective-permute-start(bf16[256,896]{1,0:T(8,128)(2,1)} %get-tuple-element.245), channel_id=1, source_target_pairs={{0,6},{2,4},{4,2},{6,0},{1,7},{3,5},{5,3},{7,1},{8,14},{10,12},{12... | collective-permute-start | bytes 1376264 | tf_op jit(solution)/shard_map/ppermute | solution.py:731
  226.0 24.9 %collective-permute-start.33 = (bf16[256,896]{1,0:T(8,128)(2,1)}, bf16[256,896]{1,0:T(8,128)(2,1)S(1)}, u32[]{:S(2)}, u32[]{:S(2)}) collective-permute-start(bf16[256,896]{1,0:T(8,128)(2,1)} %get-tuple-element.255), channel_id=1, source_target_pairs={{0,2},{2,0},{4,6},{6,4},{1,3},{3,1},{5,7},{7,5},{8,10},{10,8},{12,... | collective-permute-start | bytes 1376264 | tf_op jit(solution)/shard_map/ppermute | solution.py:731
  227.5 23.5 %collective-permute-start.34 = (bf16[256,896]{1,0:T(8,128)(2,1)}, bf16[256,896]{1,0:T(8,128)(2,1)S(1)}, u32[]{:S(2)}, u32[]{:S(2)}) collective-permute-start(bf16[256,896]{1,0:T(8,128)(2,1)} %get-tuple-element.256), channel_id=1, source_target_pairs={{0,4},{2,6},{4,0},{6,2},{1,5},{3,7},{5,1},{7,3},{8,12},{10,14},{12... | collective-permute-start | bytes 1376264 | tf_op jit(solution)/shard_map/ppermute | solution.py:731
  228.4 24.2 %collective-permute-start.35 = (bf16[256,896]{1,0:T(8,128)(2,1)S(1)}, bf16[256,896]{1,0:T(8,128)(2,1)S(1)}, u32[]{:S(2)}, u32[]{:S(2)}) collective-permute-start(bf16[256,896]{1,0:T(8,128)(2,1)S(1)} %copy-done.54), channel_id=1, source_target_pairs={{0,6},{2,4},{4,2},{6,0},{1,7},{3,5},{5,3},{7,1},{8,14},{10,12},{12... | collective-permute-start | bytes 1376264 | tf_op jit(solution)/shard_map/ppermute | solution.py:731
  229.6 53.1 %collective-permute-start.40 = (bf16[256,896]{1,0:T(8,128)(2,1)}, bf16[256,896]{1,0:T(8,128)(2,1)S(1)}, u32[]{:S(2)}, u32[]{:S(2)}) collective-permute-start(bf16[256,896]{1,0:T(8,128)(2,1)} %get-tuple-element.281), channel_id=1, source_target_pairs={{0,2},{2,0},{4,6},{6,4},{1,3},{3,1},{5,7},{7,5},{8,10},{10,8},{12,... | collective-permute-start | bytes 1376264 | tf_op jit(solution)/shard_map/ppermute | solution.py:731
  231.0 51.7 %collective-permute-start.41 = (bf16[256,896]{1,0:T(8,128)(2,1)}, bf16[256,896]{1,0:T(8,128)(2,1)}, u32[]{:S(2)}, u32[]{:S(2)}) collective-permute-start(bf16[256,896]{1,0:T(8,128)(2,1)} %get-tuple-element.282), channel_id=1, source_target_pairs={{0,4},{2,6},{4,0},{6,2},{1,5},{3,7},{5,1},{7,3},{8,12},{10,14},{12... | collective-permute-start | bytes 1376264 | tf_op jit(solution)/shard_map/ppermute | solution.py:731
  250.9 9.6 %collective-permute-start.36 = (bf16[256,256]{1,0:T(8,128)(2,1)}, bf16[256,256]{1,0:T(8,128)(2,1)}, u32[]{:S(2)}, u32[]{:S(2)}) collective-permute-start(bf16[256,256]{1,0:T(8,128)(2,1)} %get-tuple-element.266), channel_id=1, source_target_pairs={{0,1},{1,0},{2,3},{3,2},{4,5},{5,4},{6,7},{7,6},{8,9},{9,8},{10,11... | collective-permute-start | bytes 393224 | tf_op jit(solution)/shard_map/ppermute | solution.py:731
  251.0 10.7 %collective-permute-start.37 = (bf16[256,256]{1,0:T(8,128)(2,1)}, bf16[256,256]{1,0:T(8,128)(2,1)}, u32[]{:S(2)}, u32[]{:S(2)}) collective-permute-start(bf16[256,256]{1,0:T(8,128)(2,1)} %get-tuple-element.267), channel_id=1, source_target_pairs={{0,2},{1,3},{2,0},{3,1},{4,6},{5,7},{6,4},{7,5},{8,10},{9,11},{10,... | collective-permute-start | bytes 393224 | tf_op jit(solution)/shard_map/ppermute | solution.py:731
  252.5 9.9 %collective-permute-start.38 = (bf16[256,256]{1,0:T(8,128)(2,1)}, bf16[256,256]{1,0:T(8,128)(2,1)}, u32[]{:S(2)}, u32[]{:S(2)}) collective-permute-start(bf16[256,256]{1,0:T(8,128)(2,1)} %get-tuple-element.268), channel_id=1, source_target_pairs={{0,3},{1,2},{2,1},{3,0},{4,7},{5,6},{6,5},{7,4},{8,11},{9,10},{10,... | collective-permute-start | bytes 393224 | tf_op jit(solution)/shard_map/ppermute | solution.py:731
  260.5 22.2 %collective-permute-start.42 = (bf16[256,896]{1,0:T(8,128)(2,1)}, bf16[256,896]{1,0:T(8,128)(2,1)S(1)}, u32[]{:S(2)}, u32[]{:S(2)}) collective-permute-start(bf16[256,896]{1,0:T(8,128)(2,1)} %get-tuple-element.283), channel_id=1, source_target_pairs={{0,6},{2,4},{4,2},{6,0},{1,7},{3,5},{5,3},{7,1},{8,14},{10,12},{12... | collective-permute-start | bytes 1376264 | tf_op jit(solution)/shard_map/ppermute | solution.py:731
  261.8 18.9 %collective-permute-start.39 = (bf16[512,896]{1,0:T(8,128)(2,1)S(1)}, bf16[512,896]{1,0:T(8,128)(2,1)}, u32[]{:S(2)}, u32[]{:S(2)}) collective-permute-start(bf16[512,896]{1,0:T(8,128)(2,1)S(1)} %convolution_convert_fusion.2), channel_id=1, source_target_pairs={{0,1},{1,0},{2,3},{3,2},{4,5},{5,4},{6,7},{7,6},{8,9},{9,8},{10,11... | collective-permute-start | bytes 2752520 | tf_op jit(solution)/shard_map/ppermute | solution.py:727
  284.5 4.9 %collective-permute-start.43 = (bf16[512,896]{1,0:T(8,128)(2,1)}, bf16[512,896]{1,0:T(8,128)(2,1)}, u32[]{:S(2)}, u32[]{:S(2)}) collective-permute-start(bf16[512,896]{1,0:T(8,128)(2,1)} %convolution_convert_fusion), channel_id=1, source_target_pairs={{0,1},{1,0},{2,3},{3,2},{4,5},{5,4},{6,7},{7,6},{8,9},{9,8},{10,11... | collective-permute-start | bytes 2752520 | tf_op jit(solution)/shard_map/ppermute | solution.py:727
  284.7 6.2 %collective-permute-start.44 = (bf16[256,256]{1,0:T(8,128)(2,1)}, bf16[256,256]{1,0:T(8,128)(2,1)S(1)}, u32[]{:S(2)}, u32[]{:S(2)}) collective-permute-start(bf16[256,256]{1,0:T(8,128)(2,1)} %get-tuple-element.292), channel_id=1, source_target_pairs={{0,1},{1,0},{2,3},{3,2},{4,5},{5,4},{6,7},{7,6},{8,9},{9,8},{10,11... | collective-permute-start | bytes 393224 | tf_op jit(solution)/shard_map/ppermute | solution.py:731
  285.2 6.6 %collective-permute-start.45 = (bf16[256,256]{1,0:T(8,128)(2,1)}, bf16[256,256]{1,0:T(8,128)(2,1)S(1)}, u32[]{:S(2)}, u32[]{:S(2)}) collective-permute-start(bf16[256,256]{1,0:T(8,128)(2,1)} %get-tuple-element.293), channel_id=1, source_target_pairs={{0,2},{1,3},{2,0},{3,1},{4,6},{5,7},{6,4},{7,5},{8,10},{9,11},{10,... | collective-permute-start | bytes 393224 | tf_op jit(solution)/shard_map/ppermute | solution.py:731
  286.2 6.7 %collective-permute-start.46 = (bf16[256,256]{1,0:T(8,128)(2,1)S(1)}, bf16[256,256]{1,0:T(8,128)(2,1)S(1)}, u32[]{:S(2)}, u32[]{:S(2)}) collective-permute-start(bf16[256,256]{1,0:T(8,128)(2,1)S(1)} %copy-done.70), channel_id=1, source_target_pairs={{0,3},{1,2},{2,1},{3,0},{4,7},{5,6},{6,5},{7,4},{8,11},{9,10},{10,... | collective-permute-start | bytes 393224 | tf_op jit(solution)/shard_map/ppermute | solution.py:731
  293.7 12.7 %collective-permute-start.47 = (bf16[128,896]{1,0:T(8,128)(2,1)}, bf16[128,896]{1,0:T(8,128)(2,1)S(1)}, u32[]{:S(2)}, u32[]{:S(2)}) collective-permute-start(bf16[128,896]{1,0:T(8,128)(2,1)} %get-tuple-element.347), channel_id=1, source_target_pairs={{0,2},{2,0},{4,6},{6,4},{1,3},{3,1},{5,7},{7,5},{8,10},{10,8},{12,... | collective-permute-start | bytes 688136 | tf_op jit(solution)/shard_map/ppermute | solution.py:731
  295.4 11.6 %collective-permute-start.48 = (bf16[128,896]{1,0:T(8,128)(2,1)}, bf16[128,896]{1,0:T(8,128)(2,1)S(1)}, u32[]{:S(2)}, u32[]{:S(2)}) collective-permute-start(bf16[128,896]{1,0:T(8,128)(2,1)} %get-tuple-element.349), channel_id=1, source_target_pairs={{0,4},{2,6},{4,0},{6,2},{1,5},{3,7},{5,1},{7,3},{8,12},{10,14},{12... | collective-permute-start | bytes 688136 | tf_op jit(solution)/shard_map/ppermute | solution.py:731
  296.3 12.3 %collective-permute-start.49 = (bf16[128,896]{1,0:T(8,128)(2,1)S(1)}, bf16[128,896]{1,0:T(8,128)(2,1)}, u32[]{:S(2)}, u32[]{:S(2)}) collective-permute-start(bf16[128,896]{1,0:T(8,128)(2,1)S(1)} %get-tuple-element.348), channel_id=1, source_target_pairs={{0,6},{2,4},{4,2},{6,0},{1,7},{3,5},{5,3},{7,1},{8,14},{10,12},{12... | collective-permute-start | bytes 688136 | tf_op jit(solution)/shard_map/ppermute | solution.py:731
  312.0 4.7 %collective-permute-start.50 = (bf16[512,256]{1,0:T(8,128)(2,1)S(1)}, bf16[512,256]{1,0:T(8,128)(2,1)S(1)}, u32[]{:S(2)}, u32[]{:S(2)}) collective-permute-start(bf16[512,256]{1,0:T(8,128)(2,1)S(1)} %fusion.5), channel_id=1, source_target_pairs={{0,1},{1,0},{2,3},{3,2},{4,5},{5,4},{6,7},{7,6},{8,9},{9,8},{10,11... | collective-permute-start | bytes 786440 | tf_op jit(solution)/shard_map/ppermute | solution.py:727
  313.0 9.4 %collective-permute-start.54 = (bf16[128,896]{1,0:T(8,128)(2,1)}, bf16[128,896]{1,0:T(8,128)(2,1)S(1)}, u32[]{:S(2)}, u32[]{:S(2)}) collective-permute-start(bf16[128,896]{1,0:T(8,128)(2,1)} %get-tuple-element.350), channel_id=1, source_target_pairs={{0,2},{2,0},{4,6},{6,4},{1,3},{3,1},{5,7},{7,5},{8,10},{10,8},{12,... | collective-permute-start | bytes 688136 | tf_op jit(solution)/shard_map/ppermute | solution.py:731
  313.7 12.7 %collective-permute-start.55 = (bf16[128,896]{1,0:T(8,128)(2,1)}, bf16[128,896]{1,0:T(8,128)(2,1)}, u32[]{:S(2)}, u32[]{:S(2)}) collective-permute-start(bf16[128,896]{1,0:T(8,128)(2,1)} %get-tuple-element.352), channel_id=1, source_target_pairs={{0,4},{2,6},{4,0},{6,2},{1,5},{3,7},{5,1},{7,3},{8,12},{10,14},{12... | collective-permute-start | bytes 688136 | tf_op jit(solution)/shard_map/ppermute | solution.py:731
  315.2 11.7 %collective-permute-start.56 = (bf16[128,896]{1,0:T(8,128)(2,1)}, bf16[128,896]{1,0:T(8,128)(2,1)}, u32[]{:S(2)}, u32[]{:S(2)}) collective-permute-start(bf16[128,896]{1,0:T(8,128)(2,1)} %get-tuple-element.351), channel_id=1, source_target_pairs={{0,6},{2,4},{4,2},{6,0},{1,7},{3,5},{5,3},{7,1},{8,14},{10,12},{12... | collective-permute-start | bytes 688136 | tf_op jit(solution)/shard_map/ppermute | solution.py:731
  320.1 11.5 %collective-permute-start.51 = (bf16[128,256]{1,0:T(8,128)(2,1)S(1)}, bf16[128,256]{1,0:T(8,128)(2,1)S(1)}, u32[]{:S(2)}, u32[]{:S(2)}) collective-permute-start(bf16[128,256]{1,0:T(8,128)(2,1)S(1)} %get-tuple-element.355), channel_id=1, source_target_pairs={{0,2},{2,0},{4,6},{6,4},{1,3},{3,1},{5,7},{7,5},{8,10},{10,8},{12,... | collective-permute-start | bytes 196616 | tf_op jit(solution)/shard_map/ppermute | solution.py:731
  320.9 11.3 %collective-permute-start.52 = (bf16[128,256]{1,0:T(8,128)(2,1)S(1)}, bf16[128,256]{1,0:T(8,128)(2,1)S(1)}, u32[]{:S(2)}, u32[]{:S(2)}) collective-permute-start(bf16[128,256]{1,0:T(8,128)(2,1)S(1)} %get-tuple-element.357), channel_id=1, source_target_pairs={{0,4},{2,6},{4,0},{6,2},{1,5},{3,7},{5,1},{7,3},{8,12},{10,14},{12... | collective-permute-start | bytes 196616 | tf_op jit(solution)/shard_map/ppermute | solution.py:731
  322.4 10.5 %collective-permute-start.53 = (bf16[128,256]{1,0:T(8,128)(2,1)S(1)}, bf16[128,256]{1,0:T(8,128)(2,1)S(1)}, u32[]{:S(2)}, u32[]{:S(2)}) collective-permute-start(bf16[128,256]{1,0:T(8,128)(2,1)S(1)} %get-tuple-element.356), channel_id=1, source_target_pairs={{0,6},{2,4},{4,2},{6,0},{1,7},{3,5},{5,3},{7,1},{8,14},{10,12},{12... | collective-permute-start | bytes 196616 | tf_op jit(solution)/shard_map/ppermute | solution.py:731
  328.1 14.9 %collective-permute-start.59 = (bf16[28,3840]{1,0:T(8,128)(2,1)}, bf16[28,3840]{1,0:T(8,128)(2,1)S(1)}, u32[]{:S(2)}, u32[]{:S(2)}) collective-permute-start(bf16[28,3840]{1,0:T(8,128)(2,1)} %get-tuple-element.336), channel_id=1, source_target_pairs={{0,0},{1,4},{2,2},{3,6},{4,1},{5,5},{6,3},{7,7},{8,8},{9,12},{10,1... | collective-permute-start | bytes 645128 | tf_op jit(solution)/shard_map/ppermute | solution.py:747
  329.7 13.3 %collective-permute-start.60 = (bf16[28,3840]{1,0:T(8,128)(2,1)}, bf16[28,3840]{1,0:T(8,128)(2,1)S(1)}, u32[]{:S(2)}, u32[]{:S(2)}) collective-permute-start(bf16[28,3840]{1,0:T(8,128)(2,1)} %get-tuple-element.337), channel_id=1, source_target_pairs={{0,1},{1,5},{2,3},{3,7},{4,0},{5,4},{6,2},{7,6},{8,9},{9,13},{10,1... | collective-permute-start | bytes 645128 | tf_op jit(solution)/shard_map/ppermute | solution.py:747
  331.7 11.3 %collective-permute-start.61 = (bf16[28,3840]{1,0:T(8,128)(2,1)}, bf16[28,3840]{1,0:T(8,128)(2,1)S(1)}, u32[]{:S(2)}, u32[]{:S(2)}) collective-permute-start(bf16[28,3840]{1,0:T(8,128)(2,1)} %get-tuple-element.338), channel_id=1, source_target_pairs={{0,2},{1,6},{2,0},{3,4},{4,3},{5,7},{6,1},{7,5},{8,10},{9,14},{10,... | collective-permute-start | bytes 645128 | tf_op jit(solution)/shard_map/ppermute | solution.py:747
  332.2 12.7 %collective-permute-start.62 = (bf16[28,3840]{1,0:T(8,128)(2,1)}, bf16[28,3840]{1,0:T(8,128)(2,1)S(1)}, u32[]{:S(2)}, u32[]{:S(2)}) collective-permute-start(bf16[28,3840]{1,0:T(8,128)(2,1)} %get-tuple-element.339), channel_id=1, source_target_pairs={{0,3},{1,7},{2,1},{3,5},{4,2},{5,6},{6,0},{7,4},{8,11},{9,15},{10,... | collective-permute-start | bytes 645128 | tf_op jit(solution)/shard_map/ppermute | solution.py:747
  333.0 8.4 %collective-permute-start.57 = (bf16[64,2048]{1,0:T(8,128)(2,1)S(1)}, bf16[64,2048]{1,0:T(8,128)(2,1)S(1)}, u32[]{:S(2)}, u32[]{:S(2)}) collective-permute-start(bf16[64,2048]{1,0:T(8,128)(2,1)S(1)} %slice.89), channel_id=1, source_target_pairs={{0,8},{8,0},{16,24},{24,16},{1,9},{9,1},{17,25},{25,17},{2,10},{10... | collective-permute-start | bytes 786440 | tf_op jit(solution)/shard_map/ppermute | solution.py:727
  341.5 8.5 %collective-permute-start.58 = (bf16[32,2048]{1,0:T(8,128)(2,1)S(1)}, bf16[32,2048]{1,0:T(8,128)(2,1)S(1)}, u32[]{:S(2)}, u32[]{:S(2)}) collective-permute-start(bf16[32,2048]{1,0:T(8,128)(2,1)S(1)} %slice.105), channel_id=1, source_target_pairs={{0,16},{8,24},{16,0},{24,8},{1,17},{9,25},{17,1},{25,9},{2,18},{10... | collective-permute-start | bytes 393224 | tf_op jit(solution)/shard_map/ppermute | solution.py:727
  (75 other events, 430.8 us)
Sparse Core Ops, SparseCore 0:
  48.7 69.7 all-gather.1
  224.5 73.9 reduce-scatter.1

commit v2 on v1

--- a/solution.py
+++ b/solution.py
@@ -16,7 +16,7 @@
 SCALE = HD ** (-0.5)
 TILE = 256
 MIB = 1 << 20
-VMEM_LIMIT = 60 * MIB
+VMEM_LIMIT = 54 * MIB
 F32 = jnp.float32
 BF16 = jnp.bfloat16
 AXES = ("fz", "fy", "cx", "cc")

time: 366 us -> 364 us (level)
    unnamed x152 -> x172, local copies, waits for them, and re-layouts: 6 us -> 8.37 us
  transfers between devices with their start and end apart: 65 -> 65, of which waited for: 21 -> 20; matrix products, arithmetic and copies ran while one was open for 8% -> 6% of each run, Pallas kernels for 49% -> 49%
where the time goes in v2:
time: 364 us; the launch traced here: 358 us
  Pallas kernels  179 us (49%)
  starting transfers between devices  70.9 us (19%)
  waiting for transfers between devices  56.5 us (16%)
  other arithmetic  16 us (4%)
  between operations  15.4 us (4%)
  local copies, waits for them, and re-layouts  14.8 us (4%)
  matrix products  6.01 us (2%)
    pallas_call x2, Pallas kernels, mlp(): pl.pallas_call(mlp_kernel, grid=(2,), in_specs=[*[once(0)] * 4, *[once(se...  52.4 us
    ppermute x39, starting transfers between devices, jump_swap(): return lax.ppermute(value, axes, [(i, i ^ jump) for i in range(4)])  43.2 us
    pallas_call x2, Pallas kernels, attend_back(): pl.pallas_call(attend_back_kernel, grid=(1,), in_specs=[pl.BlockSpec(memo...  36.5 us
    ppermute x39, waiting for transfers between devices, jump_swap(): return lax.ppermute(value, axes, [(i, i ^ jump) for i in range(4)])  24 us
    pallas_call x1, Pallas kernels, mlp_grad(): pl.pallas_call(mlp_grad_kernel, grid=(3,), in_specs=[turned_block, turned...  20 us
    pallas_call x2, Pallas kernels, attend(): pl.pallas_call(attend_kernel, grid=(1,), in_specs=[pl.BlockSpec(memory_sp...  19.2 us
    ppermute x16, waiting for transfers between devices, bit_swap(): return lax.ppermute(value, axis, [(i, i ^ 1 << bit) for i in range(size)])  17.8 us
    ppermute x16, starting transfers between devices, bit_swap(): return lax.ppermute(value, axis, [(i, i ^ 1 << bit) for i in range(size)])  16.4 us
  transfers between devices with their start and end apart: 65, of which 20 were waited for; matrix products, arithmetic and copies ran while one was open for 6% of the time, Pallas kernels for 49%

profile of v2, /device:TPU:0, one launch (start us, length us, event | category | flops | bytes accessed | tf_op | source)
XLA Modules:
  0.0 358.3 jit_solution(11087827765734669043)
XLA Ops:
  9.0 4.1 %collective-permute-start = (bf16[32,2048]{1,0:T(8,128)(2,1)S(1)}, bf16[32,2048]{1,0:T(8,128)(2,1)S(1)}, u32[]{:S(2)}, u32[]{:S(2)}) collective-permute-start(bf16[32,2048]{1,0:T(8,128)(2,1)S(1)} %pad_maximum_fusion.7), channel_id=1, source_target_pairs={{0,16},{8,24},{16,0},{24,8},{1,17},{9,25},{17,1},{25,9},{2,18},{10... | collective-permute-start | bytes 393224 | tf_op jit(solution)/shard_map/ppermute | solution.py:727
  13.1 1.5 collective-permute-start.2
  17.1 1.8 fusion.14
  18.9 2.2 pack_columns.1
  21.9 1.6 collective-permute-start.1
  23.6 2.0 fusion.order_ref.refs_14_
  26.2 2.8 collective-permute-start.4
  29.6 2.2 collective-permute-start.6
  31.8 4.9 %collective-permute-done.4.refs_1_ = bf16[28,3840]{1,0:T(8,128)(2,1)S(1)} collective-permute-done((bf16[28,3840]{1,0:T(8,128)(2,1)S(1)}, bf16[28,3840]{1,0:T(8,128)(2,1)S(1)}, u32[]{:S(2)}, u32[]{:S(2)}) %collective-permute-start.4) | collective-permute-done | bytes 215072 | tf_op jit(solution)/shard_map/ppermute | solution.py:739
  36.7 5.2 %collective-permute-done.5.refs_2_ = bf16[28,3840]{1,0:T(8,128)(2,1)S(1)} collective-permute-done((bf16[28,3840]{1,0:T(8,128)(2,1)S(1)}, bf16[28,3840]{1,0:T(8,128)(2,1)S(1)}, u32[]{:S(2)}, u32[]{:S(2)}) %collective-permute-start.5) | collective-permute-done | bytes 215072 | tf_op jit(solution)/shard_map/ppermute | solution.py:739
  41.9 2.8 collective-permute-done.6.refs_3_
  45.7 2.9 assemble_rows.1
  49.7 2.9 collective-permute-start.8
  52.7 5.9 %collective-permute-done.7 = bf16[128,1152]{1,0:T(8,128)(2,1)S(1)} collective-permute-done((bf16[128,1152]{1,0:T(8,128)(2,1)S(1)}, bf16[128,1152]{1,0:T(8,128)(2,1)S(1)}, u32[]{:S(2)}, u32[]{:S(2)}) %collective-permute-start.7) | collective-permute-done | bytes 294944 | tf_op jit(solution)/shard_map/ppermute | solution.py:731
  58.5 6.7 %collective-permute-done.8 = bf16[128,1152]{1,0:T(8,128)(2,1)S(1)} collective-permute-done((bf16[128,1152]{1,0:T(8,128)(2,1)S(1)}, bf16[128,1152]{1,0:T(8,128)(2,1)S(1)}, u32[]{:S(2)}, u32[]{:S(2)}) %collective-permute-start.8) | collective-permute-done | bytes 294944 | tf_op jit(solution)/shard_map/ppermute | solution.py:731
  66.2 1.8 collective-permute-start.14
  70.0 8.0 %norm_project_rotate.1 = (bf16[512,512]{1,0:T(8,128)(2,1)}, bf16[512,512]{1,0:T(8,128)(2,1)}, bf16[512,896]{1,0:T(8,128)(2,1)}, bf16[512,256]{1,0:T(8,128)(2,1)}, f32[1,896]{1,0:T(1,128)}, /*index=5*/f32[1,896]{1,0:T(1,128)}) custom-call(bf16[512,896]{1,0:T(8,128)(2,1)} %bitcast.47, bf16[896,1024]{1,0:T(8,128)(2,1)} %fusion.order_ref.refs_14_, ...), custom_call_target="tpu_custom_call" | custom-call | flops 2147483648 | bytes 12582912 | tf_op jit(solution)/shard_map/norm_project_rotate/pallas_call | solution.py:119
  78.1 1.5 collective-permute-start.12
  79.6 7.1 %collective-permute-done.12.kv_2 = bf16[2,256,256]{2,1,0:T(8,128)(2,1)S(1)} collective-permute-done((bf16[2,256,256]{2,1,0:T(8,128)(2,1)}, bf16[2,256,256]{2,1,0:T(8,128)(2,1)S(1)}, u32[]{:S(2)}, u32[]{:S(2)}) %collective-permute-start.12) | collective-permute-done | bytes 262176 | tf_op jit(solution)/shard_map/ppermute | solution.py:727
  87.3 1.6 collective-permute-done.14.c_2
  88.9 1.5 collective-permute-start.15
  91.3 1.2 collective-permute-start.17
  93.2 9.4 %attention_forward.2 = (bf16[256,896]{1,0:T(8,128)(2,1)}, f32[256,128]{1,0:T(8,128)}) custom-call(s32[1]{0:T(128)} %bitcast.block_ref, bf16[512,896]{1,0:T(8,128)(2,1)} %get-tuple-element.193.q_ref, bf16[2,256,256]{2,1,0:T(8,128)(2,1)} %bitcast.61, bf16[2,256,256]{2,1,0:T(8,128)(2,1)} %copy-done.69, bf16[2,256,256]{2,1,0:T(8,128)(2,1)} %copy-done.67, ...), custom_call_target="tpu_custom_call" | custom-call | flops 3758096384 | bytes 917504 | tf_op jit(solution)/shard_map/attention_forward/pallas_call | solution.py:377
  102.9 1.8 collective-permute-start.22
  106.3 5.3 %project_out_norm.2 = (f32[256,896]{1,0:T(8,128)}, bf16[256,896]{1,0:T(8,128)(2,1)}) custom-call(bf16[256,896]{1,0:T(8,128)(2,1)} %get-tuple-element.202.attended_ref.out_ref, bf16[512,896]{1,0:T(8,128)(2,1)} %bitcast.48, bf16[512,896]{1,0:T(8,128)(2,1)} %copy-done, bf16[512,896]{1,0:T(8,128)(2,1)} %copy-done.1, bf16[896,1024]{1,0:T(8,128)(2,1)} %fusion.order_ref.refs_14_, ...), custom_call_target="tpu_custom_call" | custom-call | flops 1233125376 | bytes 8388608 | tf_op jit(solution)/shard_map/project_out_norm/pallas_call | solution.py:174
  111.5 1.5 collective-permute-start.19
  115.0 9.8 %attention_forward.3 = (bf16[256,896]{1,0:T(8,128)(2,1)}, f32[256,128]{1,0:T(8,128)}) custom-call(s32[1]{0:T(128)} %bitcast.block_ref, bf16[512,896]{1,0:T(8,128)(2,1)} %get-tuple-element.193.q_ref, bf16[2,256,256]{2,1,0:T(8,128)(2,1)} %bitcast.62, bf16[2,256,256]{2,1,0:T(8,128)(2,1)} %copy-done.69, bf16[2,256,256]{2,1,0:T(8,128)(2,1)} %copy-done.67, ...), custom_call_target="tpu_custom_call" | custom-call | flops 3758096384 | bytes 917504 | tf_op jit(solution)/shard_map/attention_forward/pallas_call | solution.py:377
  124.9 5.6 %project_out_norm.3 = (f32[256,896]{1,0:T(8,128)}, bf16[256,896]{1,0:T(8,128)(2,1)}) custom-call(bf16[256,896]{1,0:T(8,128)(2,1)} %get-tuple-element.221.attended_ref.out_ref, bf16[512,896]{1,0:T(8,128)(2,1)} %bitcast.49, bf16[512,896]{1,0:T(8,128)(2,1)} %copy-done, bf16[512,896]{1,0:T(8,128)(2,1)} %copy-done.1, bf16[896,1024]{1,0:T(8,128)(2,1)} %fusion.order_ref.refs_14_, ...), custom_call_target="tpu_custom_call" | custom-call | flops 1233125376 | bytes 8388608 | tf_op jit(solution)/shard_map/project_out_norm/pallas_call | solution.py:174
  130.4 1.5 collective-permute-start.24
  134.0 3.5 collective-permute-done.21.n_3
  137.6 26.0 %feed_forward.2 = (f32[256,896]{1,0:T(8,128)}, bf16[256,896]{1,0:T(8,128)(2,1)}, bf16[256,896]{1,0:T(8,128)(2,1)}, bf16[256,896]{1,0:T(8,128)(2,1)}, f32[256,896...) custom-call(bf16[256,896]{1,0:T(8,128)(2,1)} %get-tuple-element.206., ...), custom_call_target="tpu_custom_call" | custom-call | flops 14092861440 | bytes 14745600 | tf_op jit(solution)/shard_map/feed_forward/pallas_call | solution.py:563
  163.6 1.5 collective-permute-start.27
  167.2 26.3 %feed_forward.3 = (f32[256,896]{1,0:T(8,128)}, bf16[256,896]{1,0:T(8,128)(2,1)}, bf16[256,896]{1,0:T(8,128)(2,1)}, bf16[256,896]{1,0:T(8,128)(2,1)}, f32[256,896...) custom-call(bf16[256,896]{1,0:T(8,128)(2,1)} %get-tuple-element.223., ...), custom_call_target="tpu_custom_call" | custom-call | flops 14092861440 | bytes 14745600 | tf_op jit(solution)/shard_map/feed_forward/pallas_call | solution.py:563
  193.5 1.5 collective-permute-start.30
  195.8 1.2 collective-permute-start.32
  198.0 5.8 %norm_back_project.2 = (f32[256,896]{1,0:T(8,128)}, bf16[256,512]{1,0:T(8,128)(2,1)}, bf16[256,512]{1,0:T(8,128)(2,1)}, bf16[256,896]{1,0:T(8,128)(2,1)}, f32[1,896]{1,0:T(1,128)}) custom-call(f32[256,896]{1,0:T(8,128)} %get-tuple-element.233.own_ref, bf16[256,896]{1,0:T(8,128)(2,1)} %copy-done.33, bf16[256,896]{1,0:T(8,128)(2,1)} %copy-done.34, ...), custom_call_target="tpu_custom_call" | custom-call | flops 822083584 | bytes 12582912 | tf_op jit(solution)/shard_map/norm_back_project/pallas_call | solution.py:233
  203.8 20.0 %feed_forward_gradients.1 = bf16[896,3840]{1,0:T(8,128)(2,1)} custom-call(bf16[2,896,1024]{2,1,0:T(8,128)(2,1)} %get-tuple-element.216.turned_0, bf16[2,896,1024]{2,1,0:T(8,128)(2,1)} %get-tuple-element.239.turned_1, bf16[3,1024,1280]{2,1,0:T(8,128)(2,1)} %get-tuple-element.240.kept_0, bf16[3,1024,1280]{2,1,0:T(8,128)(2,1)} %get-tuple-element.228.kept_1), custom_call_target="tpu_custom_call" | custom-call | flops 14092861440 | bytes 22609920 | tf_op jit(solution)/shard_map/feed_forward_gradients/pallas_call | solution.py:607
  226.3 1.5 collective-permute-start.33
  229.8 1.5 collective-permute-start.40
  232.7 18.3 %attention_backward.2 = (bf16[256,896]{1,0:T(8,128)(2,1)}, f32[256,256]{1,0:T(8,128)}, bf16[256,256]{1,0:T(8,128)(2,1)}, bf16[256,256]{1,0:T(8,128)(2,1)}, bf16[256,256]{1,0:T(8,128)(2,1)}) custom-call(s32[1]{0:T(128)} %bitcast.block_ref, bf16[512,896]{1,0:T(8,128)(2,1)} %get-tuple-element.193.q_ref, bf16[2,256,256]{2,1,0:T(8,128)(2,1)} %bitcast.63, ...), custom_call_target="tpu_custom_call" | custom-call | flops 9395240960 | bytes 1835008 | tf_op jit(solution)/shard_map/attention_backward/pallas_call | solution.py:484
  251.1 1.6 collective-permute-start.37
  253.0 5.9 %norm_back_project.3 = (f32[256,896]{1,0:T(8,128)}, bf16[256,512]{1,0:T(8,128)(2,1)}, bf16[256,512]{1,0:T(8,128)(2,1)}, bf16[256,896]{1,0:T(8,128)(2,1)}, f32[1,896]{1,0:T(1,128)}) custom-call(f32[256,896]{1,0:T(8,128)} %get-tuple-element.259.own_ref, bf16[256,896]{1,0:T(8,128)(2,1)} %copy-done.30, bf16[256,896]{1,0:T(8,128)(2,1)} %copy-done.31, ...), custom_call_target="tpu_custom_call" | custom-call | flops 822083584 | bytes 12582912 | tf_op jit(solution)/shard_map/norm_back_project/pallas_call | solution.py:233
  258.9 1.7 convolution_convert_fusion.2
  260.7 1.3 collective-permute-start.42
  263.1 18.2 %attention_backward.3 = (bf16[256,896]{1,0:T(8,128)(2,1)}, f32[256,256]{1,0:T(8,128)}, bf16[256,256]{1,0:T(8,128)(2,1)}, bf16[256,256]{1,0:T(8,128)(2,1)}, bf16[256,256]{1,0:T(8,128)(2,1)}) custom-call(s32[1]{0:T(128)} %bitcast.block_ref, bf16[512,896]{1,0:T(8,128)(2,1)} %get-tuple-element.193.q_ref, bf16[2,256,256]{2,1,0:T(8,128)(2,1)} %bitcast.64, ...), custom_call_target="tpu_custom_call" | custom-call | flops 9395240960 | bytes 1835008 | tf_op jit(solution)/shard_map/attention_backward/pallas_call | solution.py:484
  282.6 1.7 convolution_convert_fusion
  286.4 1.4 pad_maximum_fusion.refs_11_
  289.2 1.4 add_convert_fusion
  292.7 2.0 collective-permute-start.47
  296.4 9.2 %input_gradient.1 = (bf16[512,256]{1,0:T(8,128)(2,1)}, bf16[512,896]{1,0:T(8,128)(2,1)}, f32[1,896]{1,0:T(1,128)}, f32[1,1152]{1,0:T(1,128)}) custom-call(bf16[256,896]{1,0:T(8,128)(2,1)} %get-tuple-element.258.refs_0_, bf16[256,896]{1,0:T(8,128)(2,1)} %get-tuple-element.284.refs_1_, f32[256,256]{1,0:T(8,128)} %get-tuple-element.285.refs_2_, ...), custom_call_target="tpu_custom_call" | custom-call | flops 3170893824 | bytes 16777216 | tf_op jit(solution)/shard_map/input_gradient/pallas_call | solution.py:269
  305.8 1.7 collective-permute-done.49
  311.4 1.8 collective-permute-start.55
  313.2 1.2 collective-permute-start.56
  315.1 3.0 cut_rows.1
  318.7 1.8 collective-permute-start.52
  320.4 1.2 collective-permute-start.53
  321.6 2.3 collective-permute-done.55
  326.0 1.6 collective-permute-start.59
  327.6 2.2 collective-permute-start.60
  331.1 1.7 collective-permute-start.57
  333.4 6.1 %collective-permute-done.57 = bf16[64,2048]{1,0:T(8,128)(2,1)S(1)} collective-permute-done((bf16[64,2048]{1,0:T(8,128)(2,1)S(1)}, bf16[64,2048]{1,0:T(8,128)(2,1)S(1)}, u32[]{:S(2)}, u32[]{:S(2)}) %collective-permute-start.57) | collective-permute-done | bytes 262176 | tf_op jit(solution)/shard_map/ppermute | solution.py:727
  341.2 1.7 collective-permute-done.62.refs_3_
  343.7 2.7 unpack_columns.1
  346.4 1.7 collective-permute-done.58
  (324 shorter events, 53.4 us)
Async XLA Ops:
  7.2 130.4 %all-gather.2.cloned.1.call-start = ((), (), s32[]{:S(2)}) async-start(), calls=%async_computation.1 | async-start | bytes 7741440 | tf_op jit(solution)/shard_map/all_gather | solution.py:874
  9.0 12.9 %collective-permute-start = (bf16[32,2048]{1,0:T(8,128)(2,1)S(1)}, bf16[32,2048]{1,0:T(8,128)(2,1)S(1)}, u32[]{:S(2)}, u32[]{:S(2)}) collective-permute-start(bf16[32,2048]{1,0:T(8,128)(2,1)S(1)} %pad_maximum_fusion.7), channel_id=1, source_target_pairs={{0,16},{8,24},{16,0},{24,8},{1,17},{9,25},{17,1},{25,9},{2,18},{10... | collective-permute-start | bytes 393224 | tf_op jit(solution)/shard_map/ppermute | solution.py:727
  13.1 31.6 %collective-permute-start.2 = (bf16[512,896]{1,0:T(8,128)(2,1)}, bf16[512,896]{1,0:T(8,128)(2,1)S(1)}, u32[]{:S(2)}, u32[]{:S(2)}) collective-permute-start(bf16[512,896]{1,0:T(8,128)(2,1)} %bitcast.41), channel_id=1, source_target_pairs={{0,2},{2,0},{1,3},{3,1},{4,6},{6,4},{5,7},{7,5},{8,10},{10,8},{9,1... | collective-permute-start | bytes 2752520 | tf_op jit(solution)/shard_map/ppermute | solution.py:727
  21.9 7.6 %collective-permute-start.1 = (bf16[64,2048]{1,0:T(8,128)(2,1)S(1)}, bf16[64,2048]{1,0:T(8,128)(2,1)S(1)}, u32[]{:S(2)}, u32[]{:S(2)}) collective-permute-start(bf16[64,2048]{1,0:T(8,128)(2,1)S(1)} %pad_maximum_fusion.6), channel_id=1, source_target_pairs={{0,8},{8,0},{16,24},{24,16},{1,9},{9,1},{17,25},{25,17},{2,10},{10... | collective-permute-start | bytes 786440 | tf_op jit(solution)/shard_map/ppermute | solution.py:727
  25.5 6.2 %collective-permute-start.3 = (bf16[28,3840]{1,0:T(8,128)(2,1)S(1)}, bf16[28,3840]{1,0:T(8,128)(2,1)S(1)}, u32[]{:S(2)}, u32[]{:S(2)}) collective-permute-start(bf16[28,3840]{1,0:T(8,128)(2,1)S(1)} %copy-done.76), channel_id=1, source_target_pairs={{0,0},{1,4},{2,2},{3,6},{4,1},{5,5},{6,3},{7,7},{8,8},{9,12},{10,1... | collective-permute-start | bytes 645128 | tf_op jit(solution)/shard_map/ppermute | solution.py:739
  26.2 10.4 %collective-permute-start.4 = (bf16[28,3840]{1,0:T(8,128)(2,1)S(1)}, bf16[28,3840]{1,0:T(8,128)(2,1)S(1)}, u32[]{:S(2)}, u32[]{:S(2)}) collective-permute-start(bf16[28,3840]{1,0:T(8,128)(2,1)S(1)} %copy-done.75), channel_id=1, source_target_pairs={{0,4},{1,0},{2,6},{3,2},{4,5},{5,1},{6,7},{7,3},{8,12},{9,8},{10,1... | collective-permute-start | bytes 645128 | tf_op jit(solution)/shard_map/ppermute | solution.py:739
  29.0 12.8 %collective-permute-start.5 = (bf16[28,3840]{1,0:T(8,128)(2,1)S(1)}, bf16[28,3840]{1,0:T(8,128)(2,1)S(1)}, u32[]{:S(2)}, u32[]{:S(2)}) collective-permute-start(bf16[28,3840]{1,0:T(8,128)(2,1)S(1)} %copy-done.74), channel_id=1, source_target_pairs={{0,2},{1,6},{2,0},{3,4},{4,3},{5,7},{6,1},{7,5},{8,10},{9,14},{10,... | collective-permute-start | bytes 645128 | tf_op jit(solution)/shard_map/ppermute | solution.py:739
  29.6 15.1 %collective-permute-start.6 = (bf16[28,3840]{1,0:T(8,128)(2,1)S(1)}, bf16[28,3840]{1,0:T(8,128)(2,1)S(1)}, u32[]{:S(2)}, u32[]{:S(2)}) collective-permute-start(bf16[28,3840]{1,0:T(8,128)(2,1)S(1)} %copy-done.73), channel_id=1, source_target_pairs={{0,6},{1,2},{2,4},{3,0},{4,7},{5,3},{6,5},{7,1},{8,14},{9,10},{10,... | collective-permute-start | bytes 645128 | tf_op jit(solution)/shard_map/ppermute | solution.py:739
  48.6 266.5 %reduce-scatter.2.cloned.1.call-start = ((), (), s32[]{:S(2)}) async-start(), calls=%async_computation.2 | async-start | bytes 7741440 | tf_op jit(solution)/shard_map/reduce_scatter | solution.py:922
  48.6 9.9 %collective-permute-start.7 = (bf16[128,1152]{1,0:T(8,128)(2,1)S(1)}, bf16[128,1152]{1,0:T(8,128)(2,1)S(1)}, u32[]{:S(2)}, u32[]{:S(2)}) collective-permute-start(bf16[128,1152]{1,0:T(8,128)(2,1)S(1)} %slice.80), channel_id=1, source_target_pairs={{0,2},{2,0},{4,6},{6,4},{1,3},{3,1},{5,7},{7,5},{8,10},{10,8},{12,... | collective-permute-start | bytes 884744 | tf_op jit(solution)/shard_map/ppermute | solution.py:731
  49.7 15.5 %collective-permute-start.8 = (bf16[128,1152]{1,0:T(8,128)(2,1)S(1)}, bf16[128,1152]{1,0:T(8,128)(2,1)S(1)}, u32[]{:S(2)}, u32[]{:S(2)}) collective-permute-start(bf16[128,1152]{1,0:T(8,128)(2,1)S(1)} %slice.80), channel_id=1, source_target_pairs={{0,4},{2,6},{4,0},{6,2},{1,5},{3,7},{5,1},{7,3},{8,12},{10,14},{12... | collective-permute-start | bytes 884744 | tf_op jit(solution)/shard_map/ppermute | solution.py:731
  52.7 13.3 %collective-permute-start.9 = (bf16[128,1152]{1,0:T(8,128)(2,1)S(1)}, bf16[128,1152]{1,0:T(8,128)(2,1)S(1)}, u32[]{:S(2)}, u32[]{:S(2)}) collective-permute-start(bf16[128,1152]{1,0:T(8,128)(2,1)S(1)} %slice.80), channel_id=1, source_target_pairs={{0,6},{2,4},{4,2},{6,0},{1,7},{3,5},{5,3},{7,1},{8,14},{10,12},{12... | collective-permute-start | bytes 884744 | tf_op jit(solution)/shard_map/ppermute | solution.py:731
  66.1 2.9 collective-permute-start.10
  66.2 22.8 %collective-permute-start.14 = (bf16[512,896]{1,0:T(8,128)(2,1)S(1)}, bf16[512,896]{1,0:T(8,128)(2,1)S(1)}, u32[]{:S(2)}, u32[]{:S(2)}) collective-permute-start(bf16[512,896]{1,0:T(8,128)(2,1)S(1)} %bitcast.46), channel_id=1, source_target_pairs={{0,4},{4,0},{1,5},{5,1},{2,6},{6,2},{3,7},{7,3},{8,12},{12,8},{9,1... | collective-permute-start | bytes 2752520 | tf_op jit(solution)/shard_map/ppermute | solution.py:727
  78.1 8.6 %collective-permute-start.12 = (bf16[2,256,256]{2,1,0:T(8,128)(2,1)}, bf16[2,256,256]{2,1,0:T(8,128)(2,1)S(1)}, u32[]{:S(2)}, u32[]{:S(2)}) collective-permute-start(bf16[2,256,256]{2,1,0:T(8,128)(2,1)} %bitcast.59), channel_id=1, source_target_pairs={{0,2},{2,0},{1,3},{3,1},{4,6},{6,4},{5,7},{7,5},{8,10},{10,8},{9,1... | collective-permute-start | bytes 786440 | tf_op jit(solution)/shard_map/ppermute | solution.py:727
  86.7 5.8 %collective-permute-start.11 = (bf16[2,256,256]{2,1,0:T(8,128)(2,1)}, bf16[2,256,256]{2,1,0:T(8,128)(2,1)S(1)}, u32[]{:S(2)}, u32[]{:S(2)}) collective-permute-start(bf16[2,256,256]{2,1,0:T(8,128)(2,1)} %bitcast.60), channel_id=1, source_target_pairs={{0,1},{1,0},{2,3},{3,2},{4,5},{5,4},{6,7},{7,6},{8,9},{9,8},{10,11... | collective-permute-start | bytes 786440 | tf_op jit(solution)/shard_map/ppermute | solution.py:727
  88.9 13.7 %collective-permute-start.15 = (bf16[128,896]{1,0:T(8,128)(2,1)S(1)}, bf16[128,896]{1,0:T(8,128)(2,1)S(1)}, u32[]{:S(2)}, u32[]{:S(2)}) collective-permute-start(bf16[128,896]{1,0:T(8,128)(2,1)S(1)} %slice.81), channel_id=1, source_target_pairs={{0,2},{2,0},{4,6},{6,4},{1,3},{3,1},{5,7},{7,5},{8,10},{10,8},{12,... | collective-permute-start | bytes 688136 | tf_op jit(solution)/shard_map/ppermute | solution.py:731
  90.5 12.2 %collective-permute-start.16 = (bf16[128,896]{1,0:T(8,128)(2,1)S(1)}, bf16[128,896]{1,0:T(8,128)(2,1)S(1)}, u32[]{:S(2)}, u32[]{:S(2)}) collective-permute-start(bf16[128,896]{1,0:T(8,128)(2,1)S(1)} %slice.81), channel_id=1, source_target_pairs={{0,4},{2,6},{4,0},{6,2},{1,5},{3,7},{5,1},{7,3},{8,12},{10,14},{12... | collective-permute-start | bytes 688136 | tf_op jit(solution)/shard_map/ppermute | solution.py:731
  91.3 11.4 %collective-permute-start.17 = (bf16[128,896]{1,0:T(8,128)(2,1)S(1)}, bf16[128,896]{1,0:T(8,128)(2,1)S(1)}, u32[]{:S(2)}, u32[]{:S(2)}) collective-permute-start(bf16[128,896]{1,0:T(8,128)(2,1)S(1)} %slice.81), channel_id=1, source_target_pairs={{0,6},{2,4},{4,2},{6,0},{1,7},{3,5},{5,3},{7,1},{8,14},{10,12},{12... | collective-permute-start | bytes 688136 | tf_op jit(solution)/shard_map/ppermute | solution.py:731
  102.8 2.5 collective-permute-start.18
  102.9 22.0 %collective-permute-start.22 = (bf16[256,896]{1,0:T(8,128)(2,1)S(1)}, bf16[256,896]{1,0:T(8,128)(2,1)S(1)}, u32[]{:S(2)}, u32[]{:S(2)}) collective-permute-start(bf16[256,896]{1,0:T(8,128)(2,1)S(1)} %slice.82), channel_id=1, source_target_pairs={{0,4},{4,0},{1,5},{5,1},{2,6},{6,2},{3,7},{7,3},{8,12},{12,8},{9,1... | collective-permute-start | bytes 1376264 | tf_op jit(solution)/shard_map/ppermute | solution.py:727
  104.7 20.2 %collective-permute-start.23 = (bf16[256,896]{1,0:T(8,128)(2,1)S(1)}, bf16[256,896]{1,0:T(8,128)(2,1)S(1)}, u32[]{:S(2)}, u32[]{:S(2)}) collective-permute-start(bf16[256,896]{1,0:T(8,128)(2,1)S(1)} %slice.83), channel_id=1, source_target_pairs={{0,2},{2,0},{1,3},{3,1},{4,6},{6,4},{5,7},{7,5},{8,10},{10,8},{9,1... | collective-permute-start | bytes 1376264 | tf_op jit(solution)/shard_map/ppermute | solution.py:727
  111.5 21.3 %collective-permute-start.19 = (bf16[256,896]{1,0:T(8,128)(2,1)}, bf16[256,896]{1,0:T(8,128)(2,1)S(1)}, u32[]{:S(2)}, u32[]{:S(2)}) collective-permute-start(bf16[256,896]{1,0:T(8,128)(2,1)} %get-tuple-element.206.n_0), channel_id=1, source_target_pairs={{0,2},{2,0},{4,6},{6,4},{1,3},{3,1},{5,7},{7,5},{8,10},{10,8},{12,... | collective-permute-start | bytes 1376264 | tf_op jit(solution)/shard_map/ppermute | solution.py:731
  113.0 21.0 %collective-permute-start.20 = (bf16[256,896]{1,0:T(8,128)(2,1)}, bf16[256,896]{1,0:T(8,128)(2,1)S(1)}, u32[]{:S(2)}, u32[]{:S(2)}) collective-permute-start(bf16[256,896]{1,0:T(8,128)(2,1)} %get-tuple-element.206.n_0), channel_id=1, source_target_pairs={{0,4},{2,6},{4,0},{6,2},{1,5},{3,7},{5,1},{7,3},{8,12},{10,14},{12... | collective-permute-start | bytes 1376264 | tf_op jit(solution)/shard_map/ppermute | solution.py:731
  113.8 23.8 %collective-permute-start.21 = (bf16[256,896]{1,0:T(8,128)(2,1)}, bf16[256,896]{1,0:T(8,128)(2,1)}, u32[]{:S(2)}, u32[]{:S(2)}) collective-permute-start(bf16[256,896]{1,0:T(8,128)(2,1)} %get-tuple-element.206.n_0), channel_id=1, source_target_pairs={{0,6},{2,4},{4,2},{6,0},{1,7},{3,5},{5,3},{7,1},{8,14},{10,12},{12... | collective-permute-start | bytes 1376264 | tf_op jit(solution)/shard_map/ppermute | solution.py:731
  130.4 33.1 %collective-permute-start.24 = (bf16[256,896]{1,0:T(8,128)(2,1)}, bf16[256,896]{1,0:T(8,128)(2,1)S(1)}, u32[]{:S(2)}, u32[]{:S(2)}) collective-permute-start(bf16[256,896]{1,0:T(8,128)(2,1)} %get-tuple-element.223.n_0), channel_id=1, source_target_pairs={{0,2},{2,0},{4,6},{6,4},{1,3},{3,1},{5,7},{7,5},{8,10},{10,8},{12,... | collective-permute-start | bytes 1376264 | tf_op jit(solution)/shard_map/ppermute | solution.py:731
  132.0 31.6 %collective-permute-start.25 = (bf16[256,896]{1,0:T(8,128)(2,1)}, bf16[256,896]{1,0:T(8,128)(2,1)S(1)}, u32[]{:S(2)}, u32[]{:S(2)}) collective-permute-start(bf16[256,896]{1,0:T(8,128)(2,1)} %get-tuple-element.223.n_0), channel_id=1, source_target_pairs={{0,4},{2,6},{4,0},{6,2},{1,5},{3,7},{5,1},{7,3},{8,12},{10,14},{12... | collective-permute-start | bytes 1376264 | tf_op jit(solution)/shard_map/ppermute | solution.py:731
  132.8 30.8 %collective-permute-start.26 = (bf16[256,896]{1,0:T(8,128)(2,1)}, bf16[256,896]{1,0:T(8,128)(2,1)S(1)}, u32[]{:S(2)}, u32[]{:S(2)}) collective-permute-start(bf16[256,896]{1,0:T(8,128)(2,1)} %get-tuple-element.223.n_0), channel_id=1, source_target_pairs={{0,6},{2,4},{4,2},{6,0},{1,7},{3,5},{5,3},{7,1},{8,14},{10,12},{12... | collective-permute-start | bytes 1376264 | tf_op jit(solution)/shard_map/ppermute | solution.py:731
  163.6 32.2 %collective-permute-start.27 = (bf16[256,896]{1,0:T(8,128)(2,1)}, bf16[256,896]{1,0:T(8,128)(2,1)S(1)}, u32[]{:S(2)}, u32[]{:S(2)}) collective-permute-start(bf16[256,896]{1,0:T(8,128)(2,1)} %get-tuple-element.230), channel_id=1, source_target_pairs={{0,2},{2,0},{4,6},{6,4},{1,3},{3,1},{5,7},{7,5},{8,10},{10,8},{12,... | collective-permute-start | bytes 1376264 | tf_op jit(solution)/shard_map/ppermute | solution.py:731
  165.2 31.9 %collective-permute-start.28 = (bf16[256,896]{1,0:T(8,128)(2,1)}, bf16[256,896]{1,0:T(8,128)(2,1)S(1)}, u32[]{:S(2)}, u32[]{:S(2)}) collective-permute-start(bf16[256,896]{1,0:T(8,128)(2,1)} %get-tuple-element.231), channel_id=1, source_target_pairs={{0,4},{2,6},{4,0},{6,2},{1,5},{3,7},{5,1},{7,3},{8,12},{10,14},{12... | collective-permute-start | bytes 1376264 | tf_op jit(solution)/shard_map/ppermute | solution.py:731
  166.0 31.1 %collective-permute-start.29 = (bf16[256,896]{1,0:T(8,128)(2,1)}, bf16[256,896]{1,0:T(8,128)(2,1)S(1)}, u32[]{:S(2)}, u32[]{:S(2)}) collective-permute-start(bf16[256,896]{1,0:T(8,128)(2,1)} %get-tuple-element.232), channel_id=1, source_target_pairs={{0,6},{2,4},{4,2},{6,0},{1,7},{3,5},{5,3},{7,1},{8,14},{10,12},{12... | collective-permute-start | bytes 1376264 | tf_op jit(solution)/shard_map/ppermute | solution.py:731
  193.5 30.3 %collective-permute-start.30 = (bf16[256,896]{1,0:T(8,128)(2,1)}, bf16[256,896]{1,0:T(8,128)(2,1)S(1)}, u32[]{:S(2)}, u32[]{:S(2)}) collective-permute-start(bf16[256,896]{1,0:T(8,128)(2,1)} %get-tuple-element.243), channel_id=1, source_target_pairs={{0,2},{2,0},{4,6},{6,4},{1,3},{3,1},{5,7},{7,5},{8,10},{10,8},{12,... | collective-permute-start | bytes 1376264 | tf_op jit(solution)/shard_map/ppermute | solution.py:731
  195.0 28.8 %collective-permute-start.31 = (bf16[256,896]{1,0:T(8,128)(2,1)}, bf16[256,896]{1,0:T(8,128)(2,1)S(1)}, u32[]{:S(2)}, u32[]{:S(2)}) collective-permute-start(bf16[256,896]{1,0:T(8,128)(2,1)} %get-tuple-element.244), channel_id=1, source_target_pairs={{0,4},{2,6},{4,0},{6,2},{1,5},{3,7},{5,1},{7,3},{8,12},{10,14},{12... | collective-permute-start | bytes 1376264 | tf_op jit(solution)/shard_map/ppermute | solution.py:731
  195.8 28.0 %collective-permute-start.32 = (bf16[256,896]{1,0:T(8,128)(2,1)}, bf16[256,896]{1,0:T(8,128)(2,1)S(1)}, u32[]{:S(2)}, u32[]{:S(2)}) collective-permute-start(bf16[256,896]{1,0:T(8,128)(2,1)} %get-tuple-element.245), channel_id=1, source_target_pairs={{0,6},{2,4},{4,2},{6,0},{1,7},{3,5},{5,3},{7,1},{8,14},{10,12},{12... | collective-permute-start | bytes 1376264 | tf_op jit(solution)/shard_map/ppermute | solution.py:731
  226.3 24.7 %collective-permute-start.33 = (bf16[256,896]{1,0:T(8,128)(2,1)S(1)}, bf16[256,896]{1,0:T(8,128)(2,1)S(1)}, u32[]{:S(2)}, u32[]{:S(2)}) collective-permute-start(bf16[256,896]{1,0:T(8,128)(2,1)S(1)} %copy-done.59), channel_id=1, source_target_pairs={{0,2},{2,0},{4,6},{6,4},{1,3},{3,1},{5,7},{7,5},{8,10},{10,8},{12,... | collective-permute-start | bytes 1376264 | tf_op jit(solution)/shard_map/ppermute | solution.py:731
  227.8 23.4 %collective-permute-start.34 = (bf16[256,896]{1,0:T(8,128)(2,1)S(1)}, bf16[256,896]{1,0:T(8,128)(2,1)S(1)}, u32[]{:S(2)}, u32[]{:S(2)}) collective-permute-start(bf16[256,896]{1,0:T(8,128)(2,1)S(1)} %copy-done.58), channel_id=1, source_target_pairs={{0,4},{2,6},{4,0},{6,2},{1,5},{3,7},{5,1},{7,3},{8,12},{10,14},{12... | collective-permute-start | bytes 1376264 | tf_op jit(solution)/shard_map/ppermute | solution.py:731
  228.6 24.1 %collective-permute-start.35 = (bf16[256,896]{1,0:T(8,128)(2,1)S(1)}, bf16[256,896]{1,0:T(8,128)(2,1)S(1)}, u32[]{:S(2)}, u32[]{:S(2)}) collective-permute-start(bf16[256,896]{1,0:T(8,128)(2,1)S(1)} %copy-done.57), channel_id=1, source_target_pairs={{0,6},{2,4},{4,2},{6,0},{1,7},{3,5},{5,3},{7,1},{8,14},{10,12},{12... | collective-permute-start | bytes 1376264 | tf_op jit(solution)/shard_map/ppermute | solution.py:731
  229.8 52.4 %collective-permute-start.40 = (bf16[256,896]{1,0:T(8,128)(2,1)}, bf16[256,896]{1,0:T(8,128)(2,1)S(1)}, u32[]{:S(2)}, u32[]{:S(2)}) collective-permute-start(bf16[256,896]{1,0:T(8,128)(2,1)} %get-tuple-element.281), channel_id=1, source_target_pairs={{0,2},{2,0},{4,6},{6,4},{1,3},{3,1},{5,7},{7,5},{8,10},{10,8},{12,... | collective-permute-start | bytes 1376264 | tf_op jit(solution)/shard_map/ppermute | solution.py:731
  231.2 51.0 %collective-permute-start.41 = (bf16[256,896]{1,0:T(8,128)(2,1)S(1)}, bf16[256,896]{1,0:T(8,128)(2,1)S(1)}, u32[]{:S(2)}, u32[]{:S(2)}) collective-permute-start(bf16[256,896]{1,0:T(8,128)(2,1)S(1)} %copy-done.56), channel_id=1, source_target_pairs={{0,4},{2,6},{4,0},{6,2},{1,5},{3,7},{5,1},{7,3},{8,12},{10,14},{12... | collective-permute-start | bytes 1376264 | tf_op jit(solution)/shard_map/ppermute | solution.py:731
  251.0 9.7 %collective-permute-start.36 = (bf16[256,256]{1,0:T(8,128)(2,1)}, bf16[256,256]{1,0:T(8,128)(2,1)S(1)}, u32[]{:S(2)}, u32[]{:S(2)}) collective-permute-start(bf16[256,256]{1,0:T(8,128)(2,1)} %get-tuple-element.266), channel_id=1, source_target_pairs={{0,1},{1,0},{2,3},{3,2},{4,5},{5,4},{6,7},{7,6},{8,9},{9,8},{10,11... | collective-permute-start | bytes 393224 | tf_op jit(solution)/shard_map/ppermute | solution.py:731
  251.1 10.9 %collective-permute-start.37 = (bf16[256,256]{1,0:T(8,128)(2,1)}, bf16[256,256]{1,0:T(8,128)(2,1)S(1)}, u32[]{:S(2)}, u32[]{:S(2)}) collective-permute-start(bf16[256,256]{1,0:T(8,128)(2,1)} %get-tuple-element.267), channel_id=1, source_target_pairs={{0,2},{1,3},{2,0},{3,1},{4,6},{5,7},{6,4},{7,5},{8,10},{9,11},{10,... | collective-permute-start | bytes 393224 | tf_op jit(solution)/shard_map/ppermute | solution.py:731
  252.7 9.8 %collective-permute-start.38 = (bf16[256,256]{1,0:T(8,128)(2,1)}, bf16[256,256]{1,0:T(8,128)(2,1)S(1)}, u32[]{:S(2)}, u32[]{:S(2)}) collective-permute-start(bf16[256,256]{1,0:T(8,128)(2,1)} %get-tuple-element.268), channel_id=1, source_target_pairs={{0,3},{1,2},{2,1},{3,0},{4,7},{5,6},{6,5},{7,4},{8,11},{9,10},{10,... | collective-permute-start | bytes 393224 | tf_op jit(solution)/shard_map/ppermute | solution.py:731
  260.7 21.5 %collective-permute-start.42 = (bf16[256,896]{1,0:T(8,128)(2,1)S(1)}, bf16[256,896]{1,0:T(8,128)(2,1)S(1)}, u32[]{:S(2)}, u32[]{:S(2)}) collective-permute-start(bf16[256,896]{1,0:T(8,128)(2,1)S(1)} %copy-done.55), channel_id=1, source_target_pairs={{0,6},{2,4},{4,2},{6,0},{1,7},{3,5},{5,3},{7,1},{8,14},{10,12},{12... | collective-permute-start | bytes 1376264 | tf_op jit(solution)/shard_map/ppermute | solution.py:731
  262.0 19.4 %collective-permute-start.39 = (bf16[512,896]{1,0:T(8,128)(2,1)S(1)}, bf16[512,896]{1,0:T(8,128)(2,1)S(1)}, u32[]{:S(2)}, u32[]{:S(2)}) collective-permute-start(bf16[512,896]{1,0:T(8,128)(2,1)S(1)} %convolution_convert_fusion.2), channel_id=1, source_target_pairs={{0,1},{1,0},{2,3},{3,2},{4,5},{5,4},{6,7},{7,6},{8,9},{9,8},{10,11... | collective-permute-start | bytes 2752520 | tf_op jit(solution)/shard_map/ppermute | solution.py:727
  284.2 4.9 %collective-permute-start.43 = (bf16[512,896]{1,0:T(8,128)(2,1)}, bf16[512,896]{1,0:T(8,128)(2,1)}, u32[]{:S(2)}, u32[]{:S(2)}) collective-permute-start(bf16[512,896]{1,0:T(8,128)(2,1)} %convolution_convert_fusion), channel_id=1, source_target_pairs={{0,1},{1,0},{2,3},{3,2},{4,5},{5,4},{6,7},{7,6},{8,9},{9,8},{10,11... | collective-permute-start | bytes 2752520 | tf_op jit(solution)/shard_map/ppermute | solution.py:727
  284.5 6.1 %collective-permute-start.44 = (bf16[256,256]{1,0:T(8,128)(2,1)}, bf16[256,256]{1,0:T(8,128)(2,1)S(1)}, u32[]{:S(2)}, u32[]{:S(2)}) collective-permute-start(bf16[256,256]{1,0:T(8,128)(2,1)} %get-tuple-element.292), channel_id=1, source_target_pairs={{0,1},{1,0},{2,3},{3,2},{4,5},{5,4},{6,7},{7,6},{8,9},{9,8},{10,11... | collective-permute-start | bytes 393224 | tf_op jit(solution)/shard_map/ppermute | solution.py:731
  285.0 6.6 %collective-permute-start.45 = (bf16[256,256]{1,0:T(8,128)(2,1)}, bf16[256,256]{1,0:T(8,128)(2,1)S(1)}, u32[]{:S(2)}, u32[]{:S(2)}) collective-permute-start(bf16[256,256]{1,0:T(8,128)(2,1)} %get-tuple-element.293), channel_id=1, source_target_pairs={{0,2},{1,3},{2,0},{3,1},{4,6},{5,7},{6,4},{7,5},{8,10},{9,11},{10,... | collective-permute-start | bytes 393224 | tf_op jit(solution)/shard_map/ppermute | solution.py:731
  286.1 6.5 %collective-permute-start.46 = (bf16[256,256]{1,0:T(8,128)(2,1)S(1)}, bf16[256,256]{1,0:T(8,128)(2,1)S(1)}, u32[]{:S(2)}, u32[]{:S(2)}) collective-permute-start(bf16[256,256]{1,0:T(8,128)(2,1)S(1)} %copy-done.80), channel_id=1, source_target_pairs={{0,3},{1,2},{2,1},{3,0},{4,7},{5,6},{6,5},{7,4},{8,11},{9,10},{10,... | collective-permute-start | bytes 393224 | tf_op jit(solution)/shard_map/ppermute | solution.py:731
  292.7 12.9 %collective-permute-start.47 = (bf16[128,896]{1,0:T(8,128)(2,1)S(1)}, bf16[128,896]{1,0:T(8,128)(2,1)S(1)}, u32[]{:S(2)}, u32[]{:S(2)}) collective-permute-start(bf16[128,896]{1,0:T(8,128)(2,1)S(1)} %get-tuple-element.347), channel_id=1, source_target_pairs={{0,2},{2,0},{4,6},{6,4},{1,3},{3,1},{5,7},{7,5},{8,10},{10,8},{12,... | collective-permute-start | bytes 688136 | tf_op jit(solution)/shard_map/ppermute | solution.py:731
  294.6 11.2 %collective-permute-start.48 = (bf16[128,896]{1,0:T(8,128)(2,1)S(1)}, bf16[128,896]{1,0:T(8,128)(2,1)S(1)}, u32[]{:S(2)}, u32[]{:S(2)}) collective-permute-start(bf16[128,896]{1,0:T(8,128)(2,1)S(1)} %get-tuple-element.349), channel_id=1, source_target_pairs={{0,4},{2,6},{4,0},{6,2},{1,5},{3,7},{5,1},{7,3},{8,12},{10,14},{12... | collective-permute-start | bytes 688136 | tf_op jit(solution)/shard_map/ppermute | solution.py:731
  295.4 12.1 %collective-permute-start.49 = (bf16[128,896]{1,0:T(8,128)(2,1)S(1)}, bf16[128,896]{1,0:T(8,128)(2,1)S(1)}, u32[]{:S(2)}, u32[]{:S(2)}) collective-permute-start(bf16[128,896]{1,0:T(8,128)(2,1)S(1)} %get-tuple-element.348), channel_id=1, source_target_pairs={{0,6},{2,4},{4,2},{6,0},{1,7},{3,5},{5,3},{7,1},{8,14},{10,12},{12... | collective-permute-start | bytes 688136 | tf_op jit(solution)/shard_map/ppermute | solution.py:731
  310.0 4.7 %collective-permute-start.50 = (bf16[512,256]{1,0:T(8,128)(2,1)S(1)}, bf16[512,256]{1,0:T(8,128)(2,1)S(1)}, u32[]{:S(2)}, u32[]{:S(2)}) collective-permute-start(bf16[512,256]{1,0:T(8,128)(2,1)S(1)} %fusion.5), channel_id=1, source_target_pairs={{0,1},{1,0},{2,3},{3,2},{4,5},{5,4},{6,7},{7,6},{8,9},{9,8},{10,11... | collective-permute-start | bytes 786440 | tf_op jit(solution)/shard_map/ppermute | solution.py:727
  310.9 9.5 %collective-permute-start.54 = (bf16[128,896]{1,0:T(8,128)(2,1)}, bf16[128,896]{1,0:T(8,128)(2,1)S(1)}, u32[]{:S(2)}, u32[]{:S(2)}) collective-permute-start(bf16[128,896]{1,0:T(8,128)(2,1)} %get-tuple-element.350), channel_id=1, source_target_pairs={{0,2},{2,0},{4,6},{6,4},{1,3},{3,1},{5,7},{7,5},{8,10},{10,8},{12,... | collective-permute-start | bytes 688136 | tf_op jit(solution)/shard_map/ppermute | solution.py:731
  311.4 12.5 %collective-permute-start.55 = (bf16[128,896]{1,0:T(8,128)(2,1)}, bf16[128,896]{1,0:T(8,128)(2,1)}, u32[]{:S(2)}, u32[]{:S(2)}) collective-permute-start(bf16[128,896]{1,0:T(8,128)(2,1)} %get-tuple-element.352), channel_id=1, source_target_pairs={{0,4},{2,6},{4,0},{6,2},{1,5},{3,7},{5,1},{7,3},{8,12},{10,14},{12... | collective-permute-start | bytes 688136 | tf_op jit(solution)/shard_map/ppermute | solution.py:731
  313.2 11.6 %collective-permute-start.56 = (bf16[128,896]{1,0:T(8,128)(2,1)}, bf16[128,896]{1,0:T(8,128)(2,1)}, u32[]{:S(2)}, u32[]{:S(2)}) collective-permute-start(bf16[128,896]{1,0:T(8,128)(2,1)} %get-tuple-element.351), channel_id=1, source_target_pairs={{0,6},{2,4},{4,2},{6,0},{1,7},{3,5},{5,3},{7,1},{8,14},{10,12},{12... | collective-permute-start | bytes 688136 | tf_op jit(solution)/shard_map/ppermute | solution.py:731
  318.1 11.7 %collective-permute-start.51 = (bf16[128,256]{1,0:T(8,128)(2,1)S(1)}, bf16[128,256]{1,0:T(8,128)(2,1)S(1)}, u32[]{:S(2)}, u32[]{:S(2)}) collective-permute-start(bf16[128,256]{1,0:T(8,128)(2,1)S(1)} %get-tuple-element.355), channel_id=1, source_target_pairs={{0,2},{2,0},{4,6},{6,4},{1,3},{3,1},{5,7},{7,5},{8,10},{10,8},{12,... | collective-permute-start | bytes 196616 | tf_op jit(solution)/shard_map/ppermute | solution.py:731
  318.7 11.6 %collective-permute-start.52 = (bf16[128,256]{1,0:T(8,128)(2,1)S(1)}, bf16[128,256]{1,0:T(8,128)(2,1)S(1)}, u32[]{:S(2)}, u32[]{:S(2)}) collective-permute-start(bf16[128,256]{1,0:T(8,128)(2,1)S(1)} %get-tuple-element.357), channel_id=1, source_target_pairs={{0,4},{2,6},{4,0},{6,2},{1,5},{3,7},{5,1},{7,3},{8,12},{10,14},{12... | collective-permute-start | bytes 196616 | tf_op jit(solution)/shard_map/ppermute | solution.py:731
  320.4 10.5 %collective-permute-start.53 = (bf16[128,256]{1,0:T(8,128)(2,1)S(1)}, bf16[128,256]{1,0:T(8,128)(2,1)S(1)}, u32[]{:S(2)}, u32[]{:S(2)}) collective-permute-start(bf16[128,256]{1,0:T(8,128)(2,1)S(1)} %get-tuple-element.356), channel_id=1, source_target_pairs={{0,6},{2,4},{4,2},{6,0},{1,7},{3,5},{5,3},{7,1},{8,14},{10,12},{12... | collective-permute-start | bytes 196616 | tf_op jit(solution)/shard_map/ppermute | solution.py:731
  326.0 15.2 %collective-permute-start.59 = (bf16[28,3840]{1,0:T(8,128)(2,1)}, bf16[28,3840]{1,0:T(8,128)(2,1)S(1)}, u32[]{:S(2)}, u32[]{:S(2)}) collective-permute-start(bf16[28,3840]{1,0:T(8,128)(2,1)} %get-tuple-element.336), channel_id=1, source_target_pairs={{0,0},{1,4},{2,2},{3,6},{4,1},{5,5},{6,3},{7,7},{8,8},{9,12},{10,1... | collective-permute-start | bytes 645128 | tf_op jit(solution)/shard_map/ppermute | solution.py:747
  327.6 13.6 %collective-permute-start.60 = (bf16[28,3840]{1,0:T(8,128)(2,1)}, bf16[28,3840]{1,0:T(8,128)(2,1)S(1)}, u32[]{:S(2)}, u32[]{:S(2)}) collective-permute-start(bf16[28,3840]{1,0:T(8,128)(2,1)} %get-tuple-element.337), channel_id=1, source_target_pairs={{0,1},{1,5},{2,3},{3,7},{4,0},{5,4},{6,2},{7,6},{8,9},{9,13},{10,1... | collective-permute-start | bytes 645128 | tf_op jit(solution)/shard_map/ppermute | solution.py:747
  329.8 11.4 %collective-permute-start.61 = (bf16[28,3840]{1,0:T(8,128)(2,1)}, bf16[28,3840]{1,0:T(8,128)(2,1)S(1)}, u32[]{:S(2)}, u32[]{:S(2)}) collective-permute-start(bf16[28,3840]{1,0:T(8,128)(2,1)} %get-tuple-element.338), channel_id=1, source_target_pairs={{0,2},{1,6},{2,0},{3,4},{4,3},{5,7},{6,1},{7,5},{8,10},{9,14},{10,... | collective-permute-start | bytes 645128 | tf_op jit(solution)/shard_map/ppermute | solution.py:747
  330.3 12.7 %collective-permute-start.62 = (bf16[28,3840]{1,0:T(8,128)(2,1)}, bf16[28,3840]{1,0:T(8,128)(2,1)S(1)}, u32[]{:S(2)}, u32[]{:S(2)}) collective-permute-start(bf16[28,3840]{1,0:T(8,128)(2,1)} %get-tuple-element.339), channel_id=1, source_target_pairs={{0,3},{1,7},{2,1},{3,5},{4,2},{5,6},{6,0},{7,4},{8,11},{9,15},{10,... | collective-permute-start | bytes 645128 | tf_op jit(solution)/shard_map/ppermute | solution.py:747
  331.1 8.4 %collective-permute-start.57 = (bf16[64,2048]{1,0:T(8,128)(2,1)S(1)}, bf16[64,2048]{1,0:T(8,128)(2,1)S(1)}, u32[]{:S(2)}, u32[]{:S(2)}) collective-permute-start(bf16[64,2048]{1,0:T(8,128)(2,1)S(1)} %slice.89), channel_id=1, source_target_pairs={{0,8},{8,0},{16,24},{24,16},{1,9},{9,1},{17,25},{25,17},{2,10},{10... | collective-permute-start | bytes 786440 | tf_op jit(solution)/shard_map/ppermute | solution.py:727
  339.6 8.5 %collective-permute-start.58 = (bf16[32,2048]{1,0:T(8,128)(2,1)S(1)}, bf16[32,2048]{1,0:T(8,128)(2,1)S(1)}, u32[]{:S(2)}, u32[]{:S(2)}) collective-permute-start(bf16[32,2048]{1,0:T(8,128)(2,1)S(1)} %slice.105), channel_id=1, source_target_pairs={{0,16},{8,24},{16,0},{24,8},{1,17},{9,25},{17,1},{25,9},{2,18},{10... | collective-permute-start | bytes 393224 | tf_op jit(solution)/shard_map/ppermute | solution.py:727
  (85 other events, 469.3 us)
Sparse Core Ops, SparseCore 0:
  48.7 69.7 all-gather.1
  224.0 73.8 reduce-scatter.1
